TPU v7x, 32 devices: a whole 2x2x4 slice. The times are simulated.
32 devices in a mesh: dp: 16 (over z, y, x), mp: 2 (over core).
Axes of the slice: x: 2, y: 2, z: 4, core: 2. Of those that a mesh axis runs over, the one named last changes fastest.
Arguments:
- input_codes: int32 [2, 16, 800], P(None, 'dp'), may hold values from 0 to 4095
- target_codes: int32 [2, 16, 800], P(None, 'dp'), may hold values from 0 to 4095
- item_lengths: int32 [2, 16, 8], P(None, 'dp'), may hold values from 0 to 680, as said below
- item_labels: int32 [2, 16, 8], P(None, 'dp'), may hold values from 0 to 999
- code_table: float32 [4096, 1024], P('dp'), may hold values from -6 to 6
- class_table: float32 [1000, 1024], P(None, 'dp'), may hold values from -6 to 6
- adaln_weight: float32 [1024, 6144], P('dp'), may hold values from -0.1875 to 0.1875
- qkv_weight: float32 [3, 1024, 1024], P(None, 'dp', 'mp'), may hold values from -0.1875 to 0.1875
- proj_weight: float32 [1024, 1024], P('mp', 'dp'), may hold values from -1 to 1
- expand_weight: float32 [1024, 4096], P('dp', 'mp'), may hold values from -0.1875 to 0.1875
- contract_weight: float32 [4096, 1024], P('mp', 'dp'), may hold values from -0.09375 to 0.09375
- head_weight: float32 [1024, 4096], P('dp', 'mp')
- code_moment: float32 [4096, 1024], P('dp'), may hold values from -3.7252903e-09 to 3.7252903e-09
- class_moment: float32 [1000, 1024], P(None, 'dp'), may hold values from -1.1920929e-07 to 1.1920929e-07
- adaln_moment: float32 [1024, 6144], P('dp'), may hold values from -1.1920929e-07 to 1.1920929e-07
- qkv_moment: float32 [3, 1024, 1024], P(None, 'dp', 'mp'), may hold values from -1.1920929e-07 to 1.1920929e-07
- proj_moment: float32 [1024, 1024], P('mp', 'dp'), may hold values from -1.1920929e-07 to 1.1920929e-07
- expand_moment: float32 [1024, 4096], P('dp', 'mp'), may hold values from -1.1920929e-07 to 1.1920929e-07
- contract_moment: float32 [4096, 1024], P('mp', 'dp'), may hold values from -1.1920929e-07 to 1.1920929e-07
- head_moment: float32 [1024, 4096], P('dp', 'mp'), may hold values from -1.1920929e-07 to 1.1920929e-07
- code_square: float32 [4096, 1024], P('dp'), may hold values from 1.4672444e-18 to 5.8689776e-18
- class_square: float32 [1000, 1024], P(None, 'dp'), may hold values from 1.859513e-15 to 7.423911e-15
- adaln_square: float32 [1024, 6144], P('dp'), may hold values from 1.859513e-15 to 7.423911e-15
- qkv_square: float32 [3, 1024, 1024], P(None, 'dp', 'mp'), may hold values from 1.859513e-15 to 7.423911e-15
- proj_square: float32 [1024, 1024], P('mp', 'dp'), may hold values from 1.859513e-15 to 7.423911e-15
- expand_square: float32 [1024, 4096], P('dp', 'mp'), may hold values from 1.859513e-15 to 7.423911e-15
- contract_square: float32 [4096, 1024], P('mp', 'dp'), may hold values from 1.859513e-15 to 7.423911e-15
- head_square: float32 [1024, 4096], P('dp', 'mp'), may hold values from 1.859513e-15 to 7.423911e-15
Outputs:
- code_first: float32 [4096, 1024], P('dp')
- class_first: float32 [1000, 1024], P(None, 'dp')
- adaln_first: float32 [1024, 6144], P('dp')
- qkv_first: float32 [3, 1024, 1024], P(None, 'dp', 'mp')
- proj_first: float32 [1024, 1024], P('mp', 'dp')
- expand_first: float32 [1024, 4096], P('dp', 'mp')
- contract_first: float32 [4096, 1024], P('mp', 'dp')
- head_first: float32 [1024, 4096], P('dp', 'mp')
- code_second: float32 [4096, 1024], P('dp')
- class_second: float32 [1000, 1024], P(None, 'dp')
- adaln_second: float32 [1024, 6144], P('dp')
- qkv_second: float32 [3, 1024, 1024], P(None, 'dp', 'mp')
- proj_second: float32 [1024, 1024], P('mp', 'dp')
- expand_second: float32 [1024, 4096], P('dp', 'mp')
- contract_second: float32 [4096, 1024], P('mp', 'dp')
- head_second: float32 [1024, 4096], P('dp', 'mp')
- code_new: float32 [4096, 1024], P('dp')
- class_new: float32 [1000, 1024], P(None, 'dp')
- adaln_new: float32 [1024, 6144], P('dp')
- qkv_new: float32 [3, 1024, 1024], P(None, 'dp', 'mp')
- proj_new: float32 [1024, 1024], P('mp', 'dp')
- expand_new: float32 [1024, 4096], P('dp', 'mp')
- contract_new: float32 [4096, 1024], P('mp', 'dp')
- head_new: float32 [1024, 4096], P('dp', 'mp')
- loss: float32 [], replicated
- scale_counts: float32 [10], replicated
- grad_norm: float32 [], replicated
Inputs may be any that keep to these rules, and one draw needn't show every extreme that they name: `item_lengths`: every entry is 0 or one of 1, 5, 14, 30, 55, 91, 155, 255, 424, 680 (an item ends at a scale of the pyramid); in a row the nonzero entries come first and sum to at most 800.
All inputs are finite; a program needn't handle non-finite values.
Results may differ from a plain program's by a relative error of at most 0.012.
The roundings to bfloat16 on the way count: a program that leaves them out, or rounds other values in their place, can miss the bound.
Values may be sent and summed in bfloat16 or wider, within the bound.
No kernel may reach another device: no remote copies, remote signals or barrier semaphores. Data moves between devices by JAX's collectives and lax.ppermute only.
A program may use at most 576 MiB of HBM per device.

v0:
```python
import math

import jax
import jax.numpy as jnp
from jax import lax
from jax.sharding import PartitionSpec as P

D = 1024
HEAD_WIDTH = 64
FF = 4096
CLASSES = 1000
LEN = 800
ITEMS = 8
NSCALES = 10
MICRO = 2
STEP = 10


EPSILON = 1e-06
SOFTMAX_WARMTH = 12.0
CLIP_NORM = 0.001
BETA_ONE = 0.9
BETA_TWO = 0.95
DECAY = 0.05
ADAM_EPSILON = 1e-08
PYRAMID = (1, 5, 14, 30, 55, 91, 155, 255, 424)


def layout(lengths):
    ends = jnp.cumsum(lengths)
    places = jnp.arange(LEN, dtype=jnp.int32)
    passed = places[:, None] >= ends[None, :]
    segment = jnp.sum(passed.astype(jnp.int32), axis=1)
    start = jnp.sum(jnp.where(passed, lengths[None, :], 0), axis=1)
    offset = places - start
    bounds = jnp.array(PYRAMID, dtype=jnp.int32)
    scale_id = jnp.sum((offset[:, None] >= bounds[None, :]).astype(jnp.int32), axis=1)
    usable = places < ends[-1]
    return (segment, scale_id, usable)


def norm_rows(values):
    centered = values - jnp.mean(values, axis=-1, keepdims=True)
    return centered * lax.rsqrt(jnp.mean(centered * centered, axis=-1, keepdims=True) + EPSILON)


def unit_heads(values):
    return values * lax.rsqrt(jnp.mean(values * values, axis=-1, keepdims=True) + EPSILON)


def modulate(values, scale_part, shift_part):
    return norm_rows(values) * (1.0 + scale_part) + shift_part


def gelu_tanh(values):
    return jax.nn.gelu(values, approximate=True)


def matmul(left, right):
    return jnp.dot(left, right, preferred_element_type=jnp.float32)


def matmul_tn(left, right):
    return lax.dot_general(
        left, right, (((0,), (0,)), ((), ())), preferred_element_type=jnp.float32
    )


def matmul_nt(left, right):
    return lax.dot_general(
        left, right, (((1,), (1,)), ((), ())), preferred_element_type=jnp.float32
    )


def branch_total(partial_sum):
    return lax.psum(partial_sum, "mp")


def input_total(partial_sum):
    return lax.psum(partial_sum, "mp")


def row_scores(query_normed, key_normed, segment, scale_id):
    attention_scores = jnp.einsum(
        "ygp,ugp->gyu", query_normed, key_normed, preferred_element_type=jnp.float32
    ) * (SOFTMAX_WARMTH / HEAD_WIDTH)
    allowed = (segment[:, None] == segment[None, :]) & (scale_id[None, :] <= scale_id[:, None])
    return jnp.where(allowed[None], attention_scores, -1e30)


def attend_row(parts):
    query_normed, key_normed, value_b, segment, scale_id = parts
    attention_scores = row_scores(query_normed, key_normed, segment, scale_id)
    row_max = jnp.max(attention_scores, axis=-1, keepdims=True)
    raised = jnp.exp(attention_scores - row_max)
    denominator = jnp.sum(raised, axis=-1, keepdims=True)
    attention = (raised / denominator).astype(jnp.bfloat16)
    attended = jnp.einsum("hqk,khd->qhd", attention, value_b, preferred_element_type=jnp.float32)
    return (attended, (row_max + jnp.log(denominator))[..., 0])


def attend_back(parts):
    query_normed, key_normed, value_b, segment, scale_id, log_total, grad_out = parts
    attention_scores = row_scores(query_normed, key_normed, segment, scale_id)
    attention = jnp.exp(attention_scores - log_total[..., None])
    grad_values = jnp.einsum(
        "hqk,qhd->khd", attention.astype(jnp.bfloat16), grad_out, preferred_element_type=jnp.float32
    )
    grad_probs = jnp.einsum("ygp,ugp->gyu", grad_out, value_b, preferred_element_type=jnp.float32)
    row_dot = jnp.sum(attention * grad_probs, axis=-1, keepdims=True)
    grad_scores = (attention * (grad_probs - row_dot)).astype(jnp.bfloat16)
    scale_factor = SOFTMAX_WARMTH / HEAD_WIDTH
    grad_query_n = (
        jnp.einsum("hqk,khd->qhd", grad_scores, key_normed, preferred_element_type=jnp.float32)
        * scale_factor
    )
    grad_key_n = (
        jnp.einsum("hqk,qhd->khd", grad_scores, query_normed, preferred_element_type=jnp.float32)
        * scale_factor
    )
    return (grad_query_n, grad_key_n, grad_values)


def layer_forward(weights, code_ids, target_ids, lengths, labels, inv_counts):
    code_low, class_low, adaln_low, qkv_low, proj_low, expand_low, contract_low, head_low = weights
    row_count = code_ids.shape[0]
    local_width = qkv_low.shape[2]
    local_heads = local_width // HEAD_WIDTH
    segment, scale_id, usable = jax.vmap(layout)(lengths)
    tokens = jnp.take(code_low, code_ids.reshape(-1), axis=0).astype(jnp.float32)
    class_rows = jnp.take(class_low, labels.reshape(-1), axis=0).astype(jnp.float32)
    class_vec = jax.nn.silu(class_rows).astype(jnp.bfloat16)
    modulation = matmul(class_vec, adaln_low).reshape(row_count, ITEMS, 6 * D)
    padded = jnp.concatenate([modulation, jnp.zeros((row_count, 1, 6 * D), jnp.float32)], axis=1)
    item_ids = segment + (ITEMS + 1) * jnp.arange(row_count, dtype=jnp.int32)[:, None]
    item_ids = item_ids.reshape(-1)
    per_token = jnp.take(padded.reshape(row_count * (ITEMS + 1), 6 * D), item_ids, axis=0)
    gate_attn, gate_mlp, scale_attn, scale_mlp, shift_attn, shift_mlp = jnp.split(
        per_token, 6, axis=1
    )
    normed_attn = modulate(tokens, scale_attn, shift_attn).astype(jnp.bfloat16)
    queries = matmul(normed_attn, qkv_low[0]).reshape(-1, local_heads, HEAD_WIDTH)
    keys_raw = matmul(normed_attn, qkv_low[1]).reshape(-1, local_heads, HEAD_WIDTH)
    value_b = (
        matmul(normed_attn, qkv_low[2])
        .astype(jnp.bfloat16)
        .reshape(row_count, LEN, local_heads, HEAD_WIDTH)
    )
    query_normed = (
        unit_heads(queries).astype(jnp.bfloat16).reshape(row_count, LEN, local_heads, HEAD_WIDTH)
    )
    key_normed = (
        unit_heads(keys_raw).astype(jnp.bfloat16).reshape(row_count, LEN, local_heads, HEAD_WIDTH)
    )
    attended, log_softmax_total = lax.map(
        attend_row, (query_normed, key_normed, value_b, segment, scale_id)
    )
    attended_b = attended.reshape(-1, local_width).astype(jnp.bfloat16)
    attn_out = branch_total(matmul(attended_b, proj_low))
    middle = tokens + gate_attn * attn_out
    normed_mlp = modulate(middle, scale_mlp, shift_mlp).astype(jnp.bfloat16)
    hidden_pre = matmul(normed_mlp, expand_low)
    active = gelu_tanh(hidden_pre).astype(jnp.bfloat16)
    mlp_out = branch_total(matmul(active, contract_low))
    residual = middle + gate_mlp * mlp_out
    normed_head = norm_rows(residual).astype(jnp.bfloat16)
    logits = matmul(normed_head, head_low)
    local_codes = head_low.shape[1]
    shifted = target_ids.reshape(-1) - lax.axis_index("mp") * local_codes
    is_target = jnp.arange(local_codes, dtype=jnp.int32)[None, :] == shifted[:, None]
    target_local = jnp.sum(jnp.where(is_target, logits, 0.0), axis=1)
    row_max = lax.pmax(jnp.max(logits, axis=1), "mp")
    exp_local = jnp.sum(jnp.exp(logits - row_max[:, None]), axis=1)
    exp_total, target_logit = lax.psum((exp_local, target_local), "mp")
    log_total = row_max + jnp.log(exp_total)
    token_weight = jnp.where(usable.reshape(-1), jnp.take(inv_counts, scale_id.reshape(-1)), 0.0)
    loss_part = jnp.sum((log_total - target_logit) * token_weight)
    kept = (
        tokens,
        per_token,
        class_rows,
        class_vec,
        normed_attn,
        queries,
        keys_raw,
        query_normed,
        key_normed,
        value_b,
        segment,
        scale_id,
        log_softmax_total,
        attended_b,
        attn_out,
        middle,
        normed_mlp,
        hidden_pre,
        active,
        mlp_out,
        residual,
        normed_head,
        logits,
        log_total,
        token_weight,
        is_target,
        item_ids,
    )
    return (kept, loss_part)


def layer_backward(weights, kept, code_ids):
    code_low, class_low, adaln_low, qkv_low, proj_low, expand_low, contract_low, head_low = weights
    (
        tokens,
        per_token,
        class_rows,
        class_vec,
        normed_attn,
        queries,
        keys_raw,
        query_normed,
        key_normed,
        value_b,
        segment,
        scale_id,
        log_softmax_total,
        attended_b,
        attn_out,
        middle,
        normed_mlp,
        hidden_pre,
        active,
        mlp_out,
        residual,
        normed_head,
        logits,
        log_total,
        token_weight,
        is_target,
        item_ids,
    ) = kept
    row_count = code_ids.shape[0]
    local_width = qkv_low.shape[2]
    local_heads = local_width // HEAD_WIDTH
    gate_attn, gate_mlp, scale_attn, scale_mlp, shift_attn, shift_mlp = jnp.split(
        per_token, 6, axis=1
    )
    softmax_logits = jnp.exp(logits - log_total[:, None])
    grad_logits = ((softmax_logits - is_target.astype(jnp.float32)) * token_weight[:, None]).astype(
        jnp.bfloat16
    )
    grad_head = matmul_tn(normed_head, grad_logits)
    grad_normed_head = input_total(matmul_nt(grad_logits, head_low))
    _, norm_back = jax.vjp(norm_rows, residual)
    grad_residual = norm_back(grad_normed_head)[0]
    grad_mlp_out = (gate_mlp * grad_residual).astype(jnp.bfloat16)
    grad_gate_mlp = grad_residual * mlp_out
    grad_contract = matmul_tn(active, grad_mlp_out)
    grad_active = matmul_nt(grad_mlp_out, contract_low)
    _, gelu_back = jax.vjp(gelu_tanh, hidden_pre)
    grad_pre = gelu_back(grad_active)[0].astype(jnp.bfloat16)
    grad_expand = matmul_tn(normed_mlp, grad_pre)
    grad_normed_mlp = input_total(matmul_nt(grad_pre, expand_low))
    _, mlp_norm_back = jax.vjp(modulate, middle, scale_mlp, shift_mlp)
    grad_middle_part, grad_scale_mlp, grad_shift_mlp = mlp_norm_back(grad_normed_mlp)
    grad_middle = grad_residual + grad_middle_part
    grad_attn_out = (gate_attn * grad_middle).astype(jnp.bfloat16)
    grad_gate_attn = grad_middle * attn_out
    grad_proj = matmul_tn(attended_b, grad_attn_out)
    grad_attended = matmul_nt(grad_attn_out, proj_low).astype(jnp.bfloat16)
    grad_attended = grad_attended.reshape(row_count, LEN, local_heads, HEAD_WIDTH)
    grad_query_n, grad_key_n, grad_values = lax.map(
        attend_back,
        (query_normed, key_normed, value_b, segment, scale_id, log_softmax_total, grad_attended),
    )
    _, query_back = jax.vjp(unit_heads, queries)
    grad_queries = (
        query_back(grad_query_n.reshape(queries.shape))[0]
        .reshape(-1, local_width)
        .astype(jnp.bfloat16)
    )
    _, key_back = jax.vjp(unit_heads, keys_raw)
    grad_keys = (
        key_back(grad_key_n.reshape(keys_raw.shape))[0]
        .reshape(-1, local_width)
        .astype(jnp.bfloat16)
    )
    grad_values_b = grad_values.reshape(-1, local_width).astype(jnp.bfloat16)
    grad_qkv = jnp.stack(
        [
            matmul_tn(normed_attn, grad_queries),
            matmul_tn(normed_attn, grad_keys),
            matmul_tn(normed_attn, grad_values_b),
        ]
    )
    grad_normed_attn = input_total(
        matmul_nt(grad_queries, qkv_low[0])
        + matmul_nt(grad_keys, qkv_low[1])
        + matmul_nt(grad_values_b, qkv_low[2])
    )
    _, attn_norm_back = jax.vjp(modulate, tokens, scale_attn, shift_attn)
    grad_tokens_part, grad_scale_attn, grad_shift_attn = attn_norm_back(grad_normed_attn)
    grad_tokens = grad_middle + grad_tokens_part
    grad_per_token = jnp.concatenate(
        [
            grad_gate_attn,
            grad_gate_mlp,
            grad_scale_attn,
            grad_scale_mlp,
            grad_shift_attn,
            grad_shift_mlp,
        ],
        axis=1,
    )
    grad_items = jax.ops.segment_sum(grad_per_token, item_ids, num_segments=row_count * (ITEMS + 1))
    grad_modulation = grad_items.reshape(row_count, ITEMS + 1, 6 * D)[:, :ITEMS]
    grad_modulation = grad_modulation.reshape(row_count * ITEMS, 6 * D).astype(jnp.bfloat16)
    grad_class_vec = matmul_nt(grad_modulation, adaln_low)
    _, silu_back = jax.vjp(jax.nn.silu, class_rows)
    grad_class_rows = silu_back(grad_class_vec)[0]
    grad_code = jax.ops.segment_sum(
        grad_tokens, code_ids.reshape(-1), num_segments=code_low.shape[0]
    )
    six = (grad_code, grad_qkv, grad_proj, grad_expand, grad_contract, grad_head)
    return (six, (grad_modulation, class_vec, grad_class_rows))


def step_rates():
    return (
        2.5,
        2.5,
        2.5 / math.sqrt(D),
        2.5 / math.sqrt(D),
        2.5 / math.sqrt(D // 32),
        2.5 / math.sqrt(D),
        2.5 / math.sqrt(FF),
        5.0 / math.sqrt(D),
    )


def adamw_update(weight, grad, moment, square, rate):
    first = BETA_ONE * moment + (1.0 - BETA_ONE) * grad
    second = BETA_TWO * square + (1.0 - BETA_TWO) * grad * grad
    corrected = (
        first / (1.0 - BETA_ONE**STEP) / (jnp.sqrt(second / (1.0 - BETA_TWO**STEP)) + ADAM_EPSILON)
    )
    return (first, second, weight - rate * (corrected + DECAY * weight))


def on_device(
    input_codes,
    target_codes,
    item_lengths,
    item_labels,
    code_table,
    class_table,
    adaln_weight,
    qkv_weight,
    proj_weight,
    expand_weight,
    contract_weight,
    head_weight,
    code_moment,
    class_moment,
    adaln_moment,
    qkv_moment,
    proj_moment,
    expand_moment,
    contract_moment,
    head_moment,
    code_square,
    class_square,
    adaln_square,
    qkv_square,
    proj_square,
    expand_square,
    contract_square,
    head_square,
):
    masters = (
        code_table,
        class_table,
        adaln_weight,
        qkv_weight,
        proj_weight,
        expand_weight,
        contract_weight,
        head_weight,
    )
    moments = (
        code_moment,
        class_moment,
        adaln_moment,
        qkv_moment,
        proj_moment,
        expand_moment,
        contract_moment,
        head_moment,
    )
    squares = (
        code_square,
        class_square,
        adaln_square,
        qkv_square,
        proj_square,
        expand_square,
        contract_square,
        head_square,
    )
    gathered = (
        lax.all_gather(code_table.astype(jnp.bfloat16), "dp", axis=0, tiled=True),
        lax.all_gather(class_table.astype(jnp.bfloat16), "dp", axis=1, tiled=True),
        lax.all_gather(adaln_weight.astype(jnp.bfloat16), "dp", axis=0, tiled=True),
        lax.all_gather(qkv_weight.astype(jnp.bfloat16), "dp", axis=1, tiled=True),
        lax.all_gather(proj_weight.astype(jnp.bfloat16), "dp", axis=1, tiled=True),
        lax.all_gather(expand_weight.astype(jnp.bfloat16), "dp", axis=0, tiled=True),
        lax.all_gather(contract_weight.astype(jnp.bfloat16), "dp", axis=1, tiled=True),
        lax.all_gather(head_weight.astype(jnp.bfloat16), "dp", axis=0, tiled=True),
    )
    _, scale_ids, usable_all = jax.vmap(jax.vmap(layout))(item_lengths)
    picked = (scale_ids[..., None] == jnp.arange(NSCALES, dtype=jnp.int32)) & usable_all[..., None]
    scale_counts = lax.psum(jnp.sum(picked.astype(jnp.float32), axis=(0, 1, 2)), "dp")
    inv_counts = 1.0 / (NSCALES * jnp.maximum(scale_counts, 1.0))
    loss_local = jnp.zeros((), jnp.float32)
    summed = None
    adaln_sum = None
    class_sum = None
    for micro_idx in range(MICRO):
        kept, loss_part = layer_forward(
            gathered,
            input_codes[micro_idx],
            target_codes[micro_idx],
            item_lengths[micro_idx],
            item_labels[micro_idx],
            inv_counts,
        )
        loss_local = loss_local + loss_part
        six, factors = layer_backward(gathered, kept, input_codes[micro_idx])
        grad_modulation, class_vec, grad_class_rows = factors
        micro_labels = item_labels[micro_idx].reshape(-1)
        if summed is None:
            summed = six
        else:
            summed = tuple((total + extra for total, extra in zip(summed, six)))
        adaln_part = matmul_tn(class_vec, grad_modulation)
        class_part = jax.ops.segment_sum(grad_class_rows, micro_labels, num_segments=CLASSES)
        if adaln_sum is None:
            adaln_sum, class_sum = (adaln_part, class_part)
        else:
            adaln_sum, class_sum = (adaln_sum + adaln_part, class_sum + class_part)
    summed = (
        lax.psum_scatter(summed[0], "dp", scatter_dimension=0, tiled=True),
        lax.psum_scatter(summed[1], "dp", scatter_dimension=1, tiled=True),
        lax.psum_scatter(summed[2], "dp", scatter_dimension=1, tiled=True),
        lax.psum_scatter(summed[3], "dp", scatter_dimension=0, tiled=True),
        lax.psum_scatter(summed[4], "dp", scatter_dimension=1, tiled=True),
        lax.psum_scatter(summed[5], "dp", scatter_dimension=0, tiled=True),
    )
    adaln_grad, class_grad = (
        lax.psum_scatter(adaln_sum, "dp", scatter_dimension=0, tiled=True),
        lax.psum_scatter(class_sum, "dp", scatter_dimension=1, tiled=True),
    )
    gradients = (
        summed[0],
        class_grad,
        adaln_grad,
        summed[1],
        summed[2],
        summed[3],
        summed[4],
        summed[5],
    )
    shared_sq = (
        jnp.sum(gradients[0] * gradients[0])
        + jnp.sum(gradients[1] * gradients[1])
        + jnp.sum(gradients[2] * gradients[2])
    )
    own_sq = jnp.zeros((), jnp.float32)
    for grad in gradients[3:]:
        own_sq = own_sq + jnp.sum(grad * grad)
    squared, loss = lax.psum((own_sq + 0.5 * shared_sq, 0.5 * loss_local), ("dp", "mp"))
    grad_norm = jnp.sqrt(squared)
    clip = jnp.minimum(1.0, CLIP_NORM / (grad_norm + 1e-06))
    firsts, seconds, updated = ([], [], [])
    for weight, grad, moment, square, rate in zip(
        masters, gradients, moments, squares, step_rates()
    ):
        first, second, fresh = adamw_update(weight, grad * clip, moment, square, rate)
        firsts.append(first)
        seconds.append(second)
        updated.append(fresh)
    return (
        firsts[0],
        firsts[1],
        firsts[2],
        firsts[3],
        firsts[4],
        firsts[5],
        firsts[6],
        firsts[7],
        seconds[0],
        seconds[1],
        seconds[2],
        seconds[3],
        seconds[4],
        seconds[5],
        seconds[6],
        seconds[7],
        updated[0],
        updated[1],
        updated[2],
        updated[3],
        updated[4],
        updated[5],
        updated[6],
        updated[7],
        loss,
        scale_counts,
        grad_norm,
    )


def solution(mesh):
    placed = (
        P(None, "dp", None),
        P(None, "dp", None),
        P(None, "dp", None),
        P(None, "dp", None),
        P("dp", None),
        P(None, "dp"),
        P("dp", None),
        P(None, "dp", "mp"),
        P("mp", "dp"),
        P("dp", "mp"),
        P("mp", "dp"),
        P("dp", "mp"),
        P("dp", None),
        P(None, "dp"),
        P("dp", None),
        P(None, "dp", "mp"),
        P("mp", "dp"),
        P("dp", "mp"),
        P("mp", "dp"),
        P("dp", "mp"),
        P("dp", None),
        P(None, "dp"),
        P("dp", None),
        P(None, "dp", "mp"),
        P("mp", "dp"),
        P("dp", "mp"),
        P("mp", "dp"),
        P("dp", "mp"),
    )
    return jax.shard_map(
        on_device,
        mesh=mesh,
        in_specs=placed,
        out_specs=(
            P("dp", None),
            P(None, "dp"),
            P("dp", None),
            P(None, "dp", "mp"),
            P("mp", "dp"),
            P("dp", "mp"),
            P("mp", "dp"),
            P("dp", "mp"),
            P("dp", None),
            P(None, "dp"),
            P("dp", None),
            P(None, "dp", "mp"),
            P("mp", "dp"),
            P("dp", "mp"),
            P("mp", "dp"),
            P("dp", "mp"),
            P("dp", None),
            P(None, "dp"),
            P("dp", None),
            P(None, "dp", "mp"),
            P("mp", "dp"),
            P("dp", "mp"),
            P("mp", "dp"),
            P("dp", "mp"),
            P(),
            P(),
            P(),
        ),
        check_vma=False,
    )
```

profile of v0, /device:TPU:0, one launch (start us, length us, event | category | flops | bytes accessed | tf_op | source)
XLA Modules:
  0.0 2915.3 jit_solution(2396015262814065631)
XLA Ops:
  20.6 54.2 %all-gather.11.cloned.1.call-done = bf16[1000,1024]{0,1:T(8,128)(2,1)} async-done(((bf16[1000,64]{0,1:T(8,128)(2,1)}), bf16[1000,1024]{0,1:T(8,128)(2,1)}) %all-gather.11.cloned.1.call-update) | async-done | bytes 2048016 | tf_op jit(solution)/shard_map/all_gather | solution.py:411
  79.0 65.4 %all-gather.15.cloned.1.call-done = bf16[3,1024,512]{2,1,0:T(8,128)(2,1)} async-done(((bf16[3,64,512]{2,1,0:T(8,128)(2,1)}), bf16[3,1024,512]{2,1,0:T(8,128)(2,1)}) %all-gather.15.cloned.1.call-update) | async-done | bytes 3145744 | tf_op jit(solution)/shard_map/all_gather | solution.py:413
  148.0 111.8 %all-gather.9.cloned.1.call-done = bf16[4096,1024]{1,0:T(8,128)(2,1)} async-done(((bf16[256,1024]{1,0:T(8,128)(2,1)}), bf16[4096,1024]{1,0:T(8,128)(2,1)}) %all-gather.9.cloned.1.call-update) | async-done | bytes 8388624 | tf_op jit(solution)/shard_map/all_gather | solution.py:410
  259.8 9.5 gather_fusion
  270.5 9.8 gather_fusion.3
  282.3 130.9 %all-gather.13.cloned.1.call-done = bf16[1024,6144]{1,0:T(8,128)(2,1)} async-done(((bf16[64,6144]{1,0:T(8,128)(2,1)}), bf16[1024,6144]{1,0:T(8,128)(2,1)}) %all-gather.13.cloned.1.call-update) | async-done | bytes 12582928 | tf_op jit(solution)/shard_map/all_gather | solution.py:412
  423.2 10.0 gather_fusion.2
  451.0 10.0 gather_fusion.5
  461.0 8.6 broadcast_select_fusion
  489.3 13.3 fusion.178
  502.7 9.7 fusion.1
  512.4 9.8 fusion.82
  522.3 10.1 fusion.179
  532.4 9.8 fusion
  542.2 9.7 fusion.83
  562.1 28.3 all-reduce.24.cloned.1.call-done
  611.2 60.2 %all-gather.19.cloned.1.call-done = bf16[1024,2048]{1,0:T(8,128)(2,1)} async-done(((bf16[64,2048]{1,0:T(8,128)(2,1)}), bf16[1024,2048]{1,0:T(8,128)(2,1)}) %all-gather.19.cloned.1.call-update) | async-done | bytes 4194320 | tf_op jit(solution)/shard_map/all_gather | solution.py:415
  671.4 9.2 fusion.183
  686.3 63.5 %all-gather.21.cloned.1.call-done = bf16[2048,1024]{0,1:T(8,128)(2,1)} async-done(((bf16[2048,64]{0,1:T(8,128)(2,1)}), bf16[2048,1024]{0,1:T(8,128)(2,1)}) %all-gather.21.cloned.1.call-update) | async-done | bytes 4194320 | tf_op jit(solution)/shard_map/all_gather | solution.py:416
  749.8 9.9 fusion.157
  768.5 39.7 %psum.122 = f32[10]{0:T(128)S(1)} all-reduce(f32[10]{0:T(128)S(1)} %fusion.120), channel_id=1, replica_groups=mesh['dp'=16,'mp'=2] {'dp'}, use_global_device_ids=true, to_apply=%region_24.28 | all-reduce | flops 10 | bytes 80 | tf_op jit(solution)/shard_map/psum | solution.py:421
  821.9 55.4 %all-gather.23.cloned.1.call-done = bf16[1024,2048]{1,0:T(8,128)(2,1)} async-done(((bf16[64,2048]{1,0:T(8,128)(2,1)}), bf16[1024,2048]{1,0:T(8,128)(2,1)}) %all-gather.23.cloned.1.call-update) | async-done | bytes 4194320 | tf_op jit(solution)/shard_map/all_gather | solution.py:417
  877.4 9.6 fusion.181
  940.6 31.3 %all-reduce.20.cloned.1.call-done = (f32[800,1024]{1,0:T(8,128)}, f32[800,1024]{1,0:T(8,128)}) async-done(((f32[800,1024]{1,0:T(8,128)}, f32[800,1024]{1,0:T(8,128)}), (f32[800,1024]{1,0:T(8,128)}, f32[800,1024]{1,0:T(8,128)})) %all-reduce.20.cloned.1.call-update) | async-done | bytes 6553616 | tf_op jit(solution)/shard_map/psum | solution.py:80
  998.0 10.3 fusion.20
  1019.9 33.1 %all-reduce.18.cloned.1.call-done = (f32[800,1024]{1,0:T(8,128)}, f32[800,1024]{1,0:T(8,128)}) async-done(((f32[800,1024]{1,0:T(8,128)}, f32[800,1024]{1,0:T(8,128)}), (f32[800,1024]{1,0:T(8,128)}, f32[800,1024]{1,0:T(8,128)})) %all-reduce.18.cloned.1.call-update) | async-done | bytes 6553616 | tf_op jit(solution)/shard_map/psum | solution.py:80
  1069.7 12.2 fusion.84
  1081.9 14.6 multiply_reduce_fusion.1
  1096.5 19.8 multiply_convert_fusion.1
  1116.3 10.3 fusion.70
  1126.7 8.8 fusion.72
  1153.3 11.3 fusion.87
  1164.6 14.5 multiply_reduce_fusion
  1179.1 15.3 multiply_convert_fusion
  1253.8 11.5 convolution_add_fusion.2
  1320.5 39.6 %scatter_custom_fusion.1 = f32[9,6144]{1,0:T(8,128)} fusion(s32[800]{0:T(1024)} %copy-done.171, f32[800,6144]{1,0:T(8,128)} %constant_dynamic-update-slice_fusion, f32[]{:T(128)} %constant.179.clone.1), kind=kCustom, calls=%fused_computation.270 | custom fusion | flops 4915200 | bytes 221696 | tf_op jit(solution)/shard_map/scatter-add | solution.py:314
  1375.6 52.3 %scatter_custom_fusion.2 = f32[9,6144]{1,0:T(8,128)} fusion(s32[800]{0:T(1024)} %copy-done.170, f32[800,6144]{1,0:T(8,128)} %constant_dynamic-update-slice_fusion.2, f32[]{:T(128)} %constant.179.clone.1), kind=kCustom, calls=%fused_computation.268 | custom fusion | flops 4915200 | bytes 221696 | tf_op jit(solution)/shard_map/scatter-add | solution.py:314
  1437.7 8.6 fusion.130
  1467.8 24.9 scatter_custom_fusion
  1493.5 10.4 fusion.117
  1503.9 16.4 convolution_add_fusion
  1526.0 175.4 %reduce-scatter.19.cloned.1.call-done = f32[2048,64]{0,1:T(8,128)} async-done(((f32[2048,1024]{0,1:T(8,128)}), f32[2048,64]{0,1:T(8,128)}) %reduce-scatter.19.cloned.1.call-update) | async-done | bytes 524304 | tf_op jit(solution)/shard_map/reduce_scatter | solution.py:455
  1703.2 180.7 %reduce-scatter.17.cloned.1.call-done = f32[64,2048]{1,0:T(8,128)} async-done(((f32[1024,2048]{1,0:T(8,128)}), f32[64,2048]{1,0:T(8,128)}) %reduce-scatter.17.cloned.1.call-update) | async-done | bytes 524304 | tf_op jit(solution)/shard_map/reduce_scatter | solution.py:454
  1885.7 139.1 %reduce-scatter.13.cloned.1.call-done = f32[3,64,512]{2,1,0:T(8,128)} async-done(((f32[3,1024,512]{2,1,0:T(8,128)}), f32[3,64,512]{2,1,0:T(8,128)}) %reduce-scatter.13.cloned.1.call-update) | async-done | bytes 393232 | tf_op jit(solution)/shard_map/reduce_scatter | solution.py:452
  2029.8 93.9 %reduce-scatter.25.cloned.1.call-done = f32[64,1000]{1,0:T(8,128)} async-done(((f32[1024,1000]{1,0:T(8,128)}), f32[64,1000]{1,0:T(8,128)}) %reduce-scatter.25.cloned.1.call-update) | async-done | bytes 256016
  2125.6 346.3 %reduce-scatter.11.cloned.1.call-done = f32[256,1024]{1,0:T(8,128)} async-done(((f32[4096,1024]{1,0:T(8,128)}), f32[256,1024]{1,0:T(8,128)}) %reduce-scatter.11.cloned.1.call-update) | async-done | bytes 1048592 | tf_op jit(solution)/shard_map/reduce_scatter | solution.py:451
  2475.3 370.6 %reduce-scatter.23.cloned.1.call-done = f32[64,6144]{1,0:T(8,128)} async-done(((f32[1024,6144]{1,0:T(8,128)}), f32[64,6144]{1,0:T(8,128)}) %reduce-scatter.23.cloned.1.call-update) | async-done | bytes 1572880 | tf_op jit(solution)/shard_map/reduce_scatter | solution.py:459
  2849.1 39.3 %all-reduce.2 = (f32[]{:T(128)}, f32[]{:T(128)}) all-reduce(f32[]{:T(128)S(6)} %add.548, f32[]{:T(128)S(6)} %mul.1266), channel_id=1, replica_groups=mesh['dp'=16,'mp'=2] {'dp','mp'}, use_global_device_ids=true, to_apply=%region_89.94 | all-reduce | flops 2 | bytes 16 | tf_op jit(solution)/shard_map/psum | solution.py:480
  (770 shorter events, 450.5 us)
Async XLA Ops:
  7.2 67.6 %all-gather.11.cloned.1.call-start = ((), (), s32[]{:S(2)}) async-start(), calls=%async_computation.9 | async-start | bytes 2228224 | tf_op jit(solution)/shard_map/all_gather | solution.py:411
  9.1 135.4 %all-gather.15.cloned.1.call-start = ((), (), s32[]{:S(2)}) async-start(), calls=%async_computation.11 | async-start | bytes 3342336 | tf_op jit(solution)/shard_map/all_gather | solution.py:413
  10.8 248.9 %all-gather.9.cloned.1.call-start = ((), (), s32[]{:S(2)}) async-start(), calls=%async_computation.8 | async-start | bytes 8912896 | tf_op jit(solution)/shard_map/all_gather | solution.py:410
  13.0 400.2 %all-gather.13.cloned.1.call-start = ((), (), s32[]{:S(2)}) async-start(), calls=%async_computation.10 | async-start | bytes 13369344 | tf_op jit(solution)/shard_map/all_gather | solution.py:412
  14.0 537.9 %all-gather.17.cloned.1.call-start = ((), (), s32[]{:S(2)}) async-start(), calls=%async_computation.12 | async-start | bytes 1114112 | tf_op jit(solution)/shard_map/all_gather | solution.py:414
  14.8 575.6 %all-reduce.24.cloned.1.call-start = ((), (), s32[]{:S(2)}) async-start(), calls=%async_computation.28 | async-start | bytes 13107200 | tf_op jit(solution)/shard_map/psum | solution.py:76
  16.6 424.9 %copy-start.198 = (pred[800]{0:T(1024)(128)(4,1)}, pred[800]{0:T(1024)(128)(4,1)S(1)}, u32[]{:S(2)}) copy-start(pred[800]{0:T(1024)(128)(4,1)S(1)} %get-tuple-element.381) | copy-start | bytes 2404
  16.6 453.0 %copy-start.194 = (pred[800]{0:T(1024)(128)(4,1)}, pred[800]{0:T(1024)(128)(4,1)S(1)}, u32[]{:S(2)}) copy-start(pred[800]{0:T(1024)(128)(4,1)S(1)} %get-tuple-element.380) | copy-start | bytes 2404
  16.7 396.5 %copy-start.210 = (pred[8]{0:T(512)(128)(4,1)}, pred[8]{0:T(512)(128)(4,1)S(1)}, u32[]{:S(2)}) copy-start(pred[8]{0:T(512)(128)(4,1)S(1)} %get-tuple-element.334) | copy-start | bytes 28
  16.7 403.1 %copy-start.212 = (pred[8]{0:T(512)(128)(4,1)}, pred[8]{0:T(512)(128)(4,1)S(1)}, u32[]{:S(2)}) copy-start(pred[8]{0:T(512)(128)(4,1)S(1)} %get-tuple-element.312) | copy-start | bytes 28
  78.5 334.8 %copy-start.135 = (bf16[8,1024]{1,0:T(8,128)(2,1)}, bf16[8,1024]{1,0:T(8,128)(2,1)S(1)}, u32[]{:S(2)}) copy-start(bf16[8,1024]{1,0:T(8,128)(2,1)S(1)} %gather_fusion.4) | copy-start | bytes 49156
  79.0 340.7 %copy-start.138 = (bf16[8,1024]{1,0:T(8,128)(2,1)}, bf16[8,1024]{1,0:T(8,128)(2,1)S(1)}, u32[]{:S(2)}) copy-start(bf16[8,1024]{1,0:T(8,128)(2,1)S(1)} %gather_fusion.1) | copy-start | bytes 49156
  269.8 171.8 %copy-start.150 = (f32[800]{0:T(1024)}, f32[800]{0:T(1024)S(1)}, u32[]{:S(2)}) copy-start(f32[800]{0:T(1024)S(1)} %broadcast_multiply_fusion.9) | copy-start | bytes 9604
  270.5 171.0 %copy-start.180 = (f32[800]{0:T(1024)}, f32[800]{0:T(1024)S(1)}, u32[]{:S(2)}) copy-start(f32[800]{0:T(1024)S(1)} %fusion.143) | copy-start | bytes 9604
  280.4 189.2 %copy-start.9 = (bf16[800,1024]{1,0:T(8,128)(2,1)}, bf16[800,1024]{1,0:T(8,128)(2,1)S(1)}, u32[]{:S(2)}) copy-start(bf16[800,1024]{1,0:T(8,128)(2,1)S(1)} %gather_fusion.3) | copy-start | bytes 4915204
  280.9 188.7 %copy-start.148 = (f32[800]{0:T(1024)}, f32[800]{0:T(1024)S(1)}, u32[]{:S(2)}) copy-start(f32[800]{0:T(1024)S(1)} %broadcast_multiply_fusion.6) | copy-start | bytes 9604
  282.3 187.4 %copy-start.178 = (f32[800]{0:T(1024)}, f32[800]{0:T(1024)S(1)}, u32[]{:S(2)}) copy-start(f32[800]{0:T(1024)S(1)} %fusion.146) | copy-start | bytes 9604
  559.4 111.9 %all-gather.19.cloned.1.call-start = ((), (), s32[]{:S(2)}) async-start(), calls=%async_computation.13 | async-start | bytes 4456448 | tf_op jit(solution)/shard_map/all_gather | solution.py:415
  561.2 188.6 %all-gather.21.cloned.1.call-start = ((), (), s32[]{:S(2)}) async-start(), calls=%async_computation.14 | async-start | bytes 4456448 | tf_op jit(solution)/shard_map/all_gather | solution.py:416
  562.0 248.3 %all-reduce.22.cloned.1.call-start = ((), (), s32[]{:S(2)}) async-start(), calls=%async_computation.27 | async-start | bytes 13107200 | tf_op jit(solution)/shard_map/psum | solution.py:76
  594.6 215.7 %copy-start.3 = (f32[800,1024]{1,0:T(8,128)}, f32[800,1024]{1,0:T(8,128)S(1)}, u32[]{:S(2)}) copy-start(f32[800,1024]{1,0:T(8,128)S(1)} %get-tuple-element.311) | copy-start | bytes 9830404
  765.6 111.8 %all-gather.23.cloned.1.call-start = ((), (), s32[]{:S(2)}) async-start(), calls=%async_computation.15 | async-start | bytes 4456448 | tf_op jit(solution)/shard_map/all_gather | solution.py:417
  767.4 204.5 %all-reduce.20.cloned.1.call-start = ((), (), s32[]{:S(2)}) async-start(), calls=%async_computation.26 | async-start | bytes 13107200 | tf_op jit(solution)/shard_map/psum | solution.py:80
  814.0 161.5 %copy-start.182 = (f32[800]{0:T(1024)}, f32[800]{0:T(1024)S(1)}, u32[]{:S(2)}) copy-start(f32[800]{0:T(1024)S(1)} %broadcast_multiply_fusion.4) | copy-start | bytes 9604
  814.5 161.0 %copy-start.218 = (f32[800]{0:T(1024)}, f32[800]{0:T(1024)S(1)}, u32[]{:S(2)}) copy-start(f32[800]{0:T(1024)S(1)} %fusion.148) | copy-start | bytes 9604
  819.8 161.7 %copy-start.184 = (f32[800]{0:T(1024)}, f32[800]{0:T(1024)S(1)}, u32[]{:S(2)}) copy-start(f32[800]{0:T(1024)S(1)} %broadcast_multiply_fusion.7) | copy-start | bytes 9604
  821.9 159.6 %copy-start.220 = (f32[800]{0:T(1024)}, f32[800]{0:T(1024)S(1)}, u32[]{:S(2)}) copy-start(f32[800]{0:T(1024)S(1)} %fusion.145) | copy-start | bytes 9604
  940.6 112.4 %all-reduce.18.cloned.1.call-start = ((), (), s32[]{:S(2)}) async-start(), calls=%async_computation.25 | async-start | bytes 13107200 | tf_op jit(solution)/shard_map/psum | solution.py:80
  977.7 163.2 %copy-start.186 = (f32[800]{0:T(1024)}, f32[800]{0:T(1024)S(1)}, u32[]{:S(2)}) copy-start(f32[800]{0:T(1024)S(1)} %negate_multiply_fusion.2) | copy-start | bytes 9604
  1019.1 285.8 %all-reduce.16.cloned.1.call-start = ((), (), s32[]{:S(2)}) async-start(), calls=%async_computation.24 | async-start | bytes 13107200 | tf_op jit(solution)/shard_map/psum | solution.py:80
  1224.0 297.7 %reduce-scatter.21.cloned.1.call-start = ((), (), s32[]{:S(2)}) async-start(), calls=%async_computation.21 | async-start | bytes 8912896 | tf_op jit(solution)/shard_map/reduce_scatter | solution.py:456
  1240.1 284.3 %reduce-scatter.15.cloned.1.call-start = ((), (), s32[]{:S(2)}) async-start(), calls=%async_computation.18 | async-start | bytes 2228224 | tf_op jit(solution)/shard_map/reduce_scatter | solution.py:453
  1246.0 455.4 %reduce-scatter.19.cloned.1.call-start = ((), (), s32[]{:S(2)}) async-start(), calls=%async_computation.20 | async-start | bytes 8912896 | tf_op jit(solution)/shard_map/reduce_scatter | solution.py:455
  1265.4 618.5 %reduce-scatter.17.cloned.1.call-start = ((), (), s32[]{:S(2)}) async-start(), calls=%async_computation.19 | async-start | bytes 8912896 | tf_op jit(solution)/shard_map/reduce_scatter | solution.py:454
  1281.3 743.5 %reduce-scatter.13.cloned.1.call-start = ((), (), s32[]{:S(2)}) async-start(), calls=%async_computation.17 | async-start | bytes 6684672 | tf_op jit(solution)/shard_map/reduce_scatter | solution.py:452
  1295.7 827.9 %reduce-scatter.25.cloned.1.call-start = ((), (), s32[]{:S(2)}) async-start(), calls=%async_computation.23 | async-start | bytes 4456448
  1454.8 1017.1 %reduce-scatter.11.cloned.1.call-start = ((), (), s32[]{:S(2)}) async-start(), calls=%async_computation.16 | async-start | bytes 17825792 | tf_op jit(solution)/shard_map/reduce_scatter | solution.py:451
  1492.7 1353.3 %reduce-scatter.23.cloned.1.call-start = ((), (), s32[]{:S(2)}) async-start(), calls=%async_computation.22 | async-start | bytes 26738688 | tf_op jit(solution)/shard_map/reduce_scatter | solution.py:459
  1520.4 1368.8 %copy-start.127 = (f32[512,64]{0,1:T(8,128)S(1)}, f32[512,64]{0,1:T(8,128)}, u32[]{:S(2)}) copy-start(f32[512,64]{0,1:T(8,128)} %param.47) | copy-start | bytes 393220
  1523.5 1367.5 %copy-start.117 = (f32[1000,64]{0,1:T(8,128)S(1)}, f32[1000,64]{0,1:T(8,128)}, u32[]{:S(2)}) copy-start(f32[1000,64]{0,1:T(8,128)} %param.44) | copy-start | bytes 768004
  1524.4 1364.7 %copy-start.128 = (f32[512,64]{0,1:T(8,128)S(1)}, f32[512,64]{0,1:T(8,128)}, u32[]{:S(2)}) copy-start(f32[512,64]{0,1:T(8,128)} %reduce-scatter.15.cloned.1.call-done) | copy-start | bytes 393220
  2123.6 767.4 %copy-start.116 = (f32[64,1000]{1,0:T(8,128)S(1)}, f32[64,1000]{1,0:T(8,128)}, u32[]{:S(2)}) copy-start(f32[64,1000]{1,0:T(8,128)} %reduce-scatter.25.cloned.1.call-done) | copy-start | bytes 768004
  2123.6 769.4 %copy-start.110 = (f32[3,64,512]{2,1,0:T(8,128)S(1)}, f32[3,64,512]{2,1,0:T(8,128)}, u32[]{:S(2)}) copy-start(f32[3,64,512]{2,1,0:T(8,128)} %param.46) | copy-start | bytes 1179652
  2123.6 769.4 %copy-start.111 = (f32[3,64,512]{2,1,0:T(8,128)S(1)}, f32[3,64,512]{2,1,0:T(8,128)}, u32[]{:S(2)}) copy-start(f32[3,64,512]{2,1,0:T(8,128)} %reduce-scatter.13.cloned.1.call-done) | copy-start | bytes 1179652
  2123.6 769.4 %copy-start.137 = (f32[3,64,512]{2,1,0:T(8,128)S(1)}, f32[3,64,512]{2,1,0:T(8,128)}, u32[]{:S(2)}) copy-start(f32[3,64,512]{2,1,0:T(8,128)} %param.62) | copy-start | bytes 1179652
  2475.3 420.1 %copy-start.81 = (f32[64,2048]{1,0:T(8,128)S(1)}, f32[64,2048]{1,0:T(8,128)}, u32[]{:S(2)}) copy-start(f32[64,2048]{1,0:T(8,128)} %param.50) | copy-start | bytes 1572868
  2475.3 420.1 %copy-start.86 = (f32[64,2048]{1,0:T(8,128)S(1)}, f32[64,2048]{1,0:T(8,128)}, u32[]{:S(2)}) copy-start(f32[64,2048]{1,0:T(8,128)} %reduce-scatter.21.cloned.1.call-done) | copy-start | bytes 1572868
  2475.3 420.1 %copy-start.129 = (f32[64,2048]{1,0:T(8,128)S(1)}, f32[64,2048]{1,0:T(8,128)}, u32[]{:S(2)}) copy-start(f32[64,2048]{1,0:T(8,128)} %param.66) | copy-start | bytes 1572868
  (228 other events, 1769.5 us)
Sparse Core Ops, SparseCore 0:
  11.4 63.3 all-gather.10
  78.2 66.2 all-gather.14
  147.8 111.8 all-gather.8
  263.0 150.1 all-gather.12
  416.4 53.4 all-gather.16
  559.5 30.7 all-reduce.23
  594.1 77.2 all-gather.18
  675.1 74.6 all-gather.20
  765.7 31.1 all-reduce.21
  800.1 77.2 all-gather.22
  940.7 31.1 all-reduce.19
  1019.2 33.7 all-reduce.17
  1224.1 33.6 all-reduce.15
  1260.1 178.9 reduce-scatter.20
  1441.3 83.0 reduce-scatter.14
  1526.7 174.6 reduce-scatter.18
  1703.6 180.2 reduce-scatter.16
  1886.2 138.5 reduce-scatter.12
  2027.2 96.3 reduce-scatter.24
  2125.9 346.0 reduce-scatter.10
  2478.6 367.3 reduce-scatter.22
where the time goes:
time: 2920 us
  waiting for transfers between devices  1940 us (66%)
  other arithmetic  385 us (13%)
  matrix products  367 us (13%)
  local copies, waits for them, and re-layouts  109 us (4%)
  blocking collectives  84.9 us (3%)
    reduce_scatter x1, waiting for transfers between devices, on_device(): lax.psum_scatter(adaln_sum, 'dp', scatter_dimension=0, tiled=True)  371 us
    reduce_scatter x1, waiting for transfers between devices, on_device(): lax.psum_scatter(summed[0], 'dp', scatter_dimension=0, tiled=True)  346 us
    reduce_scatter x1, waiting for transfers between devices, on_device(): lax.psum_scatter(summed[3], 'dp', scatter_dimension=0, tiled=True)  181 us
    reduce_scatter x1, waiting for transfers between devices, on_device(): lax.psum_scatter(summed[4], 'dp', scatter_dimension=1, tiled=True)  175 us
    reduce_scatter x1, waiting for transfers between devices, on_device(): lax.psum_scatter(summed[1], 'dp', scatter_dimension=1, tiled=True)  139 us
    all_gather x1, waiting for transfers between devices, on_device(): lax.all_gather(adaln_weight.astype(jnp.bfloat16), 'dp', axis=0, tiled=True)  131 us
    all_gather x1, waiting for transfers between devices, on_device(): lax.all_gather(code_table.astype(jnp.bfloat16), 'dp', axis=0, tiled=True)  112 us
    unnamed x22, waiting for transfers between devices  94.2 us
  transfers between devices with their start and end apart: 21, of which 17 were waited for; matrix products, arithmetic and copies ran while one was open for 18% of the time, Pallas kernels for 0%

commit v1 on v0

v1 whole, which is shorter than its diff:
```python
import math

import jax
import jax.numpy as jnp
from jax import lax
from jax.experimental import pallas as pl
from jax.experimental.pallas import tpu as pltpu
from jax.sharding import PartitionSpec as P

D = 1024
HEAD_WIDTH = 64
FF = 4096
CLASSES = 1000
LEN = 800
ITEMS = 8
NSCALES = 10
MICRO = 2
STEP = 10


EPSILON = 1e-06
SOFTMAX_WARMTH = 12.0
CLIP_NORM = 0.001
BETA_ONE = 0.9
BETA_TWO = 0.95
DECAY = 0.05
ADAM_EPSILON = 1e-08
PYRAMID = (1, 5, 14, 30, 55, 91, 155, 255, 424)

SCORE_SCALE = SOFTMAX_WARMTH / HEAD_WIDTH
VMEM_LIMIT = 60 * 2**20

bf16 = jnp.bfloat16
f32 = jnp.float32
barrier = lax.optimization_barrier


def swap(values, bits):
    n = lax.axis_size("dp")
    return lax.ppermute(values, "dp", [(i, i ^ bits) for i in range(n)])


def swap_core(values):
    return lax.ppermute(values, "mp", [(0, 1), (1, 0)])


def quarter():
    return lax.axis_size("dp") // 4


def run_tick(stages):
    outs = []
    for kind, value in stages:
        if kind == "z":
            outs.append([swap(value, 4 * j) for j in range(1, quarter())])
        elif kind == "zs":
            outs.append([swap(value[j], 4 * j) for j in range(1, quarter())])
        elif kind == "xy":
            outs.append([swap(value[0], 1), swap(value[1], 2)])
        else:
            outs.append(swap_core(value))
    return outs


class Gather:
    def __init__(self, block, core=True):
        self.block = block
        self.step = 0
        self.core = core

    def done(self):
        return self.step == (4 if self.core else 3)

    def request(self):
        if self.step == 0:
            return ("z", self.block)
        if self.step == 1:
            return ("xy", (self.group, self.group))
        if self.step == 2:
            half = self.group.shape[0] // 2
            return ("xy", (self.from_y[:half], self.from_x[half:]))
        return ("mp", self.own)

    def accept(self, got):
        if self.step == 0:
            self.group = jnp.concatenate([self.block] + got)
        elif self.step == 1:
            self.from_x, self.from_y = got
        elif self.step == 2:
            self.own = jnp.concatenate([self.group, self.from_x, self.from_y] + got)
        else:
            self.peer = got
        self.step += 1


class Scatter:
    def __init__(self, own, peer=None, dtype=bf16):
        n = lax.axis_size("dp")
        self.dtype = dtype
        shape = (4, n // 4, own.shape[0] // n) + own.shape[1:]
        self.own = own.reshape(shape)
        self.peer = None if peer is None else peer.reshape(shape)
        self.step = 0 if peer is not None else 1
        self.total = self.own.astype(f32) if peer is None else None

    def done(self):
        return self.step == 4

    def request(self):
        half = self.own.shape[1] // 2
        if self.step == 0:
            return ("mp", self.peer)
        if self.step == 1:
            s = self.total
            return ("xy", (s[3, :half].astype(self.dtype), s[3, half:].astype(self.dtype)))
        if self.step == 2:
            s = self.total
            rest = s[1][:half], s[1][half:] + self.diag[1].astype(f32)
            rest_y = s[2][:half] + self.diag[0].astype(f32), s[2][half:]
            return (
                "xy",
                (
                    jnp.concatenate(rest).astype(self.dtype),
                    jnp.concatenate(rest_y).astype(self.dtype),
                ),
            )
        return ("zs", [self.column[j].astype(self.dtype) for j in range(quarter())])

    def accept(self, got):
        if self.step == 0:
            self.total = self.own.astype(f32) + got.astype(f32)
        elif self.step == 1:
            self.diag = got
        elif self.step == 2:
            self.column = self.total[0] + got[0].astype(f32) + got[1].astype(f32)
        else:
            out = self.column[0]
            for part in got:
                out = out + part.astype(f32)
            self.result = out
        self.step += 1


class Engine:
    def __init__(self):
        self.jobs = []
        self.last = ()

    def add(self, job):
        self.jobs.append(job)

    def tick(self, live=()):
        jobs = [job for job in self.jobs if not job.done()]
        requests = [job.request() for job in jobs]
        kinds = [kind for kind, _ in requests]
        values = [value for _, value in requests]
        values, live, _ = barrier((values, live, self.last))
        outs = barrier(run_tick(list(zip(kinds, values))))
        self.last = outs
        for job, out in zip(jobs, outs):
            job.accept(out)
        return live


def small_gather(values):
    group = jnp.stack([values] + [swap(values, 4 * j) for j in range(1, quarter())])
    return jnp.concatenate([group] + [swap(group, g) for g in (1, 2, 3)])


def total_over_all(values):
    n = lax.axis_size("dp")
    bits = 1
    while bits < n:
        values = values + swap(values, bits)
        bits *= 2
    return values + swap_core(values)


def place_of(index):
    apart = jnp.bitwise_xor(index, lax.axis_index("dp"))
    return (apart & 3) * quarter() + (apart >> 2)


def layout(lengths):
    ends = jnp.cumsum(lengths)
    places = jnp.arange(LEN, dtype=jnp.int32)
    passed = places[:, None] >= ends[None, :]
    segment = jnp.sum(passed.astype(jnp.int32), axis=1)
    start = jnp.sum(jnp.where(passed, lengths[None, :], 0), axis=1)
    offset = places - start
    bounds = jnp.array(PYRAMID, dtype=jnp.int32)
    scale_id = jnp.sum((offset[:, None] >= bounds[None, :]).astype(jnp.int32), axis=1)
    usable = places < ends[-1]
    return (segment, scale_id, usable)


def norm_rows(values):
    centered = values - jnp.mean(values, axis=-1, keepdims=True)
    return centered * lax.rsqrt(jnp.mean(centered * centered, axis=-1, keepdims=True) + EPSILON)


def unit_heads(values):
    return values * lax.rsqrt(jnp.mean(values * values, axis=-1, keepdims=True) + EPSILON)


def modulate(values, scale_part, shift_part):
    return norm_rows(values) * (1.0 + scale_part) + shift_part


def gelu_tanh(values):
    return jax.nn.gelu(values, approximate=True)


def matmul(left, right):
    return jnp.dot(left, right, preferred_element_type=f32)


def matmul_tn(left, right):
    return lax.dot_general(left, right, (((0,), (0,)), ((), ())), preferred_element_type=f32)


def matmul_nt(left, right):
    return lax.dot_general(left, right, (((1,), (1,)), ((), ())), preferred_element_type=f32)


def exact_tn(left, right):
    return lax.dot_general(
        left,
        right,
        (((0,), (0,)), ((), ())),
        precision=lax.Precision.HIGHEST,
        preferred_element_type=f32,
    )


def unit_pair(values):
    factor = lax.rsqrt(jnp.mean(values * values, axis=-1, keepdims=True) + EPSILON)
    return factor, (values * factor).astype(bf16)


def unit_back(values, factor, grad):
    inner = jnp.mean(grad * values, axis=-1, keepdims=True)
    return (factor * (grad - values * (factor * factor * inner))).astype(bf16)


def attend_kernel(q_ref, k_ref, v_ref, bias_ref, out_ref):
    outs = []
    for head in range(2):
        cut = slice(head * HEAD_WIDTH, (head + 1) * HEAD_WIDTH)
        _, query_n = unit_pair(q_ref[:, cut])
        _, key_n = unit_pair(k_ref[:, cut])
        raised = jnp.exp(matmul_nt(query_n, key_n) * SCORE_SCALE + bias_ref[...])
        share = 1.0 / jnp.sum(raised, axis=-1, keepdims=True)
        outs.append(matmul((raised * share).astype(bf16), v_ref[:, cut].astype(bf16)).astype(bf16))
    out_ref[...] = jnp.concatenate(outs, axis=1)


def attend_back_kernel(q_ref, k_ref, v_ref, g_ref, bias_ref, out_ref):
    pair, pairs = pl.program_id(0), pl.num_programs(0)
    results = [[], [], []]
    for head in range(2):
        cut = slice(head * HEAD_WIDTH, (head + 1) * HEAD_WIDTH)
        query, key = q_ref[:, cut], k_ref[:, cut]
        query_f, query_n = unit_pair(query)
        key_f, key_n = unit_pair(key)
        value_b, grad_out = v_ref[:, cut].astype(bf16), g_ref[:, cut]
        grad_q, grad_k, grad_v = [], 0.0, 0.0
        for low, high in ((0, 384), (384, LEN)):
            raised = jnp.exp(matmul_nt(key_n, query_n[low:high]) * SCORE_SCALE + bias_ref[:, low:high])
            attention = raised * (1.0 / jnp.sum(raised, axis=0, keepdims=True))
            grad_probs = matmul_nt(value_b, grad_out[low:high])
            row_dot = jnp.sum(attention * grad_probs, axis=0, keepdims=True)
            grad_scores = (attention * (grad_probs - row_dot)).astype(bf16)
            grad_v = grad_v + matmul(attention.astype(bf16), grad_out[low:high])
            grad_k = grad_k + matmul(grad_scores, query_n[low:high])
            grad_q.append(matmul_tn(key_n, grad_scores).T)
        grad_q = jnp.concatenate(grad_q, axis=0) * SCORE_SCALE
        results[0].append(unit_back(query, query_f, grad_q))
        results[1].append(unit_back(key, key_f, grad_k * SCORE_SCALE))
        results[2].append(grad_v.astype(bf16))
    for i in range(3):
        start = pl.multiple_of((i * pairs + pair) * 2 * HEAD_WIDTH, 2 * HEAD_WIDTH)
        out_ref[:, pl.ds(start, 2 * HEAD_WIDTH)] = jnp.concatenate(results[i], axis=1)


def pair_specs(pairs):
    def third(i):
        return pl.BlockSpec((LEN, 2 * HEAD_WIDTH), lambda pair: (0, i * pairs + pair))

    return [third(0), third(1), third(2)], pl.BlockSpec((LEN, LEN), lambda pair: (0, 0))


def attend(raw, bias):
    width = raw.shape[1] // 3
    thirds, bias_spec = pair_specs(width // (2 * HEAD_WIDTH))
    return pl.pallas_call(
        attend_kernel,
        grid=(width // (2 * HEAD_WIDTH),),
        in_specs=thirds + [bias_spec],
        out_specs=thirds[0],
        out_shape=jax.ShapeDtypeStruct((LEN, width), bf16),
        compiler_params=pltpu.CompilerParams(vmem_limit_bytes=VMEM_LIMIT),
        cost_estimate=pl.CostEstimate(
            flops=4 * LEN * LEN * width,
            transcendentals=LEN * LEN * width // HEAD_WIDTH,
            bytes_accessed=16 * LEN * width,
        ),
    )(raw, raw, raw, bias)


def attend_back(raw, grad_out, bias_t):
    width = raw.shape[1] // 3
    thirds, bias_spec = pair_specs(width // (2 * HEAD_WIDTH))
    return pl.pallas_call(
        attend_back_kernel,
        grid=(width // (2 * HEAD_WIDTH),),
        in_specs=thirds + [thirds[0], bias_spec],
        out_specs=pl.BlockSpec((LEN, 3 * width), lambda pair: (0, 0)),
        out_shape=jax.ShapeDtypeStruct((LEN, 3 * width), bf16),
        compiler_params=pltpu.CompilerParams(vmem_limit_bytes=VMEM_LIMIT),
        cost_estimate=pl.CostEstimate(
            flops=10 * LEN * LEN * width,
            transcendentals=LEN * LEN * width // HEAD_WIDTH,
            bytes_accessed=20 * LEN * width,
        ),
    )(raw, raw, raw, grad_out, bias_t)


def step_rates():
    return (
        2.5,
        2.5,
        2.5 / math.sqrt(D),
        2.5 / math.sqrt(D),
        2.5 / math.sqrt(D // 32),
        2.5 / math.sqrt(D),
        2.5 / math.sqrt(FF),
        5.0 / math.sqrt(D),
    )


def adamw_update(weight, grad, moment, square, rate):
    first = BETA_ONE * moment + (1.0 - BETA_ONE) * grad
    second = BETA_TWO * square + (1.0 - BETA_TWO) * grad * grad
    corrected = (
        first / (1.0 - BETA_ONE**STEP) / (jnp.sqrt(second / (1.0 - BETA_TWO**STEP)) + ADAM_EPSILON)
    )
    return (first, second, weight - rate * (corrected + DECAY * weight))


def on_device(
    input_codes,
    target_codes,
    item_lengths,
    item_labels,
    code_table,
    class_table,
    adaln_weight,
    qkv_weight,
    proj_weight,
    expand_weight,
    contract_weight,
    head_weight,
    code_moment,
    class_moment,
    adaln_moment,
    qkv_moment,
    proj_moment,
    expand_moment,
    contract_moment,
    head_moment,
    code_square,
    class_square,
    adaln_square,
    qkv_square,
    proj_square,
    expand_square,
    contract_square,
    head_square,
):
    masters = (
        code_table,
        class_table,
        adaln_weight,
        qkv_weight,
        proj_weight.T,
        expand_weight,
        contract_weight.T,
        head_weight,
    )
    moments = (
        code_moment,
        class_moment,
        adaln_moment,
        qkv_moment,
        proj_moment.T,
        expand_moment,
        contract_moment.T,
        head_moment,
    )
    squares = (
        code_square,
        class_square,
        adaln_square,
        qkv_square,
        proj_square.T,
        expand_square,
        contract_square.T,
        head_square,
    )
    n = lax.axis_size("dp")
    core = lax.axis_index("mp")
    rows = code_table.shape[0]
    half_rows = rows // 2
    width = proj_weight.shape[0]
    wide = expand_weight.shape[1]
    codes_local = head_weight.shape[1]

    def mine(values):
        return lax.dynamic_index_in_dim(values, core, 0, keepdims=False)

    code_block = lax.dynamic_slice_in_dim(code_table, core * half_rows, half_rows, 0).astype(bf16)
    attn_block = jnp.concatenate(
        [qkv_weight[0], qkv_weight[1], qkv_weight[2], proj_weight.T], axis=1
    ).astype(bf16)
    jobs = [
        Gather(block)
        for block in (
            code_block,
            attn_block,
            expand_weight.astype(bf16),
            contract_weight.T.astype(bf16),
            head_weight.astype(bf16),
        )
    ]
    numbers = small_gather(jnp.concatenate([item_lengths[:, 0], item_labels[:, 0]], axis=1))
    engine = Engine()
    engine.add(jobs[0])
    engine.tick()
    labels_own = mine(jnp.swapaxes(numbers[:, :, ITEMS:], 0, 1)).reshape(-1)
    labels_peer = mine(jnp.swapaxes(numbers[:, ::-1, ITEMS:], 0, 1)).reshape(-1)
    class_low = class_table.astype(bf16)
    adaln_low = adaln_weight.astype(bf16)

    def class_part(labels):
        picked = (labels[:, None] == jnp.arange(CLASSES, dtype=jnp.int32)[None, :]).astype(bf16)
        class_rows = matmul(picked, class_low)
        return picked, class_rows, jax.nn.silu(class_rows).astype(bf16)

    picked_own, class_rows_own, class_vec_own = class_part(labels_own)
    picked_peer, class_rows_peer, class_vec_peer = class_part(labels_peer)
    mod_job = Scatter(matmul(class_vec_own, adaln_low), None, f32)
    engine.add(mod_job)
    for job in jobs[1:4]:
        engine.add(job)
        engine.tick()

    lengths = mine(item_lengths)[0]
    code_ids = mine(input_codes)[0]
    target_ids = mine(target_codes)[0]
    segment, scale_id, usable = layout(lengths)
    bounds = jnp.array((0,) + PYRAMID, dtype=jnp.int32)
    sizes = jnp.array(PYRAMID + (LEN,), dtype=jnp.int32) - bounds
    all_lengths = numbers[:, :, :ITEMS].reshape(-1)
    scale_counts = jnp.sum(
        jnp.clip(all_lengths[:, None] - bounds[None, :], 0, sizes[None, :]), axis=0
    ).astype(f32)
    inv_counts = 1.0 / (NSCALES * jnp.maximum(scale_counts, 1.0))
    scale_hot = scale_id[:, None] == jnp.arange(NSCALES, dtype=jnp.int32)[None, :]
    token_weight = jnp.where(
        usable, jnp.sum(jnp.where(scale_hot, inv_counts[None, :], 0.0), axis=1), 0.0
    )

    block_width = D // n
    block_ids = jnp.arange(n, dtype=jnp.int32)
    block_place = place_of(block_ids)
    feature_place = (block_place[:, None] * block_width + jnp.arange(block_width)[None, :]).reshape(-1)
    turn = (feature_place[:, None] == jnp.arange(D, dtype=jnp.int32)[None, :]).astype(bf16)
    relative_block = ((jnp.arange(n) % quarter()) * 4 + jnp.arange(n) // quarter()) ^ lax.axis_index("dp")

    same = segment[:, None] == segment[None, :]
    bias = jnp.where(same & (scale_id[None, :] <= scale_id[:, None]), 0.0, -1e30)
    bias_t = jnp.where(same & (scale_id[:, None] <= scale_id[None, :]), 0.0, -1e30)
    within = code_ids % rows
    other = (within // half_rows != core).astype(jnp.int32)
    code_rows = other * (n * half_rows) + place_of(code_ids // rows) * half_rows + within % half_rows

    engine.add(jobs[4])
    table, mod, turn, code_rows = engine.tick(
        ((jobs[0].own, jobs[0].peer), mod_job.result, turn, code_rows)
    )
    tokens = matmul(jnp.take(jnp.concatenate(table), code_rows, axis=0), turn)
    mod = mod.reshape(ITEMS * 6, n, block_width)
    mod = jnp.take(mod, relative_block, axis=1).reshape(ITEMS, 6 * D)
    padded = jnp.concatenate([mod, jnp.zeros((1, 6 * D), f32)], axis=0)
    per_token = jnp.take(padded, segment, axis=0)
    gate_attn, gate_mlp, scale_attn, scale_mlp, shift_attn, shift_mlp = jnp.split(
        per_token, 6, axis=1
    )
    normed_attn = modulate(tokens, scale_attn, shift_attn).astype(bf16)
    normed_attn, bias = engine.tick((normed_attn, bias))
    attn_w = (jobs[1].own, jobs[1].peer)
    raw = [matmul(normed_attn, w[:, : 3 * width]) for w in attn_w]
    attended = [attend(r, bias) for r in raw]
    attended, normed_attn = engine.tick((attended, normed_attn))
    attn_out = sum(matmul_nt(a, w[:, 3 * width :]) for a, w in zip(attended, attn_w))
    middle = tokens + gate_attn * attn_out
    normed_mlp = modulate(middle, scale_mlp, shift_mlp).astype(bf16)
    expand_w = (jobs[2].own, jobs[2].peer)
    hidden_pre = [matmul(normed_mlp, w) for w in expand_w]
    active = [gelu_tanh(h).astype(bf16) for h in hidden_pre]
    active, middle = engine.tick((active, middle))
    contract_w = (jobs[3].own, jobs[3].peer)
    mlp_out = matmul_nt(active[0], contract_w[0]) + matmul_nt(active[1], contract_w[1])
    residual = middle + gate_mlp * mlp_out
    normed_head = norm_rows(residual).astype(bf16)
    head_w = (jobs[4].own, jobs[4].peer)
    logits = [matmul(normed_head, w) for w in head_w]
    shifted = [
        target_ids - core * codes_local,
        target_ids - (1 - core) * codes_local,
    ]
    is_target = [
        jnp.arange(codes_local, dtype=jnp.int32)[None, :] == s[:, None] for s in shifted
    ]
    target_logit = sum(jnp.sum(jnp.where(t, x, 0.0), axis=1) for t, x in zip(is_target, logits))
    row_max = jnp.maximum(jnp.max(logits[0], axis=1), jnp.max(logits[1], axis=1))
    exp_total = sum(jnp.sum(jnp.exp(x - row_max[:, None]), axis=1) for x in logits)
    log_total = row_max + jnp.log(exp_total)
    loss_local = jnp.sum((log_total - target_logit) * token_weight)

    grad_logits = [
        ((jnp.exp(x - log_total[:, None]) - t.astype(f32)) * token_weight[:, None]).astype(bf16)
        for x, t in zip(logits, is_target)
    ]

    def scatter_job(left, rights):
        return Scatter(*[matmul_tn(left, right).astype(bf16) for right in rights])

    head_job = scatter_job(normed_head, grad_logits)
    engine.add(head_job)
    grad_logits, active = engine.tick((grad_logits, active))
    grad_normed_head = matmul_nt(grad_logits[0], head_w[0]) + matmul_nt(grad_logits[1], head_w[1])
    _, norm_back = jax.vjp(norm_rows, residual)
    grad_residual = norm_back(grad_normed_head)[0]
    grad_mlp_out = (gate_mlp * grad_residual).astype(bf16)
    grad_gate_mlp = grad_residual * mlp_out
    contract_job = scatter_job(grad_mlp_out, active)
    engine.add(contract_job)
    grad_mlp_out, hidden_pre, grad_residual = engine.tick((grad_mlp_out, hidden_pre, grad_residual))
    grad_pre = []
    for h, w in zip(hidden_pre, contract_w):
        _, gelu_back = jax.vjp(gelu_tanh, h)
        grad_pre.append(gelu_back(matmul(grad_mlp_out, w))[0].astype(bf16))
    expand_job = scatter_job(normed_mlp, grad_pre)
    engine.add(expand_job)
    grad_pre, grad_residual = engine.tick((grad_pre, grad_residual))
    grad_normed_mlp = matmul_nt(grad_pre[0], expand_w[0]) + matmul_nt(grad_pre[1], expand_w[1])
    _, mlp_norm_back = jax.vjp(modulate, middle, scale_mlp, shift_mlp)
    grad_middle_part, grad_scale_mlp, grad_shift_mlp = mlp_norm_back(grad_normed_mlp)
    grad_middle = grad_residual + grad_middle_part
    grad_attn_out = (gate_attn * grad_middle).astype(bf16)
    grad_gate_attn = grad_middle * attn_out
    grad_proj = [matmul_tn(grad_attn_out, a).astype(bf16) for a in attended]
    grad_attended = [matmul(grad_attn_out, w[:, 3 * width :]).astype(bf16) for w in attn_w]
    grad_attended, raw, bias_t, grad_proj = engine.tick((grad_attended, raw, bias_t, grad_proj))
    grad_own = attend_back(raw[0], grad_attended[0], bias_t)
    grad_own, grad_attended, normed_attn = engine.tick((grad_own, grad_attended, normed_attn))
    grad_peer = attend_back(raw[1], grad_attended[1], bias_t)
    grad_raw = (grad_own, grad_peer)
    attn_job = Scatter(
        *[
            jnp.concatenate([matmul_tn(normed_attn, g).astype(bf16), p], axis=1)
            for g, p in zip(grad_raw, grad_proj)
        ]
    )
    engine.add(attn_job)
    grad_raw, grad_middle, turn = engine.tick((grad_raw, grad_middle, turn))
    grad_normed_attn = sum(matmul_nt(g, w[:, : 3 * width]) for g, w in zip(grad_raw, attn_w))
    _, attn_norm_back = jax.vjp(modulate, tokens, scale_attn, shift_attn)
    grad_tokens_part, grad_scale_attn, grad_shift_attn = attn_norm_back(grad_normed_attn)
    grad_tokens = grad_middle + grad_tokens_part
    grad_flat = matmul_nt(grad_tokens.astype(bf16), turn).astype(bf16)
    code_hot = (
        code_rows[:, None] == jnp.arange(2 * n * half_rows, dtype=jnp.int32)[None, :]
    ).astype(bf16)
    grad_code = matmul_tn(code_hot, grad_flat).astype(bf16)
    code_job = Scatter(grad_code[: n * half_rows], grad_code[n * half_rows :])
    engine.add(code_job)
    grad_scale_attn, grad_shift_attn = engine.tick((grad_scale_attn, grad_shift_attn))
    grad_per_token = jnp.concatenate(
        [
            grad_gate_attn,
            grad_gate_mlp,
            grad_scale_attn,
            grad_scale_mlp,
            grad_shift_attn,
            grad_shift_mlp,
        ],
        axis=1,
    )
    segment_hot = (segment[:, None] == jnp.arange(ITEMS, dtype=jnp.int32)[None, :]).astype(f32)
    grad_items = exact_tn(segment_hot, grad_per_token)
    grad_modulation = jnp.take(
        grad_items.reshape(ITEMS * 6, n, block_width), block_place, axis=1
    ).reshape(ITEMS, 6 * D).astype(bf16)
    item_job = Gather(grad_modulation)
    engine.add(item_job)
    for _ in range(4):
        engine.tick()
    adaln_grad = matmul_tn(class_vec_own, item_job.own) + matmul_tn(class_vec_peer, item_job.peer)

    def class_grad_part(picked, class_rows, items):
        grad_class_vec = matmul_nt(items, adaln_low)
        _, silu_back = jax.vjp(jax.nn.silu, class_rows)
        return exact_tn(picked.astype(f32), silu_back(grad_class_vec)[0])

    class_grad = class_grad_part(picked_own, class_rows_own, item_job.own) + class_grad_part(
        picked_peer, class_rows_peer, item_job.peer
    )
    code_half = code_job.result
    code_other = swap_core(code_half)
    code_grad = jnp.where(
        core == 0,
        jnp.concatenate([code_half, code_other]),
        jnp.concatenate([code_other, code_half]),
    )
    attn_grad = attn_job.result
    qkv_grad = jnp.stack([attn_grad[:, i * width : (i + 1) * width] for i in range(3)])
    gradients = (
        code_grad,
        class_grad,
        adaln_grad,
        qkv_grad,
        attn_grad[:, 3 * width :],
        expand_job.result,
        contract_job.result,
        head_job.result,
    )
    shared_sq = jnp.sum(class_grad * class_grad) + jnp.sum(adaln_grad * adaln_grad)
    own_sq = jnp.sum(code_half * code_half) + jnp.sum(attn_grad * attn_grad)
    for grad in gradients[5:]:
        own_sq = own_sq + jnp.sum(grad * grad)
    totals = total_over_all(
        jnp.concatenate([(own_sq + 0.5 * shared_sq).reshape(1), loss_local.reshape(1)])
    )
    squared, loss = totals[0], totals[1]
    grad_norm = jnp.sqrt(squared)
    clip = jnp.minimum(1.0, CLIP_NORM / (grad_norm + 1e-06))
    firsts, seconds, updated = ([], [], [])
    for place, (weight, grad, moment, square, rate) in enumerate(
        zip(masters, gradients, moments, squares, step_rates())
    ):
        for kept, value in zip(
            (firsts, seconds, updated), adamw_update(weight, grad * clip, moment, square, rate)
        ):
            kept.append(value.T if place in (4, 6) else value)
    return (*firsts, *seconds, *updated, loss, scale_counts, grad_norm)


def solution(mesh):
    token_spec = P(None, "dp", None)
    weight_specs = (
        P("dp", None),
        P(None, "dp"),
        P("dp", None),
        P(None, "dp", "mp"),
        P("mp", "dp"),
        P("dp", "mp"),
        P("mp", "dp"),
        P("dp", "mp"),
    )
    return jax.shard_map(
        on_device,
        mesh=mesh,
        in_specs=(token_spec,) * 4 + weight_specs * 3,
        out_specs=weight_specs * 3 + (P(), P(), P()),
        check_vma=False,
    )
```

time: 2920 us -> 1030 us (0.35)
  waiting for transfers between devices: 1940 us -> 231 us
  other arithmetic: 385 us -> 212 us
  starting transfers between devices: 1.28 us -> 127 us
  matrix products: 367 us -> 248 us
  Pallas kernels: 0 us -> 94.1 us
  blocking collectives: 84.9 us -> 0 us
    reduce_scatter x7 -> x0, waiting for transfers between devices: 1210 us -> none  [the longest x1 371 us: on_device(): lax.psum_scatter(adaln_sum, 'dp', scatter_dimension=0, tiled=True)]
    all_gather x8 -> x0, waiting for transfers between devices: 541 us -> none  [the longest x1 131 us: on_device(): lax.all_gather(adaln_weight.astype(jnp.bfloat16), 'dp', axis=0, tiled=True)]
    ppermute x0 -> x107, waiting for transfers between devices: none -> 231 us  [the longest x94 230 us: swap(): return lax.ppermute(values, 'dp', [(i, i ^ bits) for i in range(n)])]
    ppermute x0 -> x107, starting transfers between devices: none -> 127 us  [the longest x94 126 us: swap(): return lax.ppermute(values, 'dp', [(i, i ^ bits) for i in range(n)])]
    dot_general x28 -> x17, matrix products: 208 us -> 89 us  [the longest x14 76.3 us: matmul(): return jnp.dot(left, right, preferred_element_type=f32)]
    unnamed x22 -> x0, waiting for transfers between devices: 94.2 us -> none
    pallas_call x0 -> x4, Pallas kernels: none -> 94.1 us  [the longest x2 56.4 us: attend_back(): pl.pallas_call(attend_back_kernel, grid=(width // (2 * HEAD_WIDTH),), in_...]
    psum x5 -> x0, waiting for transfers between devices: 92.7 us -> none  [the longest x3 64.4 us: input_total(): return lax.psum(partial_sum, 'mp')]
  transfers between devices with their start and end apart: 21 -> 107, of which waited for: 17 -> 37; matrix products, arithmetic and copies ran while one was open for 18% -> 36% of each run, Pallas kernels for 0% -> 9%
where the time goes in v1:
time: 1030 us; the launch traced here: 1020 us
  matrix products  248 us (24%)
  waiting for transfers between devices  231 us (22%)
  other arithmetic  212 us (21%)
  starting transfers between devices  127 us (12%)
  local copies, waits for them, and re-layouts  103 us (10%)
  Pallas kernels  94.1 us (9%)
    ppermute x94, waiting for transfers between devices, swap(): return lax.ppermute(values, 'dp', [(i, i ^ bits) for i in range(n)])  230 us
    ppermute x94, starting transfers between devices, swap(): return lax.ppermute(values, 'dp', [(i, i ^ bits) for i in range(n)])  126 us
    dot_general x13, matrix products, matmul_tn(): lax.dot_general(left, right, (((0,), (0,)), ((), ())), preferred_element_...  80.2 us
    dot_general x12, matrix products, matmul_nt(): lax.dot_general(left, right, (((1,), (1,)), ((), ())), preferred_element_...  78.4 us
    dot_general x14, matrix products, matmul(): return jnp.dot(left, right, preferred_element_type=f32)  76.3 us
    pallas_call x2, Pallas kernels, attend_back(): pl.pallas_call(attend_back_kernel, grid=(width // (2 * HEAD_WIDTH),), in_...  56.4 us
    unnamed x361, local copies, waits for them, and re-layouts  49.7 us
    another operation x15, other arithmetic  37.9 us
  transfers between devices with their start and end apart: 107, of which 37 were waited for; matrix products, arithmetic and copies ran while one was open for 36% of the time, Pallas kernels for 9%

profile of v1, /device:TPU:0, one launch (start us, length us, event | category | flops | bytes accessed | tf_op | source)
XLA Modules:
  0.0 1023.5 jit_solution(4066335149748457455)
XLA Ops:
  44.3 10.0 collective-permute-done.14
  55.9 13.3 %collective-permute-done.11 = f32[2,8,6144]{2,1,0:T(8,128)S(1)} collective-permute-done((f32[2,8,6144]{2,1,0:T(8,128)S(1)}, f32[2,8,6144]{2,1,0:T(8,128)S(1)}, u32[]{:S(2)}, u32[]{:S(2)}) %collective-permute-start.11) | collective-permute-done | bytes 393248 | tf_op jit(solution)/shard_map/ppermute | solution.py:40
  82.4 13.0 %collective-permute-done.23 = bf16[64,2048]{1,0:T(8,128)(2,1)} collective-permute-done((bf16[64,2048]{1,0:T(8,128)(2,1)}, bf16[64,2048]{1,0:T(8,128)(2,1)}, u32[]{:S(2)}, u32[]{:S(2)}) %collective-permute-start.23) | collective-permute-done | bytes 262176 | tf_op jit(solution)/shard_map/ppermute | solution.py:40
  106.9 22.4 %collective-permute-done.17 = bf16[256,1024]{1,0:T(8,128)(2,1)S(1)} collective-permute-done((bf16[256,1024]{1,0:T(8,128)(2,1)}, bf16[256,1024]{1,0:T(8,128)(2,1)S(1)}, u32[]{:S(2)}, u32[]{:S(2)}) %collective-permute-start.17) | collective-permute-done | bytes 524320 | tf_op jit(solution)/shard_map/ppermute | solution.py:40
  147.6 11.7 %collective-permute-done.26 = f32[8,6144]{1,0:T(8,128)S(1)} collective-permute-done((f32[8,6144]{1,0:T(8,128)S(1)}, f32[8,6144]{1,0:T(8,128)S(1)}, u32[]{:S(2)}, u32[]{:S(2)}) %collective-permute-start.26) | collective-permute-done | bytes 196640 | tf_op jit(solution)/shard_map/ppermute | solution.py:40
  171.1 11.0 %collective-permute-done.34 = bf16[64,2048]{1,0:T(8,128)(2,1)S(1)} collective-permute-done((bf16[64,2048]{1,0:T(8,128)(2,1)S(1)}, bf16[64,2048]{1,0:T(8,128)(2,1)S(1)}, u32[]{:S(2)}, u32[]{:S(2)}) %collective-permute-start.34) | collective-permute-done | bytes 262176 | tf_op jit(solution)/shard_map/ppermute | solution.py:40
  186.1 15.2 %collective-permute-done.29 = bf16[128,2048]{1,0:T(8,128)(2,1)S(1)} collective-permute-done((bf16[128,2048]{1,0:T(8,128)(2,1)S(1)}, bf16[128,2048]{1,0:T(8,128)(2,1)S(1)}, u32[]{:S(2)}, u32[]{:S(2)}) %collective-permute-start.29) | collective-permute-done | bytes 524320 | tf_op jit(solution)/shard_map/ppermute | solution.py:40
  212.6 7.7 pad_maximum_fusion
  220.3 9.9 gather_fusion
  236.9 10.0 gather_fusion.1
  246.8 8.5 broadcast_select_fusion
  264.2 10.2 collective-permute-done.37
  274.5 19.5 %collective-permute-done.38 = bf16[128,2048]{1,0:T(8,128)(2,1)S(1)} collective-permute-done((bf16[128,2048]{1,0:T(8,128)(2,1)}, bf16[128,2048]{1,0:T(8,128)(2,1)S(1)}, u32[]{:S(2)}, u32[]{:S(2)}) %collective-permute-start.38) | collective-permute-done | bytes 524320 | tf_op jit(solution)/shard_map/ppermute | solution.py:40
  308.5 7.4 fusion.46.q_ref.k_ref.v_ref
  315.9 18.6 %shard_map.503 = bf16[800,512]{1,0:T(8,128)(2,1)} custom-call(f32[800,1536]{1,0:T(8,128)} %fusion.46.q_ref.k_ref.v_ref, f32[800,1536]{1,0:T(8,128)} %fusion.46.q_ref.k_ref.v_ref, f32[800,1536]{1,0:T(8,128)} %fusion.46.q_ref.k_ref.v_ref, f32[800,800]{1,0:T(8,128)} %get-tuple-element.322.bias_ref), custom_call_target="tpu_custom_call" | custom-call | flops 1310720000 | bytes 6553600 | tf_op jit(solution)/shard_map/pallas_call | solution.py:296
  336.2 7.3 fusion.42.q_ref.k_ref.v_ref
  346.8 19.0 %shard_map.502 = bf16[800,512]{1,0:T(8,128)(2,1)} custom-call(f32[800,1536]{1,0:T(8,128)} %fusion.42.q_ref.k_ref.v_ref, f32[800,1536]{1,0:T(8,128)} %fusion.42.q_ref.k_ref.v_ref, f32[800,1536]{1,0:T(8,128)} %fusion.42.q_ref.k_ref.v_ref, f32[800,800]{1,0:T(8,128)} %get-tuple-element.322.bias_ref), custom_call_target="tpu_custom_call" | custom-call | flops 1310720000 | bytes 6553600 | tf_op jit(solution)/shard_map/pallas_call | solution.py:296
  387.2 9.4 fusion.31
  396.7 7.3 fusion.23
  409.1 7.5 fusion.222
  416.7 11.8 %fusion.214 = (f32[800]{0:T(1024)S(1)}, f32[800,1024]{1,0:T(8,128)}, f32[800]{0:T(1024)S(1)}, f32[800,1024]{1,0:T(8,128)}) fusion(f32[800,1024]{1,0:T(8,128)} %copy-done.3, f32[800,6144]{1,0:T(8,128)S(1)} %bitcast.415, f32[800,1024]{1,0:T(8,128)} %fusion.222, bf16[800,2048]{1,0:T(8,128)(2,1)} %get-tuple-element.347, ...), kind=kOutput, calls=%fused_computation.535 | convolution fusion | flops 3359537664 | bytes 23861504 | tf_op jit(solution)/shard_map/dot_general | solution.py:223
  437.3 10.8 %fusion.221 = (f32[800]{0:T(1024)S(1)}, f32[800,2048]{1,0:T(8,128)}) fusion(bf16[800,1024]{1,0:T(8,128)(2,1)S(1)} %multiply_convert_fusion.4, bf16[1024,2048]{1,0:T(8,128)(2,1)} %collective-permute-done.52), kind=kOutput, calls=%fused_computation.542 | convolution fusion | flops 3357080832 | bytes 12389504 | tf_op jit(solution)/shard_map/dot_general | solution.py:215
  455.8 8.6 multiply_convert_fusion
  464.4 8.2 convolution_convert_fusion.6
  472.6 7.5 fusion.223
  480.7 9.8 multiply_reduce_fusion.3
  529.8 7.8 fusion.225
  546.2 8.8 convolution_convert_fusion.2
  559.5 9.2 convolution_convert_fusion.4
  571.7 8.9 convert_add_fusion.2
  584.5 8.3 fusion.226
  594.9 10.2 multiply_reduce_fusion.2
  609.9 7.2 multiply_dynamic-update-slice_fusion.2
  638.1 7.6 convert_add_fusion.3
  661.9 8.7 collective-permute-done.62
  671.1 7.9 collective-permute-start.64
  679.0 28.3 %shard_map.504 = bf16[800,1536]{1,0:T(8,128)(2,1)} custom-call(f32[800,1536]{1,0:T(8,128)} %fusion.42.q_ref.k_ref.v_ref, f32[800,1536]{1,0:T(8,128)} %fusion.42.q_ref.k_ref.v_ref, f32[800,1536]{1,0:T(8,128)} %fusion.42.q_ref.k_ref.v_ref, bf16[800,512]{1,0:T(8,128)(2,1)} %convolution_convert_fusion.12.g_ref, f32[800,800]{1,0:T(8,128)} %get-tuple-element.377.bias_ref), custom_call_target="tpu_custom_call" | custom-call | flops 3276800000 | bytes 8192000 | tf_op jit(solution)/shard_map/pallas_call | solution.py:314
  722.7 28.1 %shard_map.505 = bf16[800,1536]{1,0:T(8,128)(2,1)} custom-call(f32[800,1536]{1,0:T(8,128)} %fusion.46.q_ref.k_ref.v_ref, f32[800,1536]{1,0:T(8,128)} %fusion.46.q_ref.k_ref.v_ref, f32[800,1536]{1,0:T(8,128)} %fusion.46.q_ref.k_ref.v_ref, bf16[800,512]{1,0:T(8,128)(2,1)} %convolution_convert_fusion.11.g_ref, f32[800,800]{1,0:T(8,128)} %get-tuple-element.377.bias_ref), custom_call_target="tpu_custom_call" | custom-call | flops 3276800000 | bytes 8192000 | tf_op jit(solution)/shard_map/pallas_call | solution.py:314
  787.1 7.0 fusion.205
  794.1 16.7 %fusion.1 = bf16[4096,1024]{1,0:T(8,128)(2,1)} fusion(s32[800]{0:T(1024)} %copy-done.124, bf16[1024,1024]{1,0:T(8,128)(2,1)} %fusion.33, f32[800,1024]{1,0:T(8,128)} %get-tuple-element.398, f32[800,1024]{1,0:T(8,128)} %get-tuple-element.504, f32[800]{0:T(1024)S(1)} %negate_multiply_fusion), kind=kOutput, calls=%fused_computation.19 | convolution fusion | flops 8399355904 | bytes 17045760 | tf_op jit(solution)/shard_map/dot_general | solution.py:219
  810.9 6.6 fusion.216
  817.6 7.6 fusion.188
  844.9 10.6 %fusion.121 = bf16[8,6144]{1,0:T(8,128)(2,1)S(1)} fusion(f32[800,6144]{1,0:T(8,128)} %constant_dynamic-update-slice_fusion.47, s32[800]{0:T(1024)S(1)} %copy-done.112), kind=kOutput, calls=%fused_computation.281 | convolution fusion | flops 471865600 | bytes 19762304 | tf_op jit(solution)/shard_map/dot_general | solution.py:227
  877.3 24.5 %collective-permute-done.83 = bf16[2,128,1024]{2,1,0:T(8,128)(2,1)S(1)} collective-permute-done((bf16[2,128,1024]{2,1,0:T(8,128)(2,1)S(1)}, bf16[2,128,1024]{2,1,0:T(8,128)(2,1)S(1)}, u32[]{:S(2)}, u32[]{:S(2)}) %collective-permute-start.83) | collective-permute-done | bytes 524320 | tf_op jit(solution)/shard_map/ppermute | solution.py:40
  908.7 7.8 collective-permute-done.88
  921.4 8.0 collective-permute-done.90
  929.4 7.9 collective-permute-done.93
  950.1 9.5 collective-permute-done.96
  (761 shorter events, 470.6 us)
Async XLA Ops:
  37.1 32.1 %collective-permute-start.10 = (bf16[512,1024]{1,0:T(8,128)(2,1)S(1)}, bf16[512,1024]{1,0:T(8,128)(2,1)S(1)}, u32[]{:S(2)}, u32[]{:S(2)}) collective-permute-start(bf16[512,1024]{1,0:T(8,128)(2,1)S(1)} %pad_maximum_fusion.3), channel_id=1, source_target_pairs={{0,4},{2,6},{4,0},{6,2},{8,12},{10,14},{12,8},{14,10},{16,20},{18,... | collective-permute-start | bytes 3145736 | tf_op jit(solution)/shard_map/ppermute | solution.py:40
  38.6 30.5 %collective-permute-start.9 = (bf16[512,1024]{1,0:T(8,128)(2,1)S(1)}, bf16[512,1024]{1,0:T(8,128)(2,1)S(1)}, u32[]{:S(2)}, u32[]{:S(2)}) collective-permute-start(bf16[512,1024]{1,0:T(8,128)(2,1)S(1)} %pad_maximum_fusion.3), channel_id=1, source_target_pairs={{0,2},{2,0},{4,6},{6,4},{8,10},{10,8},{12,14},{14,12},{16,18},{18,... | collective-permute-start | bytes 3145736 | tf_op jit(solution)/shard_map/ppermute | solution.py:40
  80.4 48.9 %collective-permute-start.20 = (bf16[256,2048]{1,0:T(8,128)(2,1)}, bf16[256,2048]{1,0:T(8,128)(2,1)S(1)}, u32[]{:S(2)}, u32[]{:S(2)}) collective-permute-start(bf16[256,2048]{1,0:T(8,128)(2,1)} %pad_maximum_fusion.4), channel_id=1, source_target_pairs={{0,2},{2,0},{4,6},{6,4},{8,10},{10,8},{12,14},{14,12},{16,18},{18,... | collective-permute-start | bytes 3145736 | tf_op jit(solution)/shard_map/ppermute | solution.py:40
  81.7 47.6 %collective-permute-start.21 = (bf16[256,2048]{1,0:T(8,128)(2,1)}, bf16[256,2048]{1,0:T(8,128)(2,1)S(1)}, u32[]{:S(2)}, u32[]{:S(2)}) collective-permute-start(bf16[256,2048]{1,0:T(8,128)(2,1)} %pad_maximum_fusion.4), channel_id=1, source_target_pairs={{0,4},{2,6},{4,0},{6,2},{8,12},{10,14},{12,8},{14,10},{16,20},{18,... | collective-permute-start | bytes 3145736 | tf_op jit(solution)/shard_map/ppermute | solution.py:40
  95.4 33.9 %collective-permute-start.18 = (f32[4,8,6144]{2,1,0:T(8,128)}, f32[4,8,6144]{2,1,0:T(8,128)}, u32[]{:S(2)}, u32[]{:S(2)}) collective-permute-start(f32[4,8,6144]{2,1,0:T(8,128)} %get-tuple-element.259), channel_id=1, source_target_pairs={{0,2},{2,0},{4,6},{6,4},{8,10},{10,8},{12,14},{14,12},{16,18},{18,... | collective-permute-start | bytes 2359304 | tf_op jit(solution)/shard_map/ppermute | solution.py:40
  96.9 32.4 %collective-permute-start.19 = (f32[4,8,6144]{2,1,0:T(8,128)}, f32[4,8,6144]{2,1,0:T(8,128)}, u32[]{:S(2)}, u32[]{:S(2)}) collective-permute-start(f32[4,8,6144]{2,1,0:T(8,128)} %get-tuple-element.260), channel_id=1, source_target_pairs={{0,4},{2,6},{4,0},{6,2},{8,12},{10,14},{12,8},{14,10},{16,20},{18,... | collective-permute-start | bytes 2359304 | tf_op jit(solution)/shard_map/ppermute | solution.py:40
  97.8 31.4 %collective-permute-start.17 = (bf16[256,1024]{1,0:T(8,128)(2,1)}, bf16[256,1024]{1,0:T(8,128)(2,1)S(1)}, u32[]{:S(2)}, u32[]{:S(2)}) collective-permute-start(bf16[256,1024]{1,0:T(8,128)(2,1)} %slice.468), channel_id=1, source_target_pairs={{0,4},{2,6},{4,0},{6,2},{8,12},{10,14},{12,8},{14,10},{16,20},{18,... | collective-permute-start | bytes 1572872 | tf_op jit(solution)/shard_map/ppermute | solution.py:40
  134.4 68.1 %collective-permute-start.25 = (bf16[2048,1024]{1,0:T(8,128)(2,1)S(1)}, bf16[2048,1024]{1,0:T(8,128)(2,1)S(1)}, u32[]{:S(2)}, u32[]{:S(2)}) collective-permute-start(bf16[2048,1024]{1,0:T(8,128)(2,1)S(1)} %constant_dynamic-update-slice_fusion.7), channel_id=1, source_target_pairs={{0,1},{1,0},{2,3},{3,2},{4,5},{5,4},{6,7},{7,6},{8,9},{9,8},{10,11... | collective-permute-start | bytes 12582920 | tf_op jit(solution)/shard_map/ppermute | solution.py:44
  165.7 36.8 %collective-permute-start.31 = (bf16[256,2048]{1,0:T(8,128)(2,1)S(1)}, bf16[256,2048]{1,0:T(8,128)(2,1)S(1)}, u32[]{:S(2)}, u32[]{:S(2)}) collective-permute-start(bf16[256,2048]{1,0:T(8,128)(2,1)S(1)} %pad_maximum_fusion.5), channel_id=1, source_target_pairs={{0,2},{2,0},{4,6},{6,4},{8,10},{10,8},{12,14},{14,12},{16,18},{18,... | collective-permute-start | bytes 3145736 | tf_op jit(solution)/shard_map/ppermute | solution.py:40
  167.2 35.3 %collective-permute-start.32 = (bf16[256,2048]{1,0:T(8,128)(2,1)S(1)}, bf16[256,2048]{1,0:T(8,128)(2,1)S(1)}, u32[]{:S(2)}, u32[]{:S(2)}) collective-permute-start(bf16[256,2048]{1,0:T(8,128)(2,1)S(1)} %pad_maximum_fusion.5), channel_id=1, source_target_pairs={{0,4},{2,6},{4,0},{6,2},{8,12},{10,14},{12,8},{14,10},{16,20},{18,... | collective-permute-start | bytes 3145736 | tf_op jit(solution)/shard_map/ppermute | solution.py:40
  207.1 50.4 %collective-permute-start.41 = (bf16[64,2048]{1,0:T(8,128)(2,1)}, bf16[64,2048]{1,0:T(8,128)(2,1)}, u32[]{:S(2)}, u32[]{:S(2)}) collective-permute-start(bf16[64,2048]{1,0:T(8,128)(2,1)} %get-tuple-element.303), channel_id=1, source_target_pairs={{0,8},{2,10},{4,12},{6,14},{8,0},{10,2},{12,4},{14,6},{16,24},{18,... | collective-permute-start | bytes 786440 | tf_op jit(solution)/shard_map/ppermute | solution.py:40
  208.1 52.0 %collective-permute-start.42 = (bf16[64,2048]{1,0:T(8,128)(2,1)}, bf16[64,2048]{1,0:T(8,128)(2,1)}, u32[]{:S(2)}, u32[]{:S(2)}) collective-permute-start(bf16[64,2048]{1,0:T(8,128)(2,1)} %get-tuple-element.303), channel_id=1, source_target_pairs={{0,16},{2,18},{4,20},{6,22},{8,24},{10,26},{12,28},{14,30},{16,0},... | collective-permute-start | bytes 786440 | tf_op jit(solution)/shard_map/ppermute | solution.py:40
  210.1 51.6 %collective-permute-start.43 = (bf16[64,2048]{1,0:T(8,128)(2,1)}, bf16[64,2048]{1,0:T(8,128)(2,1)}, u32[]{:S(2)}, u32[]{:S(2)}) collective-permute-start(bf16[64,2048]{1,0:T(8,128)(2,1)} %get-tuple-element.303), channel_id=1, source_target_pairs={{0,24},{2,26},{4,28},{6,30},{8,16},{10,18},{12,20},{14,22},{16,8},... | collective-permute-start | bytes 786440 | tf_op jit(solution)/shard_map/ppermute | solution.py:40
  211.9 82.1 %collective-permute-start.36 = (bf16[1024,2048]{1,0:T(8,128)(2,1)}, bf16[1024,2048]{1,0:T(8,128)(2,1)}, u32[]{:S(2)}, u32[]{:S(2)}) collective-permute-start(bf16[1024,2048]{1,0:T(8,128)(2,1)} %copy-done.127), channel_id=1, source_target_pairs={{0,1},{1,0},{2,3},{3,2},{4,5},{5,4},{6,7},{7,6},{8,9},{9,8},{10,11... | collective-permute-start | bytes 12582920 | tf_op jit(solution)/shard_map/ppermute | solution.py:44
  212.0 82.0 %collective-permute-start.39 = (bf16[256,2048]{1,0:T(8,128)(2,1)}, bf16[256,2048]{1,0:T(8,128)(2,1)S(1)}, u32[]{:S(2)}, u32[]{:S(2)}) collective-permute-start(bf16[256,2048]{1,0:T(8,128)(2,1)} %pad_maximum_fusion.6), channel_id=1, source_target_pairs={{0,2},{2,0},{4,6},{6,4},{8,10},{10,8},{12,14},{14,12},{16,18},{18,... | collective-permute-start | bytes 3145736 | tf_op jit(solution)/shard_map/ppermute | solution.py:40
  257.5 36.5 %collective-permute-start.40 = (bf16[256,2048]{1,0:T(8,128)(2,1)S(1)}, bf16[256,2048]{1,0:T(8,128)(2,1)S(1)}, u32[]{:S(2)}, u32[]{:S(2)}) collective-permute-start(bf16[256,2048]{1,0:T(8,128)(2,1)S(1)} %copy-done.59), channel_id=1, source_target_pairs={{0,4},{2,6},{4,0},{6,2},{8,12},{10,14},{12,8},{14,10},{16,20},{18,... | collective-permute-start | bytes 3145736 | tf_op jit(solution)/shard_map/ppermute | solution.py:40
  261.7 32.2 %collective-permute-start.38 = (bf16[128,2048]{1,0:T(8,128)(2,1)}, bf16[128,2048]{1,0:T(8,128)(2,1)S(1)}, u32[]{:S(2)}, u32[]{:S(2)}) collective-permute-start(bf16[128,2048]{1,0:T(8,128)(2,1)} %slice.485), channel_id=1, source_target_pairs={{0,4},{2,6},{4,0},{6,2},{8,12},{10,14},{12,8},{14,10},{16,20},{18,... | collective-permute-start | bytes 1572872 | tf_op jit(solution)/shard_map/ppermute | solution.py:40
  299.6 68.4 %collective-permute-start.44 = (bf16[1024,2048]{1,0:T(8,128)(2,1)}, bf16[1024,2048]{1,0:T(8,128)(2,1)}, u32[]{:S(2)}, u32[]{:S(2)}) collective-permute-start(bf16[1024,2048]{1,0:T(8,128)(2,1)} %constant_dynamic-update-slice_fusion.23), channel_id=1, source_target_pairs={{0,1},{1,0},{2,3},{3,2},{4,5},{5,4},{6,7},{7,6},{8,9},{9,8},{10,11... | collective-permute-start | bytes 12582920 | tf_op jit(solution)/shard_map/ppermute | solution.py:44
  304.5 63.5 %collective-permute-start.47 = (bf16[256,2048]{1,0:T(8,128)(2,1)}, bf16[256,2048]{1,0:T(8,128)(2,1)S(1)}, u32[]{:S(2)}, u32[]{:S(2)}) collective-permute-start(bf16[256,2048]{1,0:T(8,128)(2,1)} %pad_maximum_fusion.7), channel_id=1, source_target_pairs={{0,2},{2,0},{4,6},{6,4},{8,10},{10,8},{12,14},{14,12},{16,18},{18,... | collective-permute-start | bytes 3145736 | tf_op jit(solution)/shard_map/ppermute | solution.py:40
  305.9 62.0 %collective-permute-start.48 = (bf16[256,2048]{1,0:T(8,128)(2,1)}, bf16[256,2048]{1,0:T(8,128)(2,1)}, u32[]{:S(2)}, u32[]{:S(2)}) collective-permute-start(bf16[256,2048]{1,0:T(8,128)(2,1)} %pad_maximum_fusion.7), channel_id=1, source_target_pairs={{0,4},{2,6},{4,0},{6,2},{8,12},{10,14},{12,8},{14,10},{16,20},{18,... | collective-permute-start | bytes 3145736 | tf_op jit(solution)/shard_map/ppermute | solution.py:40
  306.5 61.4 %collective-permute-start.45 = (bf16[128,2048]{1,0:T(8,128)(2,1)}, bf16[128,2048]{1,0:T(8,128)(2,1)S(1)}, u32[]{:S(2)}, u32[]{:S(2)}) collective-permute-start(bf16[128,2048]{1,0:T(8,128)(2,1)} %slice.486), channel_id=1, source_target_pairs={{0,2},{2,0},{4,6},{6,4},{8,10},{10,8},{12,14},{14,12},{16,18},{18,... | collective-permute-start | bytes 1572872 | tf_op jit(solution)/shard_map/ppermute | solution.py:40
  307.0 60.9 %collective-permute-start.46 = (bf16[128,2048]{1,0:T(8,128)(2,1)}, bf16[128,2048]{1,0:T(8,128)(2,1)}, u32[]{:S(2)}, u32[]{:S(2)}) collective-permute-start(bf16[128,2048]{1,0:T(8,128)(2,1)} %slice.487), channel_id=1, source_target_pairs={{0,4},{2,6},{4,0},{6,2},{8,12},{10,14},{12,8},{14,10},{16,20},{18,... | collective-permute-start | bytes 1572872 | tf_op jit(solution)/shard_map/ppermute | solution.py:40
  377.1 30.4 %collective-permute-start.49 = (bf16[1024,2048]{1,0:T(8,128)(2,1)}, bf16[1024,2048]{1,0:T(8,128)(2,1)}, u32[]{:S(2)}, u32[]{:S(2)}) collective-permute-start(bf16[1024,2048]{1,0:T(8,128)(2,1)} %constant_dynamic-update-slice_fusion.31), channel_id=1, source_target_pairs={{0,1},{1,0},{2,3},{3,2},{4,5},{5,4},{6,7},{7,6},{8,9},{9,8},{10,11... | collective-permute-start | bytes 12582920 | tf_op jit(solution)/shard_map/ppermute | solution.py:44
  480.2 34.9 %collective-permute-start.53 = (bf16[4,4,64,2048]{3,2,1,0:T(8,128)(2,1)}, bf16[4,4,64,2048]{3,2,1,0:T(8,128)(2,1)}, u32[]{:S(2)}, u32[]{:S(2)}) collective-permute-start(bf16[4,4,64,2048]{3,2,1,0:T(8,128)(2,1)} %bitcast.29), channel_id=1, source_target_pairs={{0,1},{1,0},{2,3},{3,2},{4,5},{5,4},{6,7},{7,6},{8,9},{9,8},{10,11... | collective-permute-start | bytes 12582920 | tf_op jit(solution)/shard_map/ppermute | solution.py:44
  537.6 31.2 %collective-permute-start.56 = (bf16[4,4,64,2048]{3,2,1,0:T(8,128)(2,1)}, bf16[4,4,64,2048]{3,2,1,0:T(8,128)(2,1)S(1)}, u32[]{:S(2)}, u32[]{:S(2)}) collective-permute-start(bf16[4,4,64,2048]{3,2,1,0:T(8,128)(2,1)} %bitcast.32), channel_id=1, source_target_pairs={{0,1},{1,0},{2,3},{3,2},{4,5},{5,4},{6,7},{7,6},{8,9},{9,8},{10,11... | collective-permute-start | bytes 12582920 | tf_op jit(solution)/shard_map/ppermute | solution.py:44
  537.6 31.2 %collective-permute-start.54 = (bf16[2,64,2048]{2,1,0:T(8,128)(2,1)}, bf16[2,64,2048]{2,1,0:T(8,128)(2,1)S(1)}, u32[]{:S(2)}, u32[]{:S(2)}) collective-permute-start(bf16[2,64,2048]{2,1,0:T(8,128)(2,1)} %get-tuple-element.342), channel_id=1, source_target_pairs={{0,2},{2,0},{4,6},{6,4},{8,10},{10,8},{12,14},{14,12},{16,18},{18,... | collective-permute-start | bytes 1572872 | tf_op jit(solution)/shard_map/ppermute | solution.py:40
  592.8 44.6 %collective-permute-start.61 = (bf16[4,4,64,2048]{3,2,1,0:T(8,128)(2,1)}, bf16[4,4,64,2048]{3,2,1,0:T(8,128)(2,1)}, u32[]{:S(2)}, u32[]{:S(2)}) collective-permute-start(bf16[4,4,64,2048]{3,2,1,0:T(8,128)(2,1)} %bitcast.41), channel_id=1, source_target_pairs={{0,1},{1,0},{2,3},{3,2},{4,5},{5,4},{6,7},{7,6},{8,9},{9,8},{10,11... | collective-permute-start | bytes 12582920 | tf_op jit(solution)/shard_map/ppermute | solution.py:44
  592.8 44.6 %collective-permute-start.57 = (bf16[4,64,2048]{2,1,0:T(8,128)(2,1)}, bf16[4,64,2048]{2,1,0:T(8,128)(2,1)}, u32[]{:S(2)}, u32[]{:S(2)}) collective-permute-start(bf16[4,64,2048]{2,1,0:T(8,128)(2,1)} %pad_maximum_fusion.8), channel_id=1, source_target_pairs={{0,2},{2,0},{4,6},{6,4},{8,10},{10,8},{12,14},{14,12},{16,18},{18,... | collective-permute-start | bytes 3145736 | tf_op jit(solution)/shard_map/ppermute | solution.py:40
  594.3 43.1 %collective-permute-start.58 = (bf16[4,64,2048]{2,1,0:T(8,128)(2,1)}, bf16[4,64,2048]{2,1,0:T(8,128)(2,1)}, u32[]{:S(2)}, u32[]{:S(2)}) collective-permute-start(bf16[4,64,2048]{2,1,0:T(8,128)(2,1)} %pad_maximum_fusion.9), channel_id=1, source_target_pairs={{0,4},{2,6},{4,0},{6,2},{8,12},{10,14},{12,8},{14,10},{16,20},{18,... | collective-permute-start | bytes 3145736 | tf_op jit(solution)/shard_map/ppermute | solution.py:40
  655.9 51.5 %collective-permute-start.65 = (bf16[4,64,2048]{2,1,0:T(8,128)(2,1)}, bf16[4,64,2048]{2,1,0:T(8,128)(2,1)}, u32[]{:S(2)}, u32[]{:S(2)}) collective-permute-start(bf16[4,64,2048]{2,1,0:T(8,128)(2,1)} %pad_maximum_fusion.10), channel_id=1, source_target_pairs={{0,2},{2,0},{4,6},{6,4},{8,10},{10,8},{12,14},{14,12},{16,18},{18,... | collective-permute-start | bytes 3145736 | tf_op jit(solution)/shard_map/ppermute | solution.py:40
  657.0 50.4 %collective-permute-start.66 = (bf16[4,64,2048]{2,1,0:T(8,128)(2,1)}, bf16[4,64,2048]{2,1,0:T(8,128)(2,1)}, u32[]{:S(2)}, u32[]{:S(2)}) collective-permute-start(bf16[4,64,2048]{2,1,0:T(8,128)(2,1)} %pad_maximum_fusion.11), channel_id=1, source_target_pairs={{0,4},{2,6},{4,0},{6,2},{8,12},{10,14},{12,8},{14,10},{16,20},{18,... | collective-permute-start | bytes 3145736 | tf_op jit(solution)/shard_map/ppermute | solution.py:40
  661.4 46.0 %collective-permute-start.67 = (bf16[2,64,2048]{2,1,0:T(8,128)(2,1)}, bf16[2,64,2048]{2,1,0:T(8,128)(2,1)}, u32[]{:S(2)}, u32[]{:S(2)}) collective-permute-start(bf16[2,64,2048]{2,1,0:T(8,128)(2,1)} %get-tuple-element.369), channel_id=1, source_target_pairs={{0,2},{2,0},{4,6},{6,4},{8,10},{10,8},{12,14},{14,12},{16,18},{18,... | collective-permute-start | bytes 1572872 | tf_op jit(solution)/shard_map/ppermute | solution.py:40
  670.6 36.8 %collective-permute-start.68 = (bf16[2,64,2048]{2,1,0:T(8,128)(2,1)}, bf16[2,64,2048]{2,1,0:T(8,128)(2,1)}, u32[]{:S(2)}, u32[]{:S(2)}) collective-permute-start(bf16[2,64,2048]{2,1,0:T(8,128)(2,1)} %get-tuple-element.370), channel_id=1, source_target_pairs={{0,4},{2,6},{4,0},{6,2},{8,12},{10,14},{12,8},{14,10},{16,20},{18,... | collective-permute-start | bytes 1572872 | tf_op jit(solution)/shard_map/ppermute | solution.py:40
  671.1 36.2 %collective-permute-start.64 = (bf16[64,2048]{1,0:T(8,128)(2,1)}, bf16[64,2048]{1,0:T(8,128)(2,1)S(1)}, u32[]{:S(2)}, u32[]{:S(2)}) collective-permute-start(bf16[64,2048]{1,0:T(8,128)(2,1)} %get-tuple-element.366), channel_id=1, source_target_pairs={{0,24},{2,26},{4,28},{6,30},{8,16},{10,18},{12,20},{14,22},{16,8},... | collective-permute-start | bytes 786440 | tf_op jit(solution)/shard_map/ppermute | solution.py:40
  716.7 50.3 %collective-permute-start.72 = (bf16[4,64,2048]{2,1,0:T(8,128)(2,1)}, bf16[4,64,2048]{2,1,0:T(8,128)(2,1)}, u32[]{:S(2)}, u32[]{:S(2)}) collective-permute-start(bf16[4,64,2048]{2,1,0:T(8,128)(2,1)} %pad_maximum_fusion.12), channel_id=1, source_target_pairs={{0,2},{2,0},{4,6},{6,4},{8,10},{10,8},{12,14},{14,12},{16,18},{18,... | collective-permute-start | bytes 3145736 | tf_op jit(solution)/shard_map/ppermute | solution.py:40
  717.0 50.0 %collective-permute-start.73 = (bf16[4,64,2048]{2,1,0:T(8,128)(2,1)}, bf16[4,64,2048]{2,1,0:T(8,128)(2,1)}, u32[]{:S(2)}, u32[]{:S(2)}) collective-permute-start(bf16[4,64,2048]{2,1,0:T(8,128)(2,1)} %pad_maximum_fusion.13), channel_id=1, source_target_pairs={{0,4},{2,6},{4,0},{6,2},{8,12},{10,14},{12,8},{14,10},{16,20},{18,... | collective-permute-start | bytes 3145736 | tf_op jit(solution)/shard_map/ppermute | solution.py:40
  718.3 48.7 %collective-permute-start.69 = (bf16[64,2048]{1,0:T(8,128)(2,1)}, bf16[64,2048]{1,0:T(8,128)(2,1)S(1)}, u32[]{:S(2)}, u32[]{:S(2)}) collective-permute-start(bf16[64,2048]{1,0:T(8,128)(2,1)} %get-tuple-element.383), channel_id=1, source_target_pairs={{0,8},{2,10},{4,12},{6,14},{8,0},{10,2},{12,4},{14,6},{16,24},{18,... | collective-permute-start | bytes 786440 | tf_op jit(solution)/shard_map/ppermute | solution.py:40
  718.3 48.7 %collective-permute-start.70 = (bf16[64,2048]{1,0:T(8,128)(2,1)}, bf16[64,2048]{1,0:T(8,128)(2,1)S(1)}, u32[]{:S(2)}, u32[]{:S(2)}) collective-permute-start(bf16[64,2048]{1,0:T(8,128)(2,1)} %get-tuple-element.384), channel_id=1, source_target_pairs={{0,16},{2,18},{4,20},{6,22},{8,24},{10,26},{12,28},{14,30},{16,0},... | collective-permute-start | bytes 786440 | tf_op jit(solution)/shard_map/ppermute | solution.py:40
  718.9 48.1 %collective-permute-start.71 = (bf16[64,2048]{1,0:T(8,128)(2,1)}, bf16[64,2048]{1,0:T(8,128)(2,1)S(1)}, u32[]{:S(2)}, u32[]{:S(2)}) collective-permute-start(bf16[64,2048]{1,0:T(8,128)(2,1)} %get-tuple-element.385), channel_id=1, source_target_pairs={{0,24},{2,26},{4,28},{6,30},{8,16},{10,18},{12,20},{14,22},{16,8},... | collective-permute-start | bytes 786440 | tf_op jit(solution)/shard_map/ppermute | solution.py:40
  777.2 40.2 %collective-permute-start.77 = (bf16[4,4,64,2048]{3,2,1,0:T(8,128)(2,1)}, bf16[4,4,64,2048]{3,2,1,0:T(8,128)(2,1)}, u32[]{:S(2)}, u32[]{:S(2)}) collective-permute-start(bf16[4,4,64,2048]{3,2,1,0:T(8,128)(2,1)} %bitcast.64), channel_id=1, source_target_pairs={{0,1},{1,0},{2,3},{3,2},{4,5},{5,4},{6,7},{7,6},{8,9},{9,8},{10,11... | collective-permute-start | bytes 12582920 | tf_op jit(solution)/shard_map/ppermute | solution.py:44
  777.3 40.1 %collective-permute-start.74 = (bf16[64,2048]{1,0:T(8,128)(2,1)}, bf16[64,2048]{1,0:T(8,128)(2,1)S(1)}, u32[]{:S(2)}, u32[]{:S(2)}) collective-permute-start(bf16[64,2048]{1,0:T(8,128)(2,1)} %get-tuple-element.403), channel_id=1, source_target_pairs={{0,8},{2,10},{4,12},{6,14},{8,0},{10,2},{12,4},{14,6},{16,24},{18,... | collective-permute-start | bytes 786440 | tf_op jit(solution)/shard_map/ppermute | solution.py:40
  777.4 40.1 %collective-permute-start.75 = (bf16[64,2048]{1,0:T(8,128)(2,1)}, bf16[64,2048]{1,0:T(8,128)(2,1)}, u32[]{:S(2)}, u32[]{:S(2)}) collective-permute-start(bf16[64,2048]{1,0:T(8,128)(2,1)} %get-tuple-element.404), channel_id=1, source_target_pairs={{0,16},{2,18},{4,20},{6,22},{8,24},{10,26},{12,28},{14,30},{16,0},... | collective-permute-start | bytes 786440 | tf_op jit(solution)/shard_map/ppermute | solution.py:40
  777.9 39.5 %collective-permute-start.76 = (bf16[64,2048]{1,0:T(8,128)(2,1)}, bf16[64,2048]{1,0:T(8,128)(2,1)}, u32[]{:S(2)}, u32[]{:S(2)}) collective-permute-start(bf16[64,2048]{1,0:T(8,128)(2,1)} %get-tuple-element.405), channel_id=1, source_target_pairs={{0,24},{2,26},{4,28},{6,30},{8,16},{10,18},{12,20},{14,22},{16,8},... | collective-permute-start | bytes 786440 | tf_op jit(solution)/shard_map/ppermute | solution.py:40
  865.5 36.4 %collective-permute-start.81 = (bf16[4,64,2048]{2,1,0:T(8,128)(2,1)S(1)}, bf16[4,64,2048]{2,1,0:T(8,128)(2,1)S(1)}, u32[]{:S(2)}, u32[]{:S(2)}) collective-permute-start(bf16[4,64,2048]{2,1,0:T(8,128)(2,1)S(1)} %pad_maximum_fusion.14), channel_id=1, source_target_pairs={{0,2},{2,0},{4,6},{6,4},{8,10},{10,8},{12,14},{14,12},{16,18},{18,... | collective-permute-start | bytes 3145736 | tf_op jit(solution)/shard_map/ppermute | solution.py:40
  865.8 36.1 %collective-permute-start.82 = (bf16[4,64,2048]{2,1,0:T(8,128)(2,1)S(1)}, bf16[4,64,2048]{2,1,0:T(8,128)(2,1)S(1)}, u32[]{:S(2)}, u32[]{:S(2)}) collective-permute-start(bf16[4,64,2048]{2,1,0:T(8,128)(2,1)S(1)} %pad_maximum_fusion.15), channel_id=1, source_target_pairs={{0,4},{2,6},{4,0},{6,2},{8,12},{10,14},{12,8},{14,10},{16,20},{18,... | collective-permute-start | bytes 3145736 | tf_op jit(solution)/shard_map/ppermute | solution.py:40
  904.8 33.7 %collective-permute-start.91 = (bf16[4,128,1024]{2,1,0:T(8,128)(2,1)S(1)}, bf16[4,128,1024]{2,1,0:T(8,128)(2,1)S(1)}, u32[]{:S(2)}, u32[]{:S(2)}) collective-permute-start(bf16[4,128,1024]{2,1,0:T(8,128)(2,1)S(1)} %pad_maximum_fusion.16), channel_id=1, source_target_pairs={{0,2},{2,0},{4,6},{6,4},{8,10},{10,8},{12,14},{14,12},{16,18},{18,... | collective-permute-start | bytes 3145736 | tf_op jit(solution)/shard_map/ppermute | solution.py:40
  906.5 32.0 %collective-permute-start.92 = (bf16[4,128,1024]{2,1,0:T(8,128)(2,1)S(1)}, bf16[4,128,1024]{2,1,0:T(8,128)(2,1)S(1)}, u32[]{:S(2)}, u32[]{:S(2)}) collective-permute-start(bf16[4,128,1024]{2,1,0:T(8,128)(2,1)S(1)} %pad_maximum_fusion.17), channel_id=1, source_target_pairs={{0,4},{2,6},{4,0},{6,2},{8,12},{10,14},{12,8},{14,10},{16,20},{18,... | collective-permute-start | bytes 3145736 | tf_op jit(solution)/shard_map/ppermute | solution.py:40
  968.4 49.5 %collective-permute-start.100 = (f32[128,1024]{1,0:T(8,128)}, f32[128,1024]{1,0:T(8,128)}, u32[]{:S(2)}, u32[]{:S(2)}) collective-permute-start(f32[128,1024]{1,0:T(8,128)} %get-tuple-element.493), channel_id=1, source_target_pairs={{0,1},{1,0},{2,3},{3,2},{4,5},{5,4},{6,7},{7,6},{8,9},{9,8},{10,11... | collective-permute-start | bytes 1572872 | tf_op jit(solution)/shard_map/ppermute | solution.py:44
  (217 other events, 2809.8 us)

commit v2 on v1

v2 whole, which is shorter than its diff:
```python
import math

import jax
import jax.numpy as jnp
from jax import lax
from jax.experimental import pallas as pl
from jax.experimental.pallas import tpu as pltpu
from jax.sharding import PartitionSpec as P

D = 1024
HEAD_WIDTH = 64
FF = 4096
CLASSES = 1000
LEN = 800
ITEMS = 8
NSCALES = 10
MICRO = 2
STEP = 10


EPSILON = 1e-06
SOFTMAX_WARMTH = 12.0
CLIP_NORM = 0.001
BETA_ONE = 0.9
BETA_TWO = 0.95
DECAY = 0.05
ADAM_EPSILON = 1e-08
PYRAMID = (1, 5, 14, 30, 55, 91, 155, 255, 424)

SCORE_SCALE = SOFTMAX_WARMTH / HEAD_WIDTH
GELU_C = math.sqrt(2.0 / math.pi)
PAIR = 2 * HEAD_WIDTH
BLOCK = 512
ATTEND_FLOPS = LEN * PAIR * (8 * D + 4 * LEN)
VMEM_LIMIT = 60 * 2**20

bf16 = jnp.bfloat16
f32 = jnp.float32
barrier = lax.optimization_barrier


def swap(values, bits):
    n = lax.axis_size("dp")
    return lax.ppermute(values, "dp", [(i, i ^ bits) for i in range(n)])


def swap_core(values):
    return lax.ppermute(values, "mp", [(0, 1), (1, 0)])


def quarter():
    return lax.axis_size("dp") // 4


def columns_of_chips():
    n = lax.axis_size("dp")
    return [[xy + 4 * z for z in range(n // 4)] for xy in range(4)]


def over_z(values):
    return lax.all_to_all(values, "dp", 0, 0, tiled=True, axis_index_groups=columns_of_chips())


def sum_z(values):
    return lax.psum_scatter(values, "dp", scatter_dimension=0, axis_index_groups=columns_of_chips())


def join_kernel(*refs):
    parts, out = refs[:-1], refs[-1]
    at = 0
    for part in parts:
        rows = part.shape[0]
        out[at : at + rows, :] = part[...]
        at += rows


def join(parts):
    rows = sum(part.shape[0] for part in parts)
    total = parts[0].shape[1]
    return pl.pallas_call(
        join_kernel,
        grid=(total // BLOCK,),
        in_specs=[pl.BlockSpec((part.shape[0], BLOCK), lambda i: (0, i)) for part in parts],
        out_specs=pl.BlockSpec((rows, BLOCK), lambda i: (0, i)),
        out_shape=jax.ShapeDtypeStruct((rows, total), parts[0].dtype),
    )(*parts)


class Gather:
    def __init__(self, block):
        self.block = block
        self.step = 0

    def request(self):
        if self.step == 0:
            return jnp.broadcast_to(self.block[None], (quarter(),) + self.block.shape)
        if self.step == 1:
            return self.group
        if self.step == 2:
            half = self.group.shape[0] // 2
            return (self.from_y[:half], self.from_x[half:])
        return self.own

    def send(self, values):
        self.step += 1
        if self.step == 1:
            return over_z(values)
        if self.step == 2:
            return swap(values, 1), swap(values, 2)
        if self.step == 3:
            return swap(values[0], 1), swap(values[1], 2)
        return swap_core(values)

    def accept(self, out):
        if self.step == 1:
            self.group = out.reshape((-1,) + self.block.shape[1:])
        elif self.step == 2:
            self.from_x, self.from_y = out
        elif self.step == 3:
            self.own = join([self.group, self.from_x, self.from_y, *out])
        else:
            self.peer = out


class Exchange:
    def __init__(self, block, behind=False):
        self.block = block
        self.behind = behind
        self.step = 0

    def request(self):
        n = lax.axis_size("dp")
        if self.step == 1:
            return self.own
        return self.block if self.behind else jnp.broadcast_to(self.block[None], (n,) + self.block.shape)

    def send(self, values):
        self.step += 1
        if self.step == 2:
            return swap_core(values)
        if self.behind:
            self.own = lax.all_gather(values, "dp", axis=0, tiled=True)
            return None
        return lax.all_to_all(values, "dp", 0, 0, tiled=True)

    def accept(self, out):
        if self.step == 2:
            self.peer = out
        elif not self.behind:
            self.own = out.reshape(-1, out.shape[-1])


class Scatter:
    def __init__(self, peer, own=None, behind=False, wide=False, dtype=bf16):
        self.wide = wide
        self.dtype = dtype
        self.peer = peer
        self.own = own
        self.behind = behind
        self.step = 0 if peer is not None else 1

    def group(self, g, part=slice(None)):
        n = lax.axis_size("dp")
        shape = (4, n // 4, self.own.shape[0] // n) + self.own.shape[1:]
        total = self.own.reshape(shape)[g, part].astype(f32)
        if self.peer is not None:
            total = total + self.other.reshape(shape)[g, part].astype(f32)
        return total

    def request(self):
        if self.step == 0:
            return self.peer
        half = quarter() // 2
        low, high = slice(0, half), slice(half, None)
        if self.step == 1:
            values = (self.group(3, low), self.group(3, high))
        elif self.step == 2:
            values = (
                jnp.concatenate([self.group(1, low), self.group(1, high) + self.diagonal[1].astype(f32)]),
                jnp.concatenate([self.group(2, low) + self.diagonal[0].astype(f32), self.group(2, high)]),
            )
        else:
            values = self.group(0) + self.sides[0].astype(f32) + self.sides[1].astype(f32)
            if self.behind and self.wide:
                return values
        return jax.tree.map(lambda value: value.astype(self.dtype), values)

    def send(self, values):
        self.step += 1
        if self.step == 1:
            return swap_core(values)
        if self.step < 4:
            return swap(values[0], 1), swap(values[1], 2)
        if self.behind:
            self.total = sum_z(values).astype(f32)
            return None
        return over_z(values)

    def accept(self, out):
        if self.step == 1:
            self.other = out
        elif self.step == 2:
            self.diagonal = out
        elif self.step == 3:
            self.sides = out
        elif not self.behind:
            self.total = jnp.sum(out.astype(f32), axis=0)

    def result(self):
        return self.total


class Ticks:
    def __init__(self):
        self.last = []

    def wait(self, live=()):
        outs, live = barrier(([out for _, out in self.last], live))
        for (job, _), out in zip(self.last, outs):
            if out is not None:
                job.accept(out)
        self.last = []
        return live

    def __call__(self, jobs, live=()):
        values, live = barrier(([job.request() for job in jobs], live))
        self.last = [(job, job.send(value)) for job, value in zip(jobs, values)]
        return live


def small_gather(values):
    group = jnp.stack([values] + [swap(values, 4 * j) for j in range(1, quarter())])
    group = jnp.concatenate([group] + [swap(group, g) for g in (1, 2, 3)])
    apart = jnp.bitwise_xor(jnp.arange(4 * quarter(), dtype=jnp.int32), lax.axis_index("dp"))
    return jnp.take(group, (apart & 3) * quarter() + (apart >> 2), axis=0)


def total_over_all(values):
    count = lax.axis_size("dp") * lax.axis_size("mp")
    parts = jnp.broadcast_to(values[None], (count,) + values.shape)
    return jnp.sum(lax.all_to_all(parts, ("dp", "mp"), 0, 0, tiled=True), axis=0)


def place_of(index):
    apart = jnp.bitwise_xor(index, lax.axis_index("dp")) & 3
    return apart * quarter() + (index >> 2)


def layout(lengths):
    ends = jnp.cumsum(lengths)
    places = jnp.arange(LEN, dtype=jnp.int32)
    passed = places[:, None] >= ends[None, :]
    segment = jnp.sum(passed.astype(jnp.int32), axis=1)
    start = jnp.sum(jnp.where(passed, lengths[None, :], 0), axis=1)
    offset = places - start
    bounds = jnp.array(PYRAMID, dtype=jnp.int32)
    scale_id = jnp.sum((offset[:, None] >= bounds[None, :]).astype(jnp.int32), axis=1)
    usable = places < ends[-1]
    return (segment, scale_id, usable)


def matmul(left, right):
    return jnp.dot(left, right, preferred_element_type=f32)


def matmul_tn(left, right):
    return lax.dot_general(left, right, (((0,), (0,)), ((), ())), preferred_element_type=f32)


def matmul_nt(left, right):
    return lax.dot_general(left, right, (((1,), (1,)), ((), ())), preferred_element_type=f32)


def exact_tn(left, right):
    return lax.dot_general(
        left,
        right,
        (((0,), (0,)), ((), ())),
        precision=lax.Precision.HIGHEST,
        preferred_element_type=f32,
    )


def unit_pair(values):
    factor = lax.rsqrt(jnp.mean(values * values, axis=-1, keepdims=True) + EPSILON)
    return factor, (values * factor).astype(bf16)


def unit_back(values, factor, grad):
    inner = jnp.mean(grad * values, axis=-1, keepdims=True)
    return (factor * (grad - values * (factor * factor * inner))).astype(bf16)


def normed(values):
    centered = values - jnp.mean(values, axis=-1, keepdims=True)
    factor = lax.rsqrt(jnp.mean(centered * centered, axis=-1, keepdims=True) + EPSILON)
    return centered * factor, factor


def normed_back(hat, factor, grad):
    inner = jnp.mean(grad * hat, axis=-1, keepdims=True)
    return factor * (grad - jnp.mean(grad, axis=-1, keepdims=True) - hat * inner)


def spread(hot, part):
    high = part.astype(bf16).astype(f32)
    mid = (part - high).astype(bf16).astype(f32)
    low = part - high - mid
    return matmul(hot, jnp.concatenate([high, mid, low], axis=0).astype(bf16))


def item_sum(hot_t, values):
    high = values.astype(bf16)
    low = (values - high.astype(f32)).astype(bf16)
    return matmul(hot_t, high) + matmul(hot_t, low)


def flip(values):
    return values.astype(f32).T.astype(bf16)


def gelu_parts(values):
    inner = GELU_C * (values + 0.044715 * values * values * values)
    cdf = 0.5 * (1.0 + jnp.tanh(inner))
    return cdf, values * cdf


def gelu_slope(values, cdf):
    return cdf + values * (2.0 * cdf * (1.0 - cdf)) * (GELU_C * (1.0 + 0.134145 * values * values))


def whole(*shape):
    return pl.BlockSpec(shape, lambda *_: (0,) * len(shape), pipeline_mode=pl.Buffered(1))


def columns(rows, width):
    return pl.BlockSpec((rows, width), lambda i: (0, i))


def sds(shape, dtype):
    return jax.ShapeDtypeStruct(shape, dtype)


def kernel_call(body, grid, in_specs, out_specs, out_shape, flops, scratch=()):
    return pl.pallas_call(
        body,
        grid=grid,
        in_specs=in_specs,
        out_specs=out_specs,
        out_shape=out_shape,
        scratch_shapes=list(scratch),
        compiler_params=pltpu.CompilerParams(vmem_limit_bytes=VMEM_LIMIT),
        cost_estimate=pl.CostEstimate(flops=flops, transcendentals=0, bytes_accessed=2**24),
    )


def add_up(ref, part, start=None):
    first = pl.program_id(0) == 0

    @pl.when(first)
    def _():
        ref[...] = part if start is None else start[...] + part

    @pl.when(jnp.logical_not(first))
    def _():
        ref[...] += part


def at_end(fn):
    pl.when(pl.program_id(0) == pl.num_programs(0) - 1)(fn)


def embed_kernel(code_ref, own_ref, peer_ref, turn_ref, hot_ref, mod_ref, tok_ref, na_ref, na_t_ref, acc):
    step, steps = pl.program_id(0), pl.num_programs(0)
    rows = own_ref.shape[0]
    lane = lax.broadcasted_iota(jnp.int32, (LEN, rows), 1) + step * rows
    hot_own = (lane == code_ref[...]).astype(bf16)
    hot_peer = (lane + steps * rows == code_ref[...]).astype(bf16)
    add_up(acc, matmul(hot_own, own_ref[...]) + matmul(hot_peer, peer_ref[...]))

    @at_end
    def _():
        tokens = matmul(acc[...].astype(bf16), turn_ref[...])
        tok_ref[...] = tokens.astype(bf16)
        hat, _ = normed(tokens)
        out = hat * (1.0 + spread(hot_ref[...], mod_ref[:, :D])) + spread(hot_ref[...], mod_ref[:, D:])
        na_ref[...] = out.astype(bf16)
        na_t_ref[...] = flip(out)


def embed(code_rows, own, peer, turn, hot, mod):
    rows = own.shape[0]
    block = rows // 4
    rows_spec = pl.BlockSpec((block, D), lambda i: (i, 0))
    return kernel_call(
        embed_kernel,
        (4,),
        [whole(LEN, 1), rows_spec, rows_spec, whole(D, D), whole(LEN, 24), whole(ITEMS, 2 * D)],
        [whole(LEN, D), whole(LEN, D), whole(D, LEN)],
        [sds((LEN, D), bf16), sds((LEN, D), bf16), sds((D, LEN), bf16)],
        4 * LEN * rows * D,
        [pltpu.VMEM((LEN, D), f32)],
    )(code_rows, own, peer, turn, hot, mod)


def attend_pair(na_ref, w_ref, bias_ref):
    raw = matmul(na_ref[...], w_ref[:, : 3 * PAIR])
    outs = []
    for head in range(2):
        cut = [slice(i * PAIR + head * HEAD_WIDTH, i * PAIR + (head + 1) * HEAD_WIDTH) for i in range(3)]
        _, query_n = unit_pair(raw[:, cut[0]])
        _, key_n = unit_pair(raw[:, cut[1]])
        raised = jnp.exp(matmul_nt(query_n, key_n) * SCORE_SCALE + bias_ref[...])
        share = 1.0 / jnp.sum(raised, axis=-1, keepdims=True)
        outs.append(matmul((raised * share).astype(bf16), raw[:, cut[2]].astype(bf16)).astype(bf16))
    return jnp.concatenate(outs, axis=1)


def attend_first_kernel(na_ref, w_ref, bias_ref, out_ref, acc_ref):
    out = attend_pair(na_ref, w_ref, bias_ref)
    out_ref[...] = out
    add_up(acc_ref, matmul_nt(out, w_ref[:, 3 * PAIR :]))


def attend_last_kernel(
    na_ref, w_ref, bias_ref, part_ref, tok_ref, hot_ref, mod_ref, out_ref, acc_ref, mid_ref, nm_ref, nm_t_ref
):
    out = attend_pair(na_ref, w_ref, bias_ref)
    out_ref[...] = out
    add_up(acc_ref, matmul_nt(out, w_ref[:, 3 * PAIR :]), part_ref)

    @at_end
    def _():
        middle = tok_ref[...].astype(f32) + spread(hot_ref[...], mod_ref[:, :D]) * acc_ref[...]
        mid_ref[...] = middle
        hat, _ = normed(middle)
        out = hat * (1.0 + spread(hot_ref[...], mod_ref[:, D : 2 * D])) + spread(
            hot_ref[...], mod_ref[:, 2 * D :]
        )
        nm_ref[...] = out.astype(bf16)
        nm_t_ref[...] = flip(out)


def attend_first(na, w, bias):
    steps = w.shape[1] // (4 * PAIR)
    return kernel_call(
        attend_first_kernel,
        (steps,),
        [whole(LEN, D), columns(D, 4 * PAIR), whole(LEN, LEN)],
        [columns(LEN, PAIR), whole(LEN, D)],
        [sds((LEN, steps * PAIR), bf16), sds((LEN, D), f32)],
        steps * ATTEND_FLOPS,
    )(na, w, bias)


def attend_last(na, w, bias, part, tokens, hot, mod):
    steps = w.shape[1] // (4 * PAIR)
    return kernel_call(
        attend_last_kernel,
        (steps,),
        [
            whole(LEN, D),
            columns(D, 4 * PAIR),
            whole(LEN, LEN),
            whole(LEN, D),
            whole(LEN, D),
            whole(LEN, 24),
            whole(ITEMS, 3 * D),
        ],
        [columns(LEN, PAIR), whole(LEN, D), whole(LEN, D), whole(LEN, D), whole(D, LEN)],
        [
            sds((LEN, steps * PAIR), bf16),
            sds((LEN, D), f32),
            sds((LEN, D), f32),
            sds((LEN, D), bf16),
            sds((D, LEN), bf16),
        ],
        steps * ATTEND_FLOPS,
    )(na, w, bias, part, tokens, hot, mod)


def attend_pair_back(na_ref, na_t_ref, go_ref, go_t_ref, o_ref, w_ref, bias_ref, dw_ref):
    raw = matmul(na_ref[...], w_ref[:, : 3 * PAIR])
    grad_att = matmul(go_ref[...], w_ref[:, 3 * PAIR :]).astype(bf16)
    results = [[], [], []]
    for head in range(2):
        cut = [slice(i * PAIR + head * HEAD_WIDTH, i * PAIR + (head + 1) * HEAD_WIDTH) for i in range(3)]
        query, key = raw[:, cut[0]], raw[:, cut[1]]
        query_f, query_n = unit_pair(query)
        key_f, key_n = unit_pair(key)
        value_b = raw[:, cut[2]].astype(bf16)
        grad_out = grad_att[:, head * HEAD_WIDTH : (head + 1) * HEAD_WIDTH]
        grad_q, grad_k, grad_v = [], 0.0, 0.0
        for low, high in ((0, 384), (384, LEN)):
            raised = jnp.exp(matmul_nt(key_n, query_n[low:high]) * SCORE_SCALE + bias_ref[:, low:high])
            attention = raised * (1.0 / jnp.sum(raised, axis=0, keepdims=True))
            grad_probs = matmul_nt(value_b, grad_out[low:high])
            row_dot = jnp.sum(attention * grad_probs, axis=0, keepdims=True)
            grad_scores = (attention * (grad_probs - row_dot)).astype(bf16)
            grad_v = grad_v + matmul(attention.astype(bf16), grad_out[low:high])
            grad_k = grad_k + matmul(grad_scores, query_n[low:high])
            grad_q.append(matmul_tn(key_n, grad_scores).T)
        grad_q = jnp.concatenate(grad_q, axis=0) * SCORE_SCALE
        results[0].append(unit_back(query, query_f, grad_q))
        results[1].append(unit_back(key, key_f, grad_k * SCORE_SCALE))
        results[2].append(grad_v.astype(bf16))
    grad_raw = jnp.concatenate([part for pair in results for part in pair], axis=1)
    dw_ref[:, : 3 * PAIR] = matmul(na_t_ref[...], grad_raw).astype(bf16)
    dw_ref[:, 3 * PAIR :] = matmul(go_t_ref[...], o_ref[...]).astype(bf16)
    return matmul_nt(grad_raw, w_ref[:, : 3 * PAIR])


def attend_back_first_kernel(na_ref, na_t_ref, go_ref, go_t_ref, o_ref, w_ref, bias_ref, dw_ref, acc_ref):
    add_up(acc_ref, attend_pair_back(na_ref, na_t_ref, go_ref, go_t_ref, o_ref, w_ref, bias_ref, dw_ref))


def attend_back_last_kernel(
    na_ref, na_t_ref, go_ref, go_t_ref, o_ref, w_ref, bias_ref,
    part_ref, tok_ref, gm_ref, hot_ref, hot_t_ref, mod_ref,
    dw_ref, gt_ref, items_ref, acc_ref,
):
    part = attend_pair_back(na_ref, na_t_ref, go_ref, go_t_ref, o_ref, w_ref, bias_ref, dw_ref)
    add_up(acc_ref, part, part_ref)

    @at_end
    def _():
        grad = acc_ref[...]
        hat, factor = normed(tok_ref[...].astype(f32))
        items_ref[:, :D] = item_sum(hot_t_ref[...], grad * hat)
        items_ref[:, D:] = item_sum(hot_t_ref[...], grad)
        inner = normed_back(hat, factor, grad * (1.0 + spread(hot_ref[...], mod_ref[...])))
        gt_ref[...] = (gm_ref[...] + inner).astype(bf16)


def attend_back_specs():
    return [
        whole(LEN, D),
        whole(D, LEN),
        whole(LEN, D),
        whole(D, LEN),
        columns(LEN, PAIR),
        columns(D, 4 * PAIR),
        whole(LEN, LEN),
    ]


def attend_back_first(na, na_t, go, go_t, out, w, bias_t):
    steps = w.shape[1] // (4 * PAIR)
    return kernel_call(
        attend_back_first_kernel,
        (steps,),
        attend_back_specs(),
        [columns(D, 4 * PAIR), whole(LEN, D)],
        [sds(w.shape, bf16), sds((LEN, D), f32)],
        3 * steps * ATTEND_FLOPS,
    )(na, na_t, go, go_t, out, w, bias_t)


def attend_back_last(na, na_t, go, go_t, out, w, bias_t, part, tokens, grad_middle, hot, hot_t, mod):
    steps = w.shape[1] // (4 * PAIR)
    return kernel_call(
        attend_back_last_kernel,
        (steps,),
        attend_back_specs()
        + [
            whole(LEN, D),
            whole(LEN, D),
            whole(LEN, D),
            whole(LEN, 24),
            whole(2 * ITEMS, LEN),
            whole(ITEMS, D),
        ],
        [columns(D, 4 * PAIR), whole(LEN, D), whole(2 * ITEMS, 2 * D)],
        [sds(w.shape, bf16), sds((LEN, D), bf16), sds((2 * ITEMS, 2 * D), f32)],
        3 * steps * ATTEND_FLOPS,
        [pltpu.VMEM((LEN, D), f32)],
    )(na, na_t, go, go_t, out, w, bias_t, part, tokens, grad_middle, hot, hot_t, mod)


def mlp_part(nm_ref, w_refs, h_refs):
    total = 0.0
    for w_ref, h_ref in zip(w_refs, h_refs):
        hidden = matmul(nm_ref[...], w_ref[:, :BLOCK])
        h_ref[...] = hidden
        _, active = gelu_parts(hidden)
        total = total + matmul_nt(active.astype(bf16), w_ref[:, BLOCK:])
    return total


def mlp_first_kernel(nm_ref, w0_ref, w1_ref, h0_ref, h1_ref, acc_ref):
    add_up(acc_ref, mlp_part(nm_ref, (w0_ref, w1_ref), (h0_ref, h1_ref)))


def mlp_last_kernel(
    nm_ref, w0_ref, w1_ref, part_ref, mid_ref, hot_ref, mod_ref, h0_ref, h1_ref, acc_ref, res_ref, nh_ref, nh_t_ref
):
    add_up(acc_ref, mlp_part(nm_ref, (w0_ref, w1_ref), (h0_ref, h1_ref)), part_ref)

    @at_end
    def _():
        residual = mid_ref[...] + spread(hot_ref[...], mod_ref[...]) * acc_ref[...]
        res_ref[...] = residual
        hat, _ = normed(residual)
        nh_ref[...] = hat.astype(bf16)
        nh_t_ref[...] = flip(hat)


def mlp_first(nm, ws):
    steps = ws[0].shape[1] // (2 * BLOCK)
    hidden = sds((LEN, steps * BLOCK), f32)
    *hiddens, acc = kernel_call(
        mlp_first_kernel,
        (steps,),
        [whole(LEN, D)] + [columns(D, 2 * BLOCK)] * 2,
        [columns(LEN, BLOCK)] * 2 + [whole(LEN, D)],
        [hidden, hidden, sds((LEN, D), f32)],
        8 * steps * LEN * D * BLOCK,
    )(nm, *ws)
    return hiddens, acc


def mlp_last(nm, ws, part, middle, hot, mod):
    steps = ws[0].shape[1] // (2 * BLOCK)
    hidden = sds((LEN, steps * BLOCK), f32)
    h0, h1, *rest = kernel_call(
        mlp_last_kernel,
        (steps,),
        [whole(LEN, D)]
        + [columns(D, 2 * BLOCK)] * 2
        + [whole(LEN, D), whole(LEN, D), whole(LEN, 24), whole(ITEMS, D)],
        [columns(LEN, BLOCK)] * 2 + [whole(LEN, D), whole(LEN, D), whole(LEN, D), whole(D, LEN)],
        [
            hidden,
            hidden,
            sds((LEN, D), f32),
            sds((LEN, D), f32),
            sds((LEN, D), bf16),
            sds((D, LEN), bf16),
        ],
        8 * steps * LEN * D * BLOCK,
    )(nm, *ws, part, middle, hot, mod)
    return [h0, h1], *rest


def mlp_part_back(nm_t_ref, g_ref, g_t_ref, h_refs, w_refs, dw_ref):
    total = 0.0
    for i, (h_ref, w_ref) in enumerate(zip(h_refs, w_refs)):
        hidden = h_ref[...]
        cdf, active = gelu_parts(hidden)
        at = 2 * i * BLOCK
        dw_ref[:, at + BLOCK : at + 2 * BLOCK] = matmul(g_t_ref[...], active.astype(bf16)).astype(bf16)
        grad_pre = (gelu_slope(hidden, cdf) * matmul(g_ref[...], w_ref[:, BLOCK:])).astype(bf16)
        dw_ref[:, at : at + BLOCK] = matmul(nm_t_ref[...], grad_pre).astype(bf16)
        total = total + matmul_nt(grad_pre, w_ref[:, :BLOCK])
    return total


def mlp_back_first_kernel(nm_t_ref, g_ref, g_t_ref, h0_ref, h1_ref, w0_ref, w1_ref, dw_ref, acc_ref):
    add_up(acc_ref, mlp_part_back(nm_t_ref, g_ref, g_t_ref, (h0_ref, h1_ref), (w0_ref, w1_ref), dw_ref))


def mlp_back_last_kernel(
    nm_t_ref, g_ref, g_t_ref, h0_ref, h1_ref, w0_ref, w1_ref,
    part_ref, mid_ref, gr_ref, out_ref, hot_ref, hot_t_ref, mod_ref,
    dw_ref, gm_ref, go_ref, go_t_ref, items_ref, acc_ref,
):
    part = mlp_part_back(nm_t_ref, g_ref, g_t_ref, (h0_ref, h1_ref), (w0_ref, w1_ref), dw_ref)
    add_up(acc_ref, part, part_ref)

    @at_end
    def _():
        grad = acc_ref[...]
        hat, factor = normed(mid_ref[...])
        items_ref[:, D : 2 * D] = item_sum(hot_t_ref[...], grad * hat)
        items_ref[:, 2 * D :] = item_sum(hot_t_ref[...], grad)
        grad_middle = gr_ref[...] + normed_back(
            hat, factor, grad * (1.0 + spread(hot_ref[...], mod_ref[:, D:]))
        )
        gm_ref[...] = grad_middle
        items_ref[:, :D] = item_sum(hot_t_ref[...], grad_middle * out_ref[...])
        grad_out = spread(hot_ref[...], mod_ref[:, :D]) * grad_middle
        go_ref[...] = grad_out.astype(bf16)
        go_t_ref[...] = flip(grad_out)


def mlp_back_specs():
    return (
        [whole(D, LEN), whole(LEN, D), whole(D, LEN)]
        + [columns(LEN, BLOCK)] * 2
        + [columns(D, 2 * BLOCK)] * 2
    )


def mlp_back_first(nm_t, g, g_t, hiddens, ws):
    steps = ws[0].shape[1] // (2 * BLOCK)
    return kernel_call(
        mlp_back_first_kernel,
        (steps,),
        mlp_back_specs(),
        [columns(D, 4 * BLOCK), whole(LEN, D)],
        [sds((D, 4 * steps * BLOCK), bf16), sds((LEN, D), f32)],
        16 * steps * LEN * D * BLOCK,
    )(nm_t, g, g_t, *hiddens, *ws)


def mlp_back_last(nm_t, g, g_t, hiddens, ws, part, middle, grad_res, attn_out, hot, hot_t, mod):
    steps = ws[0].shape[1] // (2 * BLOCK)
    return kernel_call(
        mlp_back_last_kernel,
        (steps,),
        mlp_back_specs()
        + [whole(LEN, D)] * 4
        + [whole(LEN, 24), whole(2 * ITEMS, LEN), whole(ITEMS, 2 * D)],
        [
            columns(D, 4 * BLOCK),
            whole(LEN, D),
            whole(LEN, D),
            whole(D, LEN),
            whole(2 * ITEMS, 3 * D),
        ],
        [
            sds((D, 4 * steps * BLOCK), bf16),
            sds((LEN, D), f32),
            sds((LEN, D), bf16),
            sds((D, LEN), bf16),
            sds((2 * ITEMS, 3 * D), f32),
        ],
        16 * steps * LEN * D * BLOCK,
        [pltpu.VMEM((LEN, D), f32)],
    )(nm_t, g, g_t, *hiddens, *ws, part, middle, grad_res, attn_out, hot, hot_t, mod)


def head_kernel(
    nh_ref, nh_t_ref, own_ref, peer_ref, target_ref, weight_ref, res_ref, mlp_ref, hot_ref, hot_t_ref, mod_ref,
    dw_own_ref, dw_peer_ref, loss_ref, gr_ref, gmo_ref, gmo_t_ref, items_ref,
    logits, most, total, chosen, acc,
):
    step = pl.program_id(0)
    half = pl.num_programs(0) // 2
    block = own_ref.shape[1]
    lane = lax.broadcasted_iota(jnp.int32, (LEN, block), 1)

    @pl.when(step == 0)
    def _():
        most[...] = jnp.full((LEN, 1), -1e30, f32)
        total[...] = jnp.zeros((LEN, 1), f32)
        chosen[...] = jnp.zeros((LEN, 1), f32)

    for which, w_ref, dw_ref in ((0, own_ref, dw_own_ref), (1, peer_ref, dw_peer_ref)):

        @pl.when(step < half)
        def _():
            place = step + which * half
            values = matmul(nh_ref[...], w_ref[...])
            logits[place] = values
            most_new = jnp.maximum(most[...], jnp.max(values, axis=1, keepdims=True))
            total[...] = total[...] * jnp.exp(most[...] - most_new) + jnp.sum(
                jnp.exp(values - most_new), axis=1, keepdims=True
            )
            most[...] = most_new
            is_target = lane + place * block == target_ref[...]
            chosen[...] += jnp.sum(jnp.where(is_target, values, 0.0), axis=1, keepdims=True)

    @pl.when(step == half - 1)
    def _():
        most[...] = most[...] + jnp.log(total[...])
        loss = jnp.sum(weight_ref[...] * (most[...] - chosen[...]), axis=0, keepdims=True)
        loss_ref[...] = jnp.broadcast_to(loss, (8, 128))

    for which, w_ref, dw_ref in ((0, own_ref, dw_own_ref), (1, peer_ref, dw_peer_ref)):

        @pl.when(step >= half)
        def _():
            place = step - half + which * half
            is_target = lane + place * block == target_ref[...]
            grad = (jnp.exp(logits[place] - most[...]) - is_target.astype(f32)) * weight_ref[...]
            grad = grad.astype(bf16)
            dw_ref[...] = matmul(nh_t_ref[...], grad).astype(bf16)
            part = matmul_nt(grad, w_ref[...])

            @pl.when(jnp.logical_and(step == half, which == 0))
            def _():
                acc[...] = part

            @pl.when(jnp.logical_not(jnp.logical_and(step == half, which == 0)))
            def _():
                acc[...] += part

    @at_end
    def _():
        hat, factor = normed(res_ref[...])
        grad_res = normed_back(hat, factor, acc[...])
        gr_ref[...] = grad_res
        items_ref[...] = item_sum(hot_t_ref[...], grad_res * mlp_ref[...])
        grad_mlp = spread(hot_ref[...], mod_ref[...]) * grad_res
        gmo_ref[...] = grad_mlp.astype(bf16)
        gmo_t_ref[...] = flip(grad_mlp)


def head(nh, nh_t, own, peer, target, weight, residual, mlp_out, hot, hot_t, mod):
    half = own.shape[1] // BLOCK
    w_spec = pl.BlockSpec((D, BLOCK), lambda i: (0, i % half))
    dw_spec = pl.BlockSpec((D, BLOCK), lambda i: (0, jnp.maximum(i - half, 0)))
    return kernel_call(
        head_kernel,
        (2 * half,),
        [
            whole(LEN, D),
            whole(D, LEN),
            w_spec,
            w_spec,
            whole(LEN, 1),
            whole(LEN, 1),
            whole(LEN, D),
            whole(LEN, D),
            whole(LEN, 24),
            whole(2 * ITEMS, LEN),
            whole(ITEMS, D),
        ],
        [
            dw_spec,
            dw_spec,
            whole(8, 128),
            whole(LEN, D),
            whole(LEN, D),
            whole(D, LEN),
            whole(2 * ITEMS, D),
        ],
        [
            sds(own.shape, bf16),
            sds(own.shape, bf16),
            sds((8, 128), f32),
            sds((LEN, D), f32),
            sds((LEN, D), bf16),
            sds((D, LEN), bf16),
            sds((2 * ITEMS, D), f32),
        ],
        12 * half * LEN * D * BLOCK,
        [
            pltpu.VMEM((2 * half, LEN, BLOCK), f32),
            pltpu.VMEM((LEN, 1), f32),
            pltpu.VMEM((LEN, 1), f32),
            pltpu.VMEM((LEN, 1), f32),
            pltpu.VMEM((LEN, D), f32),
        ],
    )(nh, nh_t, own, peer, target, weight, residual, mlp_out, hot, hot_t, mod)


def code_first_kernel(code_ref, gt_ref, turn_ref, out_ref, flat_ref):
    step, steps = pl.program_id(0), pl.num_programs(0)
    rows = out_ref.shape[0]

    @pl.when(step == 0)
    def _():
        flat_ref[...] = matmul_nt(gt_ref[...], turn_ref[...]).astype(bf16)

    row = lax.broadcasted_iota(jnp.int32, (rows, LEN), 0) + (step + steps) * rows
    out_ref[...] = matmul((row == code_ref[...]).astype(bf16), flat_ref[...]).astype(bf16)


def code_last_kernel(code_ref, flat_ref, out_ref):
    rows = out_ref.shape[0]
    row = lax.broadcasted_iota(jnp.int32, (rows, LEN), 0) + pl.program_id(0) * rows
    out_ref[...] = matmul((row == code_ref[...]).astype(bf16), flat_ref[...]).astype(bf16)


def code_back_first(code_rows, grad_tokens, turn, rows):
    spec = pl.BlockSpec((rows // 4, D), lambda i: (i, 0))
    out, flat = kernel_call(
        code_first_kernel,
        (4,),
        [whole(1, LEN), whole(LEN, D), whole(D, D)],
        [spec, whole(LEN, D)],
        [sds((rows, D), bf16), sds((LEN, D), bf16)],
        2 * LEN * rows * D,
    )(code_rows, grad_tokens, turn)
    return code_rows, flat, out


def code_back_last(code_rows, flat, rows):
    spec = pl.BlockSpec((rows // 4, D), lambda i: (i, 0))
    return kernel_call(
        code_last_kernel,
        (4,),
        [whole(1, LEN), whole(LEN, D)],
        spec,
        sds((rows, D), bf16),
        2 * LEN * rows * D,
    )(code_rows, flat)


def step_rates():
    return (
        2.5,
        2.5,
        2.5 / math.sqrt(D),
        2.5 / math.sqrt(D),
        2.5 / math.sqrt(D // 32),
        2.5 / math.sqrt(D),
        2.5 / math.sqrt(FF),
        5.0 / math.sqrt(D),
    )


def adamw_update(weight, grad, moment, square, rate):
    first = BETA_ONE * moment + (1.0 - BETA_ONE) * grad
    second = BETA_TWO * square + (1.0 - BETA_TWO) * grad * grad
    corrected = (
        first / (1.0 - BETA_ONE**STEP) / (jnp.sqrt(second / (1.0 - BETA_TWO**STEP)) + ADAM_EPSILON)
    )
    return (first, second, weight - rate * (corrected + DECAY * weight))


def on_device(
    input_codes,
    target_codes,
    item_lengths,
    item_labels,
    code_table,
    class_table,
    adaln_weight,
    qkv_weight,
    proj_weight,
    expand_weight,
    contract_weight,
    head_weight,
    code_moment,
    class_moment,
    adaln_moment,
    qkv_moment,
    proj_moment,
    expand_moment,
    contract_moment,
    head_moment,
    code_square,
    class_square,
    adaln_square,
    qkv_square,
    proj_square,
    expand_square,
    contract_square,
    head_square,
):
    masters = (
        code_table,
        class_table,
        adaln_weight,
        qkv_weight,
        proj_weight.T,
        expand_weight,
        contract_weight.T,
        head_weight,
    )
    moments = (
        code_moment,
        class_moment,
        adaln_moment,
        qkv_moment,
        proj_moment.T,
        expand_moment,
        contract_moment.T,
        head_moment,
    )
    squares = (
        code_square,
        class_square,
        adaln_square,
        qkv_square,
        proj_square.T,
        expand_square,
        contract_square.T,
        head_square,
    )
    n = lax.axis_size("dp")
    core = lax.axis_index("mp")
    rows = code_table.shape[0]
    half_rows = rows // 2
    width = proj_weight.shape[0]
    wide = expand_weight.shape[1]
    codes_local = head_weight.shape[1]

    def mine(values):
        return lax.dynamic_index_in_dim(values, core, 0, keepdims=False)

    pairs = width // PAIR
    code_block = lax.dynamic_slice_in_dim(code_table, core * half_rows, half_rows, 0).astype(bf16)
    attn_block = jnp.stack([qkv_weight[0], qkv_weight[1], qkv_weight[2], proj_weight.T], axis=1)
    attn_block = attn_block.reshape(-1, 4, pairs, PAIR).swapaxes(1, 2).reshape(-1, 4 * width)
    blocks = wide // BLOCK
    mlp_blocks = jnp.stack(
        [expand_weight.reshape(-1, blocks, BLOCK), contract_weight.T.reshape(-1, blocks, BLOCK)], axis=2
    ).astype(bf16)
    code_w, attn_w, mlp_a, mlp_b, head_w = [
        Gather(block)
        for block in (
            code_block,
            attn_block.astype(bf16),
            mlp_blocks[:, 0::2].reshape(-1, wide),
            mlp_blocks[:, 1::2].reshape(-1, wide),
            head_weight.astype(bf16),
        )
    ]
    begin = Ticks()
    begin([code_w])
    numbers = small_gather(jnp.stack([item_lengths[:, 0], item_labels[:, 0]], axis=1))
    positions = jnp.arange(n, dtype=jnp.int32)
    block_at = ((lax.axis_index("dp") & 3) ^ (positions // quarter())) + 4 * (positions % quarter())
    block_place = place_of(positions)
    labels = numbers[:, :, 1]
    labels_own = jnp.where(core == 0, labels[:, 0], labels[:, 1])
    labels_peer = jnp.where(core == 0, labels[:, 1], labels[:, 0])
    class_low = class_table.astype(bf16)
    adaln_low = adaln_weight.astype(bf16)

    def class_part(item_labels):
        ids = jnp.arange(CLASSES, dtype=jnp.int32)
        picked = (item_labels.reshape(-1, 1) == ids[None, :]).astype(bf16)
        class_rows = matmul(picked, class_low)
        return picked, class_rows, jax.nn.silu(class_rows).astype(bf16)

    _, _, class_vec = class_part(labels_own[block_at])
    order = (2, 4, 0, 1, 3, 5)
    adaln_parts = jnp.concatenate([adaln_low[:, i * D : (i + 1) * D] for i in order], axis=1)

    mod_parts = matmul(class_vec, adaln_parts)

    mod_job = Scatter(None, mod_parts, dtype=f32)
    attn_w.block, mod_job.own = begin.wait((attn_w.block, mod_job.own))
    begin([code_w, attn_w, mod_job])
    mlp_a.block = begin.wait(mlp_a.block)
    begin([code_w, mlp_a, mod_job])
    begin.wait()
    begin([code_w, attn_w, mod_job])
    begin.wait()

    lengths = mine(item_lengths)[0]
    code_ids = mine(input_codes)[0]
    target_ids = mine(target_codes)[0]
    segment, scale_id, usable = layout(lengths)
    bounds = jnp.array((0,) + PYRAMID, dtype=jnp.int32)
    sizes = jnp.array(PYRAMID + (LEN,), dtype=jnp.int32) - bounds
    all_lengths = numbers[:, :, 0].reshape(-1)
    scale_counts = jnp.sum(
        jnp.clip(all_lengths[:, None] - bounds[None, :], 0, sizes[None, :]), axis=0
    ).astype(f32)
    inv_counts = 1.0 / (NSCALES * jnp.maximum(scale_counts, 1.0))
    scale_hot = scale_id[:, None] == jnp.arange(NSCALES, dtype=jnp.int32)[None, :]
    token_weight = jnp.where(
        usable, jnp.sum(jnp.where(scale_hot, inv_counts[None, :], 0.0), axis=1), 0.0
    )
    same = segment[:, None] == segment[None, :]
    bias = jnp.where(same & (scale_id[None, :] <= scale_id[:, None]), 0.0, -1e30)
    bias_t = jnp.where(same & (scale_id[:, None] <= scale_id[None, :]), 0.0, -1e30)
    hot = (segment[:, None] == jnp.arange(3 * ITEMS, dtype=jnp.int32)[None, :] % ITEMS).astype(bf16)
    item_rows = jnp.arange(2 * ITEMS, dtype=jnp.int32)
    hot_t = ((segment[None, :] == item_rows[:, None]) & (item_rows[:, None] < ITEMS)).astype(bf16)

    block_width = D // n
    feature_place = (block_place[:, None] * block_width + jnp.arange(block_width)[None, :]).reshape(-1)
    turn = (feature_place[:, None] == jnp.arange(D, dtype=jnp.int32)[None, :]).astype(bf16)
    within = code_ids % rows
    other = (within // half_rows != core).astype(jnp.int32)
    code_rows = other * (n * half_rows) + place_of(code_ids // rows) * half_rows + within % half_rows
    target = jnp.where(target_ids // codes_local == core, 0, codes_local) + target_ids % codes_local

    def placed(values):
        values = values.reshape(-1, n, block_width)
        return jnp.take(values, block_at, axis=1).reshape(ITEMS, -1)

    def beside(*parts):
        return jnp.concatenate(parts, axis=1)

    mods_embed = placed(mod_job.total[:, : 2 * D])
    scale_attn = mods_embed[:, :D]
    code_col = code_rows.reshape(LEN, 1)

    code_own, code_peer, code_col = begin(
        [attn_w, mlp_a, mlp_b], (code_w.own, code_w.peer, code_col)
    )
    tokens, na, na_t = begin.wait(embed(code_col, code_own, code_peer, turn, hot, mods_embed))
    na = begin([attn_w, mlp_a, mlp_b, head_w], na)
    att_own, part = begin.wait(attend_first(na, attn_w.own, bias))
    mods = placed(mod_job.total[:, 2 * D :])
    gate_attn, gate_mlp, scale_mlp, shift_mlp = jnp.split(mods, 4, axis=1)
    mods_attend = beside(gate_attn, scale_mlp, shift_mlp)
    mods_back = beside(gate_attn, scale_mlp)
    part = begin([mlp_a, mlp_b, head_w], part)
    att_peer, attn_out, middle, nm, nm_t = begin.wait(
        attend_last(na, attn_w.peer, bias, part, tokens, hot, mods_attend)
    )
    nm = begin([mlp_b, head_w], nm)
    mlp_own = (mlp_a.own, mlp_b.own)
    hidden_own, part = begin.wait(mlp_first(nm, mlp_own))
    mlp_peer = (mlp_a.peer, mlp_b.peer)
    part = begin([head_w], part)
    hidden_peer, mlp_out, residual, nh, nh_t = begin.wait(
        mlp_last(nm, mlp_peer, part, middle, hot, gate_mlp)
    )
    dhead_own, dhead_peer, loss_tile, grad_res, gmo, gmo_t, items_head = head(
        nh, nh_t, head_w.own, head_w.peer, target.reshape(LEN, 1), token_weight.reshape(LEN, 1),
        residual, mlp_out, hot, hot_t, gate_mlp,
    )
    loss_local = loss_tile[0, 0]

    def turned(parts):
        values = beside(*parts)
        values = jnp.take(values.reshape(-1, n, block_width), block_place, axis=1)
        return values.reshape(ITEMS, -1).astype(bf16)

    head_job = Scatter(dhead_peer, dhead_own, behind=True, wide=True)
    gmo = begin([head_job], gmo)
    dmlp_peer, part = begin.wait(mlp_back_first(nm_t, gmo, gmo_t, hidden_peer, mlp_peer))
    mlp_job = Scatter(dmlp_peer, behind=True)
    part = begin([head_job, mlp_job], part)
    mlp_job.own, grad_middle, gao, gao_t, items_mlp = begin.wait(
        mlp_back_last(
            nm_t, gmo, gmo_t, hidden_own, mlp_own, part, middle, grad_res, attn_out, hot, hot_t, mods_back
        )
    )
    item_job = Exchange(turned([items_mlp[:ITEMS, :D], items_head[:ITEMS], items_mlp[:ITEMS, D:]]), behind=True)
    gao = begin([head_job, mlp_job, item_job], gao)
    dattn_peer, part = begin.wait(attend_back_first(na, na_t, gao, gao_t, att_peer, attn_w.peer, bias_t))
    attn_job = Scatter(dattn_peer)
    part = begin([head_job, mlp_job, attn_job], part)
    attn_job.own, grad_tokens, items_attn = begin.wait(
        attend_back_last(
            na, na_t, gao, gao_t, att_own, attn_w.own, bias_t, part, tokens, grad_middle, hot, hot_t, scale_attn
        )
    )
    late_job = Exchange(turned([items_attn[:ITEMS]]))
    grad_tokens = begin([attn_job, late_job, mlp_job], grad_tokens)
    code_row, flat, dcode_peer = begin.wait(
        code_back_first(code_rows.reshape(1, LEN), grad_tokens, turn, n * half_rows)
    )
    code_job = Scatter(dcode_peer)
    flat = begin([code_job, attn_job], flat)
    code_job.own = begin.wait(code_back_last(code_row, flat, n * half_rows))
    begin([code_job, item_job, late_job])
    begin.wait()
    begin([code_job, attn_job])
    begin.wait()
    head_job.total, mlp_job.total = begin([code_job], (head_job.total, mlp_job.total))
    begin.wait()

    def factor_part(item_labels, grads):
        picked, class_rows, class_vec = class_part(item_labels)
        grad_class_vec = matmul_nt(grads, adaln_low)
        _, silu_back = jax.vjp(jax.nn.silu, class_rows)
        return matmul_tn(class_vec, grads), exact_tn(picked.astype(f32), silu_back(grad_class_vec)[0])

    def grad_rows(which):
        early, late = getattr(item_job, which), getattr(late_job, which)
        order = [early[:, : 2 * D], late[:, :D], early[:, 2 * D : 3 * D], late[:, D:], early[:, 3 * D :]]
        return beside(*order)

    adaln_a, class_a = factor_part(labels_own, grad_rows("own"))
    adaln_b, class_b = factor_part(labels_peer, grad_rows("peer"))
    adaln_grad = adaln_a + adaln_b
    class_grad = class_a + class_b
    code_half = code_job.result()
    code_other = swap_core(code_half)
    code_grad = jnp.where(
        core == 0,
        jnp.concatenate([code_half, code_other]),
        jnp.concatenate([code_other, code_half]),
    )
    attn_grad = attn_job.result()
    kinds = attn_grad.reshape(-1, pairs, 4, PAIR).transpose(2, 0, 1, 3).reshape(4, -1, width)
    mlp_kinds = mlp_job.result().reshape(-1, blocks, 2, BLOCK)
    gradients = (
        code_grad,
        class_grad,
        adaln_grad,
        kinds[:3],
        kinds[3],
        mlp_kinds[:, :, 0].reshape(-1, wide),
        mlp_kinds[:, :, 1].reshape(-1, wide),
        head_job.result(),
    )
    shared_sq = jnp.sum(class_grad * class_grad) + jnp.sum(adaln_grad * adaln_grad)
    own_sq = jnp.sum(code_half * code_half) + jnp.sum(attn_grad * attn_grad)
    for grad in gradients[5:]:
        own_sq = own_sq + jnp.sum(grad * grad)
    totals = total_over_all(
        jnp.concatenate([(own_sq + 0.5 * shared_sq).reshape(1), loss_local.reshape(1)])
    )
    squared, loss = totals[0], totals[1]
    grad_norm = jnp.sqrt(squared)
    clip = jnp.minimum(1.0, CLIP_NORM / (grad_norm + 1e-06))
    firsts, seconds, updated = ([], [], [])
    for place, (weight, grad, moment, square, rate) in enumerate(
        zip(masters, gradients, moments, squares, step_rates())
    ):
        for kept, value in zip(
            (firsts, seconds, updated), adamw_update(weight, grad * clip, moment, square, rate)
        ):
            kept.append(value.T if place in (4, 6) else value)
    return (*firsts, *seconds, *updated, loss, scale_counts, grad_norm)


def solution(mesh):
    token_spec = P(None, "dp", None)
    weight_specs = (
        P("dp", None),
        P(None, "dp"),
        P("dp", None),
        P(None, "dp", "mp"),
        P("mp", "dp"),
        P("dp", "mp"),
        P("mp", "dp"),
        P("dp", "mp"),
    )
    return jax.shard_map(
        on_device,
        mesh=mesh,
        in_specs=(token_spec,) * 4 + weight_specs * 3,
        out_specs=weight_specs * 3 + (P(), P(), P()),
        check_vma=False,
    )
```

time: 1030 us -> 848 us (0.82)
  Pallas kernels: 94.1 us -> 368 us
  matrix products: 248 us -> 12.2 us
  other arithmetic: 212 us -> 115 us
  waiting for transfers between devices: 231 us -> 146 us
  local copies, waits for them, and re-layouts: 103 us -> 66.3 us
  starting transfers between devices: 127 us -> 107 us
  between operations: 9.64 us -> 24 us
    pallas_call x4 -> x17, Pallas kernels: 94.1 us -> 368 us  [the longest x1 53.1 us: attend_back_last(): kernel_call(attend_back_last_kernel, (steps,), attend_back_specs() + [who...]
    ppermute x94 -> x46, waiting for transfers between devices: 230 us -> 104 us  [swap(): return lax.ppermute(values, 'dp', [(i, i ^ bits) for i in range(n)])]
    dot_general x12 -> x2, matrix products: 78.4 us -> 1.35 us  [matmul_nt(): lax.dot_general(left, right, (((1,), (1,)), ((), ())), preferred_element_...]
    dot_general x13 -> x2, matrix products: 80.2 us -> 5.28 us  [matmul_tn(): lax.dot_general(left, right, (((0,), (0,)), ((), ())), preferred_element_...]
    dot_general x14 -> x3, matrix products: 76.3 us -> 2.71 us  [matmul(): return jnp.dot(left, right, preferred_element_type=f32)]
    ppermute x94 -> x46, starting transfers between devices: 126 us -> 56.4 us  [swap(): return lax.ppermute(values, 'dp', [(i, i ^ bits) for i in range(n)])]
    all_to_all x0 -> x10, starting transfers between devices: none -> 49.8 us  [the longest x8 41.6 us: over_z(): lax.all_to_all(values, 'dp', 0, 0, tiled=True, axis_index_groups=columns_...]
    all_to_all x0 -> x10, waiting for transfers between devices: none -> 41.4 us  [the longest x8 31.3 us: over_z(): lax.all_to_all(values, 'dp', 0, 0, tiled=True, axis_index_groups=columns_...]
  transfers between devices with their start and end apart: 107 -> 71, of which waited for: 37 -> 25; matrix products, arithmetic and copies ran while one was open for 36% -> 16% of each run, Pallas kernels for 9% -> 35%
where the time goes in v2:
time: 848 us; the launch traced here: 838 us
  Pallas kernels  368 us (43%)
  waiting for transfers between devices  146 us (17%)
  other arithmetic  115 us (14%)
  starting transfers between devices  107 us (13%)
  local copies, waits for them, and re-layouts  66.3 us (8%)
  between operations  24 us (3%)
  matrix products  12.2 us (1%)
    ppermute x46, waiting for transfers between devices, swap(): return lax.ppermute(values, 'dp', [(i, i ^ bits) for i in range(n)])  104 us
    ppermute x46, starting transfers between devices, swap(): return lax.ppermute(values, 'dp', [(i, i ^ bits) for i in range(n)])  56.4 us
    pallas_call x1, Pallas kernels, attend_back_last(): kernel_call(attend_back_last_kernel, (steps,), attend_back_specs() + [who...  53.1 us
    pallas_call x1, Pallas kernels, head(): kernel_call(head_kernel, (2 * half,), [whole(LEN, D), whole(D, LEN), w_sp...  49.3 us
    pallas_call x1, Pallas kernels, attend_back_first(): kernel_call(attend_back_first_kernel, (steps,), attend_back_specs(), [col...  47.2 us
    all_to_all x8, starting transfers between devices, over_z(): lax.all_to_all(values, 'dp', 0, 0, tiled=True, axis_index_groups=columns_...  41.6 us
    pallas_call x1, Pallas kernels, mlp_back_last(): kernel_call(mlp_back_last_kernel, (steps,), mlp_back_specs() + [whole(LEN...  36.5 us
    pallas_call x1, Pallas kernels, attend_last(): kernel_call(attend_last_kernel, (steps,), [whole(LEN, D), columns(D, 4 *...  35.3 us
  transfers between devices with their start and end apart: 71, of which 25 were waited for; matrix products, arithmetic and copies ran while one was open for 16% of the time, Pallas kernels for 35%

profile of v2, /device:TPU:0, one launch (start us, length us, event | category | flops | bytes accessed | tf_op | source)
XLA Modules:
  0.0 838.0 jit_solution(17652315387539549821)
XLA Ops:
  16.8 5.1 all-to-all-start
  38.4 8.4 %all-to-all-done = bf16[4,128,1024]{2,1,0:T(8,128)(2,1)} async-done(((bf16[4,128,1024]{2,1,0:T(8,128)(2,1)}), bf16[4,128,1024]{2,1,0:T(8,128)(2,1)}, u32[]{:S(2)}, u32[]{:S(2)}) %all-to-all-start) | async-done | bytes 1048608 | tf_op jit(solution)/shard_map/all_to_all | solution.py:61
  49.0 4.3 all-to-all-start.1
  70.2 15.9 %collective-permute-done.8 = f32[2,8,6144]{2,1,0:T(8,128)} collective-permute-done((f32[2,8,6144]{2,1,0:T(8,128)}, f32[2,8,6144]{2,1,0:T(8,128)}, u32[]{:S(2)}, u32[]{:S(2)}) %collective-permute-start.8) | collective-permute-done | bytes 393248 | tf_op jit(solution)/shard_map/ppermute | solution.py:44
  94.8 4.7 all-to-all-start.2
  103.6 24.4 %collective-permute-done.10.refs_3_ = bf16[256,1024]{1,0:T(8,128)(2,1)} collective-permute-done((bf16[256,1024]{1,0:T(8,128)(2,1)}, bf16[256,1024]{1,0:T(8,128)(2,1)}, u32[]{:S(2)}, u32[]{:S(2)}) %collective-permute-start.10) | collective-permute-done | bytes 524320 | tf_op jit(solution)/shard_map/ppermute | solution.py:44
  130.7 3.7 shard_map.502.own_ref
  134.5 4.8 all-to-all-start.3
  150.5 14.3 %collective-permute-done.15.refs_1_ = bf16[256,2048]{1,0:T(8,128)(2,1)S(1)} collective-permute-done((bf16[256,2048]{1,0:T(8,128)(2,1)}, bf16[256,2048]{1,0:T(8,128)(2,1)S(1)}, u32[]{:S(2)}, u32[]{:S(2)}) %collective-permute-start.15) | collective-permute-done | bytes 1048608 | tf_op jit(solution)/shard_map/ppermute | solution.py:44
  168.7 5.0 all-to-all-start.4
  182.1 16.9 %shard_map.503 = (bf16[800,1024]{1,0:T(8,128)(2,1)}, bf16[800,1024]{1,0:T(8,128)(2,1)}, bf16[1024,800]{1,0:T(8,128)(2,1)}) custom-call(s32[800,1]{1,0:T(8,128)} %get-tuple-element.271.code_ref, bf16[2048,1024]{1,0:T(8,128)(2,1)} %shard_map.502.own_ref, bf16[2048,1024]{1,0:T(8,128)(2,1)} %collective-permute-done.14.peer_ref, ...), custom_call_target="tpu_custom_call" | custom-call | flops 6710886400 | bytes 16777216 | tf_op jit(solution)/shard_map/pallas_call | solution.py:395
  199.1 11.4 %collective-permute-done.17.refs_3_ = bf16[128,2048]{1,0:T(8,128)(2,1)S(1)} collective-permute-done((bf16[128,2048]{1,0:T(8,128)(2,1)}, bf16[128,2048]{1,0:T(8,128)(2,1)S(1)}, u32[]{:S(2)}, u32[]{:S(2)}) %collective-permute-start.17) | collective-permute-done | bytes 524320 | tf_op jit(solution)/shard_map/ppermute | solution.py:44
  214.7 4.8 shard_map.504.w_ref
  220.6 4.8 all-to-all-start.5
  232.8 28.9 %shard_map.505 = (bf16[800,512]{1,0:T(8,128)(2,1)}, f32[800,1024]{1,0:T(8,128)}) custom-call(bf16[800,1024]{1,0:T(8,128)(2,1)} %get-tuple-element.289.na_ref, bf16[1024,2048]{1,0:T(8,128)(2,1)} %shard_map.504.w_ref, f32[800,800]{1,0:T(8,128)} %get-tuple-element.521.bias_ref), custom_call_target="tpu_custom_call" | custom-call | flops 4666163200 | bytes 16777216 | tf_op jit(solution)/shard_map/pallas_call | solution.py:446
  266.3 4.7 shard_map.506.w0_ref
  277.7 35.3 %shard_map.507 = (bf16[800,512]{1,0:T(8,128)(2,1)}, f32[800,1024]{1,0:T(8,128)}, f32[800,1024]{1,0:T(8,128)}, bf16[800,1024]{1,0:T(8,128)(2,1)}, bf16[1024,800]{1,0:T(8,128)(2,1)}) custom-call(bf16[800,1024]{1,0:T(8,128)(2,1)} %get-tuple-element.289.na_ref, bf16[1024,2048]{1,0:T(8,128)(2,1)} %collective-permute-done.21.w_ref, ...), custom_call_target="tpu_custom_call" | custom-call | flops 4666163200 | bytes 16777216 | tf_op jit(solution)/shard_map/pallas_call | solution.py:458
  313.9 5.1 shard_map.508.w1_ref
  321.6 14.0 %shard_map.509 = (f32[800,1024]{1,0:T(8,128)}, f32[800,1024]{1,0:T(8,128)}, f32[800,1024]{1,0:T(8,128)}) custom-call(bf16[800,1024]{1,0:T(8,128)(2,1)} %get-tuple-element.318.nm_ref, bf16[1024,2048]{1,0:T(8,128)(2,1)} %shard_map.506.w0_ref, bf16[1024,2048]{1,0:T(8,128)(2,1)} %shard_map.508.w1_ref), custom_call_target="tpu_custom_call" | custom-call | flops 6710886400 | bytes 16777216 | tf_op jit(solution)/shard_map/pallas_call | solution.py:611
  336.6 4.8 shard_map.510.own_ref
  345.1 19.4 %shard_map.511 = (f32[800,1024]{1,0:T(8,128)}, f32[800,1024]{1,0:T(8,128)}, f32[800,1024]{1,0:T(8,128)}, f32[800,1024]{1,0:T(8,128)}, bf16[800,1024]{1,0:T(8,128)(2,1)}, /*index=5*/bf16[1024,800]{1,0:T(8,128)(2,1)}) custom-call(bf16[800,1024]{1,0:T(8,128)(2,1)} %get-tuple-element.318.nm_ref, bf16[1024,2048]{1,0:T(8,128)(2,1)} %collective-permute-done.26.w0_ref, ...), custom_call_target="tpu_custom_call" | custom-call | flops 6710886400 | bytes 16777216 | tf_op jit(solution)/shard_map/pallas_call | solution.py:625
  364.5 49.3 %shard_map.512 = (bf16[1024,2048]{1,0:T(8,128)(2,1)}, bf16[1024,2048]{1,0:T(8,128)(2,1)}, f32[8,128]{1,0:T(8,128)}, f32[800,1024]{1,0:T(8,128)}, bf16[800,1024]{...) custom-call(bf16[800,1024]{1,0:T(8,128)(2,1)} %get-tuple-element.336.nh_ref, ...), custom_call_target="tpu_custom_call" | custom-call | flops 20132659200 | bytes 16777216 | tf_op jit(solution)/shard_map/pallas_call | solution.py:804
  414.4 26.4 %shard_map.513 = (bf16[1024,4096]{1,0:T(8,128)(2,1)}, f32[800,1024]{1,0:T(8,128)}) custom-call(bf16[1024,800]{1,0:T(8,128)(2,1)} %get-tuple-element.345.nm_t_ref, bf16[800,1024]{1,0:T(8,128)(2,1)} %get-tuple-element.346.g_ref, bf16[1024,800]{1,0:T(8,128)(2,1)} %get-tuple-element.347.g_t_ref, f32[800,1024]{1,0:T(8,128)} %get-tuple-element.348.h0_ref, ...), custom_call_target="tpu_custom_call" | custom-call | flops 13421772800 | bytes 16777216 | tf_op jit(solution)/shard_map/pallas_call | solution.py:696
  440.9 4.0 fusion.25
  447.9 36.5 %shard_map.514 = (bf16[1024,4096]{1,0:T(8,128)(2,1)}, f32[800,1024]{1,0:T(8,128)}, bf16[800,1024]{1,0:T(8,128)(2,1)}, bf16[1024,800]{1,0:T(8,128)(2,1)}, f32[16,3072]{1,0:T(8,128)}) custom-call(bf16[1024,800]{1,0:T(8,128)(2,1)} %get-tuple-element.345.nm_t_ref, bf16[800,1024]{1,0:T(8,128)(2,1)} %get-tuple-element.346.g_ref, ...), custom_call_target="tpu_custom_call" | custom-call | flops 13421772800 | bytes 16777216 | tf_op jit(solution)/shard_map/pallas_call | solution.py:708
  489.9 5.2 fusion.10
  503.5 47.2 %shard_map.515 = (bf16[1024,2048]{1,0:T(8,128)(2,1)}, f32[800,1024]{1,0:T(8,128)}) custom-call(bf16[800,1024]{1,0:T(8,128)(2,1)} %get-tuple-element.289.na_ref, bf16[1024,800]{1,0:T(8,128)(2,1)} %get-tuple-element.379.na_t_ref, bf16[800,1024]{1,0:T(8,128)(2,1)} %get-tuple-element.380.go_ref, bf16[1024,800]{1,0:T(8,128)(2,1)} %get-tuple-element.381.go_t_ref, ...), custom_call_target="tpu_custom_call" | custom-call | flops 13998489600 | bytes 16777216 | tf_op jit(solution)/shard_map/pallas_call | solution.py:549
  550.8 4.0 fusion.3
  564.5 5.0 convert_add_fusion
  569.5 53.1 %shard_map.516 = (bf16[1024,2048]{1,0:T(8,128)(2,1)}, bf16[800,1024]{1,0:T(8,128)(2,1)}, f32[16,2048]{1,0:T(8,128)}) custom-call(bf16[800,1024]{1,0:T(8,128)(2,1)} %get-tuple-element.289.na_ref, bf16[1024,800]{1,0:T(8,128)(2,1)} %get-tuple-element.379.na_t_ref, bf16[800,1024]{1,0:T(8,128)(2,1)} %get-tuple-element.380.go_ref, ...), custom_call_target="tpu_custom_call" | custom-call | flops 13998489600 | bytes 16777216 | tf_op jit(solution)/shard_map/pallas_call | solution.py:561
  624.5 4.0 fusion.29
  628.5 3.9 add_convert_fusion
  633.2 5.5 all-to-all-start.6
  642.9 10.0 %shard_map.517 = (bf16[2048,1024]{1,0:T(8,128)(2,1)}, bf16[800,1024]{1,0:T(8,128)(2,1)}) custom-call(s32[1,800]{1,0:T(1,128)} %fusion.93.code_ref, bf16[800,1024]{1,0:T(8,128)(2,1)} %get-tuple-element.409.gt_ref, bf16[1024,1024]{1,0:T(8,128)(2,1)} %fusion.turn_ref), custom_call_target="tpu_custom_call" | custom-call | flops 3355443200 | bytes 16777216 | tf_op jit(solution)/shard_map/pallas_call | solution.py:869
  652.9 3.6 collective-permute-done.46
  657.4 3.8 all-to-all-done.6
  680.2 7.5 shard_map.518
  687.7 9.1 %collective-permute-done.49 = bf16[4,64,2048]{2,1,0:T(8,128)(2,1)} collective-permute-done((bf16[4,64,2048]{2,1,0:T(8,128)(2,1)}, bf16[4,64,2048]{2,1,0:T(8,128)(2,1)}, u32[]{:S(2)}, u32[]{:S(2)}) %collective-permute-start.49) | collective-permute-done | bytes 1048608 | tf_op jit(solution)/shard_map/ppermute | solution.py:44
  698.8 4.2 fusion.33
  714.6 5.0 collective-permute-done.51
  727.5 8.6 %all-to-all-start.7 = ((bf16[4,64,2048]{2,1,0:T(8,128)(2,1)}), bf16[4,64,2048]{2,1,0:T(8,128)(2,1)S(1)}, u32[]{:S(2)}, u32[]{:S(2)}) async-start(bf16[4,64,2048]{2,1,0:T(8,128)(2,1)} %add_convert_fusion.2), calls=%async_computation.7 | async-start | bytes 2097152 | tf_op jit(solution)/shard_map/all_to_all | solution.py:61
  741.7 8.3 collective-permute-done.55
  750.3 10.6 %all-to-all-done.7 = bf16[4,64,2048]{2,1,0:T(8,128)(2,1)S(1)} async-done(((bf16[4,64,2048]{2,1,0:T(8,128)(2,1)}), bf16[4,64,2048]{2,1,0:T(8,128)(2,1)S(1)}, u32[]{:S(2)}, u32[]{:S(2)}) %all-to-all-start.7) | async-done | bytes 1048608 | tf_op jit(solution)/shard_map/all_to_all | solution.py:61
  760.9 4.0 add_convert_fusion.1
  764.9 4.4 all-to-all-start.8
  771.1 3.8 multiply_reduce_fusion
  782.3 12.3 %all-to-all-done.8 = bf16[4,128,1024]{2,1,0:T(8,128)(2,1)} async-done(((bf16[4,128,1024]{2,1,0:T(8,128)(2,1)}), bf16[4,128,1024]{2,1,0:T(8,128)(2,1)}, u32[]{:S(2)}, u32[]{:S(2)}) %all-to-all-start.8) | async-done | bytes 1048608 | tf_op jit(solution)/shard_map/all_to_all | solution.py:61
  805.0 6.2 all-to-all-done.9
  (503 shorter events, 227.4 us)
Async XLA Ops:
  16.8 30.1 %all-to-all-start = ((bf16[4,128,1024]{2,1,0:T(8,128)(2,1)}), bf16[4,128,1024]{2,1,0:T(8,128)(2,1)}, u32[]{:S(2)}, u32[]{:S(2)}) async-start(bf16[4,128,1024]{2,1,0:T(8,128)(2,1)} %broadcast_in_dim.88), calls=%async_computation | async-start | bytes 2097152 | tf_op jit(solution)/shard_map/all_to_all | solution.py:61
  49.0 38.4 %all-to-all-start.1 = ((bf16[4,64,2048]{2,1,0:T(8,128)(2,1)}), bf16[4,64,2048]{2,1,0:T(8,128)(2,1)}, u32[]{:S(2)}, u32[]{:S(2)}) async-start(bf16[4,64,2048]{2,1,0:T(8,128)(2,1)} %broadcast_in_dim.91), calls=%async_computation.1 | async-start | bytes 2097152 | tf_op jit(solution)/shard_map/all_to_all | solution.py:61
  53.2 34.1 %collective-permute-start.6 = (bf16[512,1024]{1,0:T(8,128)(2,1)}, bf16[512,1024]{1,0:T(8,128)(2,1)}, u32[]{:S(2)}, u32[]{:S(2)}) collective-permute-start(bf16[512,1024]{1,0:T(8,128)(2,1)} %bitcast.10.refs_0_), channel_id=1, source_target_pairs={{0,2},{2,0},{4,6},{6,4},{8,10},{10,8},{12,14},{14,12},{16,18},{18,... | collective-permute-start | bytes 3145736 | tf_op jit(solution)/shard_map/ppermute | solution.py:44
  54.8 32.6 %collective-permute-start.7 = (bf16[512,1024]{1,0:T(8,128)(2,1)}, bf16[512,1024]{1,0:T(8,128)(2,1)}, u32[]{:S(2)}, u32[]{:S(2)}) collective-permute-start(bf16[512,1024]{1,0:T(8,128)(2,1)} %bitcast.10.refs_0_), channel_id=1, source_target_pairs={{0,4},{2,6},{4,0},{6,2},{8,12},{10,14},{12,8},{14,10},{16,20},{18,... | collective-permute-start | bytes 3145736 | tf_op jit(solution)/shard_map/ppermute | solution.py:44
  56.3 29.8 %collective-permute-start.8 = (f32[2,8,6144]{2,1,0:T(8,128)}, f32[2,8,6144]{2,1,0:T(8,128)}, u32[]{:S(2)}, u32[]{:S(2)}) collective-permute-start(f32[2,8,6144]{2,1,0:T(8,128)} %get-tuple-element.243), channel_id=1, source_target_pairs={{0,2},{2,0},{4,6},{6,4},{8,10},{10,8},{12,14},{14,12},{16,18},{18,... | collective-permute-start | bytes 1179656 | tf_op jit(solution)/shard_map/ppermute | solution.py:44
  56.8 30.5 %collective-permute-start.9 = (f32[2,8,6144]{2,1,0:T(8,128)}, f32[2,8,6144]{2,1,0:T(8,128)}, u32[]{:S(2)}, u32[]{:S(2)}) collective-permute-start(f32[2,8,6144]{2,1,0:T(8,128)} %get-tuple-element.244), channel_id=1, source_target_pairs={{0,4},{2,6},{4,0},{6,2},{8,12},{10,14},{12,8},{14,10},{16,20},{18,... | collective-permute-start | bytes 1179656 | tf_op jit(solution)/shard_map/ppermute | solution.py:44
  94.8 33.5 %all-to-all-start.2 = ((bf16[4,64,2048]{2,1,0:T(8,128)(2,1)}), bf16[4,64,2048]{2,1,0:T(8,128)(2,1)}, u32[]{:S(2)}, u32[]{:S(2)}) async-start(bf16[4,64,2048]{2,1,0:T(8,128)(2,1)} %broadcast_in_dim.92), calls=%async_computation.2 | async-start | bytes 2097152 | tf_op jit(solution)/shard_map/all_to_all | solution.py:61
  99.5 28.7 %collective-permute-start.12 = (f32[4,8,6144]{2,1,0:T(8,128)}, f32[4,8,6144]{2,1,0:T(8,128)}, u32[]{:S(2)}, u32[]{:S(2)}) collective-permute-start(f32[4,8,6144]{2,1,0:T(8,128)} %get-tuple-element.254), channel_id=1, source_target_pairs={{0,2},{2,0},{4,6},{6,4},{8,10},{10,8},{12,14},{14,12},{16,18},{18,... | collective-permute-start | bytes 2359304 | tf_op jit(solution)/shard_map/ppermute | solution.py:44
  100.1 28.2 %collective-permute-start.13 = (f32[4,8,6144]{2,1,0:T(8,128)}, f32[4,8,6144]{2,1,0:T(8,128)}, u32[]{:S(2)}, u32[]{:S(2)}) collective-permute-start(f32[4,8,6144]{2,1,0:T(8,128)} %get-tuple-element.255), channel_id=1, source_target_pairs={{0,4},{2,6},{4,0},{6,2},{8,12},{10,14},{12,8},{14,10},{16,20},{18,... | collective-permute-start | bytes 2359304 | tf_op jit(solution)/shard_map/ppermute | solution.py:44
  101.6 26.4 %collective-permute-start.10 = (bf16[256,1024]{1,0:T(8,128)(2,1)}, bf16[256,1024]{1,0:T(8,128)(2,1)}, u32[]{:S(2)}, u32[]{:S(2)}) collective-permute-start(bf16[256,1024]{1,0:T(8,128)(2,1)} %slice.370), channel_id=1, source_target_pairs={{0,2},{2,0},{4,6},{6,4},{8,10},{10,8},{12,14},{14,12},{16,18},{18,... | collective-permute-start | bytes 1572872 | tf_op jit(solution)/shard_map/ppermute | solution.py:44
  134.4 31.5 %collective-permute-start.14 = (bf16[2048,1024]{1,0:T(8,128)(2,1)}, bf16[2048,1024]{1,0:T(8,128)(2,1)}, u32[]{:S(2)}, u32[]{:S(2)}) collective-permute-start(bf16[2048,1024]{1,0:T(8,128)(2,1)} %shard_map.502.own_ref), channel_id=1, source_target_pairs={{0,1},{1,0},{2,3},{3,2},{4,5},{5,4},{6,7},{7,6},{8,9},{9,8},{10,11... | collective-permute-start | bytes 12582920 | tf_op jit(solution)/shard_map/ppermute | solution.py:48
  134.5 31.4 %all-to-all-start.3 = ((f32[4,8,6144]{2,1,0:T(8,128)}), f32[4,8,6144]{2,1,0:T(8,128)S(1)}, u32[]{:S(2)}, u32[]{:S(2)}) async-start(f32[4,8,6144]{2,1,0:T(8,128)} %fusion.18), calls=%async_computation.3 | async-start | bytes 1572864 | tf_op jit(solution)/shard_map/all_to_all | solution.py:61
  168.7 42.8 %all-to-all-start.4 = ((bf16[4,64,2048]{2,1,0:T(8,128)(2,1)}), bf16[4,64,2048]{2,1,0:T(8,128)(2,1)S(1)}, u32[]{:S(2)}, u32[]{:S(2)}) async-start(bf16[4,64,2048]{2,1,0:T(8,128)(2,1)} %broadcast_in_dim.94), calls=%async_computation.4 | async-start | bytes 2097152 | tf_op jit(solution)/shard_map/all_to_all | solution.py:61
  175.6 35.2 %collective-permute-start.19 = (bf16[256,2048]{1,0:T(8,128)(2,1)}, bf16[256,2048]{1,0:T(8,128)(2,1)S(1)}, u32[]{:S(2)}, u32[]{:S(2)}) collective-permute-start(bf16[256,2048]{1,0:T(8,128)(2,1)} %bitcast.21.refs_0_), channel_id=1, source_target_pairs={{0,2},{2,0},{4,6},{6,4},{8,10},{10,8},{12,14},{14,12},{16,18},{18,... | collective-permute-start | bytes 3145736 | tf_op jit(solution)/shard_map/ppermute | solution.py:44
  176.3 35.3 %collective-permute-start.20 = (bf16[256,2048]{1,0:T(8,128)(2,1)}, bf16[256,2048]{1,0:T(8,128)(2,1)}, u32[]{:S(2)}, u32[]{:S(2)}) collective-permute-start(bf16[256,2048]{1,0:T(8,128)(2,1)} %bitcast.21.refs_0_), channel_id=1, source_target_pairs={{0,4},{2,6},{4,0},{6,2},{8,12},{10,14},{12,8},{14,10},{16,20},{18,... | collective-permute-start | bytes 3145736 | tf_op jit(solution)/shard_map/ppermute | solution.py:44
  180.3 30.1 %collective-permute-start.17 = (bf16[128,2048]{1,0:T(8,128)(2,1)}, bf16[128,2048]{1,0:T(8,128)(2,1)S(1)}, u32[]{:S(2)}, u32[]{:S(2)}) collective-permute-start(bf16[128,2048]{1,0:T(8,128)(2,1)} %slice.377), channel_id=1, source_target_pairs={{0,2},{2,0},{4,6},{6,4},{8,10},{10,8},{12,14},{14,12},{16,18},{18,... | collective-permute-start | bytes 1572872 | tf_op jit(solution)/shard_map/ppermute | solution.py:44
  181.6 29.1 %collective-permute-start.18 = (bf16[128,2048]{1,0:T(8,128)(2,1)}, bf16[128,2048]{1,0:T(8,128)(2,1)S(1)}, u32[]{:S(2)}, u32[]{:S(2)}) collective-permute-start(bf16[128,2048]{1,0:T(8,128)(2,1)} %slice.378), channel_id=1, source_target_pairs={{0,4},{2,6},{4,0},{6,2},{8,12},{10,14},{12,8},{14,10},{16,20},{18,... | collective-permute-start | bytes 1572872 | tf_op jit(solution)/shard_map/ppermute | solution.py:44
  220.6 42.6 %collective-permute-start.21 = (bf16[1024,2048]{1,0:T(8,128)(2,1)}, bf16[1024,2048]{1,0:T(8,128)(2,1)}, u32[]{:S(2)}, u32[]{:S(2)}) collective-permute-start(bf16[1024,2048]{1,0:T(8,128)(2,1)} %shard_map.504.w_ref), channel_id=1, source_target_pairs={{0,1},{1,0},{2,3},{3,2},{4,5},{5,4},{6,7},{7,6},{8,9},{9,8},{10,11... | collective-permute-start | bytes 12582920 | tf_op jit(solution)/shard_map/ppermute | solution.py:48
  220.6 42.6 %all-to-all-start.5 = ((bf16[4,64,2048]{2,1,0:T(8,128)(2,1)}), bf16[4,64,2048]{2,1,0:T(8,128)(2,1)S(1)}, u32[]{:S(2)}, u32[]{:S(2)}) async-start(bf16[4,64,2048]{2,1,0:T(8,128)(2,1)} %broadcast_in_dim.95), calls=%async_computation.5 | async-start | bytes 2097152 | tf_op jit(solution)/shard_map/all_to_all | solution.py:61
  225.4 442.4 %all-gather.2.cloned.1.call-start = ((), (), s32[]{:S(2)}) async-start(), calls=%async_computation.12 | async-start | bytes 1114112 | tf_op jit(solution)/shard_map/all_gather | solution.py:142
  225.4 37.8 %collective-permute-start.24 = (bf16[256,2048]{1,0:T(8,128)(2,1)S(1)}, bf16[256,2048]{1,0:T(8,128)(2,1)S(1)}, u32[]{:S(2)}, u32[]{:S(2)}) collective-permute-start(bf16[256,2048]{1,0:T(8,128)(2,1)S(1)} %bitcast.276), channel_id=1, source_target_pairs={{0,2},{2,0},{4,6},{6,4},{8,10},{10,8},{12,14},{14,12},{16,18},{18,... | collective-permute-start | bytes 3145736 | tf_op jit(solution)/shard_map/ppermute | solution.py:44
  226.8 36.4 %collective-permute-start.25 = (bf16[256,2048]{1,0:T(8,128)(2,1)S(1)}, bf16[256,2048]{1,0:T(8,128)(2,1)}, u32[]{:S(2)}, u32[]{:S(2)}) collective-permute-start(bf16[256,2048]{1,0:T(8,128)(2,1)S(1)} %bitcast.277), channel_id=1, source_target_pairs={{0,4},{2,6},{4,0},{6,2},{8,12},{10,14},{12,8},{14,10},{16,20},{18,... | collective-permute-start | bytes 3145736 | tf_op jit(solution)/shard_map/ppermute | solution.py:44
  228.4 33.5 %collective-permute-start.22 = (bf16[128,2048]{1,0:T(8,128)(2,1)}, bf16[128,2048]{1,0:T(8,128)(2,1)S(1)}, u32[]{:S(2)}, u32[]{:S(2)}) collective-permute-start(bf16[128,2048]{1,0:T(8,128)(2,1)} %slice.381), channel_id=1, source_target_pairs={{0,2},{2,0},{4,6},{6,4},{8,10},{10,8},{12,14},{14,12},{16,18},{18,... | collective-permute-start | bytes 1572872 | tf_op jit(solution)/shard_map/ppermute | solution.py:44
  229.1 34.0 %collective-permute-start.23 = (bf16[128,2048]{1,0:T(8,128)(2,1)}, bf16[128,2048]{1,0:T(8,128)(2,1)}, u32[]{:S(2)}, u32[]{:S(2)}) collective-permute-start(bf16[128,2048]{1,0:T(8,128)(2,1)} %slice.382), channel_id=1, source_target_pairs={{0,4},{2,6},{4,0},{6,2},{8,12},{10,14},{12,8},{14,10},{16,20},{18,... | collective-permute-start | bytes 1572872 | tf_op jit(solution)/shard_map/ppermute | solution.py:44
  271.1 42.7 %collective-permute-start.26 = (bf16[1024,2048]{1,0:T(8,128)(2,1)}, bf16[1024,2048]{1,0:T(8,128)(2,1)}, u32[]{:S(2)}, u32[]{:S(2)}) collective-permute-start(bf16[1024,2048]{1,0:T(8,128)(2,1)} %shard_map.506.w0_ref), channel_id=1, source_target_pairs={{0,1},{1,0},{2,3},{3,2},{4,5},{5,4},{6,7},{7,6},{8,9},{9,8},{10,11... | collective-permute-start | bytes 12582920 | tf_op jit(solution)/shard_map/ppermute | solution.py:48
  271.9 41.1 %collective-permute-start.29 = (bf16[256,2048]{1,0:T(8,128)(2,1)S(1)}, bf16[256,2048]{1,0:T(8,128)(2,1)S(1)}, u32[]{:S(2)}, u32[]{:S(2)}) collective-permute-start(bf16[256,2048]{1,0:T(8,128)(2,1)S(1)} %bitcast.279), channel_id=1, source_target_pairs={{0,2},{2,0},{4,6},{6,4},{8,10},{10,8},{12,14},{14,12},{16,18},{18,... | collective-permute-start | bytes 3145736 | tf_op jit(solution)/shard_map/ppermute | solution.py:44
  272.9 40.2 %collective-permute-start.30 = (bf16[256,2048]{1,0:T(8,128)(2,1)S(1)}, bf16[256,2048]{1,0:T(8,128)(2,1)S(1)}, u32[]{:S(2)}, u32[]{:S(2)}) collective-permute-start(bf16[256,2048]{1,0:T(8,128)(2,1)S(1)} %bitcast.280), channel_id=1, source_target_pairs={{0,4},{2,6},{4,0},{6,2},{8,12},{10,14},{12,8},{14,10},{16,20},{18,... | collective-permute-start | bytes 3145736 | tf_op jit(solution)/shard_map/ppermute | solution.py:44
  275.4 37.6 %collective-permute-start.27 = (bf16[128,2048]{1,0:T(8,128)(2,1)}, bf16[128,2048]{1,0:T(8,128)(2,1)S(1)}, u32[]{:S(2)}, u32[]{:S(2)}) collective-permute-start(bf16[128,2048]{1,0:T(8,128)(2,1)} %slice.383), channel_id=1, source_target_pairs={{0,2},{2,0},{4,6},{6,4},{8,10},{10,8},{12,14},{14,12},{16,18},{18,... | collective-permute-start | bytes 1572872 | tf_op jit(solution)/shard_map/ppermute | solution.py:44
  276.5 36.5 %collective-permute-start.28 = (bf16[128,2048]{1,0:T(8,128)(2,1)}, bf16[128,2048]{1,0:T(8,128)(2,1)}, u32[]{:S(2)}, u32[]{:S(2)}) collective-permute-start(bf16[128,2048]{1,0:T(8,128)(2,1)} %slice.384), channel_id=1, source_target_pairs={{0,4},{2,6},{4,0},{6,2},{8,12},{10,14},{12,8},{14,10},{16,20},{18,... | collective-permute-start | bytes 1572872 | tf_op jit(solution)/shard_map/ppermute | solution.py:44
  413.9 27.0 %collective-permute-start.35 = (bf16[1024,2048]{1,0:T(8,128)(2,1)}, bf16[1024,2048]{1,0:T(8,128)(2,1)}, u32[]{:S(2)}, u32[]{:S(2)}) collective-permute-start(bf16[1024,2048]{1,0:T(8,128)(2,1)} %get-tuple-element.344), channel_id=1, source_target_pairs={{0,1},{1,0},{2,3},{3,2},{4,5},{5,4},{6,7},{7,6},{8,9},{9,8},{10,11... | collective-permute-start | bytes 12582920 | tf_op jit(solution)/shard_map/ppermute | solution.py:48
  444.9 41.5 %collective-permute-start.38 = (bf16[1024,4096]{1,0:T(8,128)(2,1)}, bf16[1024,4096]{1,0:T(8,128)(2,1)}, u32[]{:S(2)}, u32[]{:S(2)}) collective-permute-start(bf16[1024,4096]{1,0:T(8,128)(2,1)} %get-tuple-element.357), channel_id=1, source_target_pairs={{0,1},{1,0},{2,3},{3,2},{4,5},{5,4},{6,7},{7,6},{8,9},{9,8},{10,11... | collective-permute-start | bytes 25165832 | tf_op jit(solution)/shard_map/ppermute | solution.py:48
  446.3 40.0 %collective-permute-start.36 = (bf16[2,64,2048]{2,1,0:T(8,128)(2,1)S(1)}, bf16[2,64,2048]{2,1,0:T(8,128)(2,1)S(1)}, u32[]{:S(2)}, u32[]{:S(2)}) collective-permute-start(bf16[2,64,2048]{2,1,0:T(8,128)(2,1)S(1)} %get-tuple-element.355), channel_id=1, source_target_pairs={{0,2},{2,0},{4,6},{6,4},{8,10},{10,8},{12,14},{14,12},{16,18},{18,... | collective-permute-start | bytes 1572872 | tf_op jit(solution)/shard_map/ppermute | solution.py:44
  447.4 39.0 %collective-permute-start.37 = (bf16[2,64,2048]{2,1,0:T(8,128)(2,1)S(1)}, bf16[2,64,2048]{2,1,0:T(8,128)(2,1)}, u32[]{:S(2)}, u32[]{:S(2)}) collective-permute-start(bf16[2,64,2048]{2,1,0:T(8,128)(2,1)S(1)} %get-tuple-element.356), channel_id=1, source_target_pairs={{0,4},{2,6},{4,0},{6,2},{8,12},{10,14},{12,8},{14,10},{16,20},{18,... | collective-permute-start | bytes 1572872 | tf_op jit(solution)/shard_map/ppermute | solution.py:44
  499.5 51.3 %collective-permute-start.39 = (bf16[4,64,2048]{2,1,0:T(8,128)(2,1)}, bf16[4,64,2048]{2,1,0:T(8,128)(2,1)}, u32[]{:S(2)}, u32[]{:S(2)}) collective-permute-start(bf16[4,64,2048]{2,1,0:T(8,128)(2,1)} %pad_maximum_fusion.2), channel_id=1, source_target_pairs={{0,2},{2,0},{4,6},{6,4},{8,10},{10,8},{12,14},{14,12},{16,18},{18,... | collective-permute-start | bytes 3145736 | tf_op jit(solution)/shard_map/ppermute | solution.py:44
  500.4 50.3 %collective-permute-start.40 = (bf16[4,64,2048]{2,1,0:T(8,128)(2,1)}, bf16[4,64,2048]{2,1,0:T(8,128)(2,1)}, u32[]{:S(2)}, u32[]{:S(2)}) collective-permute-start(bf16[4,64,2048]{2,1,0:T(8,128)(2,1)} %pad_maximum_fusion.3), channel_id=1, source_target_pairs={{0,4},{2,6},{4,0},{6,2},{8,12},{10,14},{12,8},{14,10},{16,20},{18,... | collective-permute-start | bytes 3145736 | tf_op jit(solution)/shard_map/ppermute | solution.py:44
  502.0 48.8 %collective-permute-start.41 = (bf16[2,64,4096]{2,1,0:T(8,128)(2,1)}, bf16[2,64,4096]{2,1,0:T(8,128)(2,1)}, u32[]{:S(2)}, u32[]{:S(2)}) collective-permute-start(bf16[2,64,4096]{2,1,0:T(8,128)(2,1)} %get-tuple-element.377), channel_id=1, source_target_pairs={{0,2},{2,0},{4,6},{6,4},{8,10},{10,8},{12,14},{14,12},{16,18},{18,... | collective-permute-start | bytes 3145736 | tf_op jit(solution)/shard_map/ppermute | solution.py:44
  503.0 47.7 %collective-permute-start.42 = (bf16[2,64,4096]{2,1,0:T(8,128)(2,1)}, bf16[2,64,4096]{2,1,0:T(8,128)(2,1)}, u32[]{:S(2)}, u32[]{:S(2)}) collective-permute-start(bf16[2,64,4096]{2,1,0:T(8,128)(2,1)} %get-tuple-element.378), channel_id=1, source_target_pairs={{0,4},{2,6},{4,0},{6,2},{8,12},{10,14},{12,8},{14,10},{16,20},{18,... | collective-permute-start | bytes 3145736 | tf_op jit(solution)/shard_map/ppermute | solution.py:44
  561.2 61.4 %collective-permute-start.45 = (bf16[1024,2048]{1,0:T(8,128)(2,1)}, bf16[1024,2048]{1,0:T(8,128)(2,1)}, u32[]{:S(2)}, u32[]{:S(2)}) collective-permute-start(bf16[1024,2048]{1,0:T(8,128)(2,1)} %get-tuple-element.393), channel_id=1, source_target_pairs={{0,1},{1,0},{2,3},{3,2},{4,5},{5,4},{6,7},{7,6},{8,9},{9,8},{10,11... | collective-permute-start | bytes 12582920 | tf_op jit(solution)/shard_map/ppermute | solution.py:48
  561.9 141.2 %reduce-scatter.5.cloned.1.call-start = ((), (), s32[]{:S(2)}) async-start(), calls=%async_computation.14 | async-start | bytes 2621440 | tf_op jit(solution)/shard_map/reduce_scatter | solution.py:65
  561.9 60.7 %collective-permute-start.43 = (bf16[4,64,4096]{2,1,0:T(8,128)(2,1)}, bf16[4,64,4096]{2,1,0:T(8,128)(2,1)S(1)}, u32[]{:S(2)}, u32[]{:S(2)}) collective-permute-start(bf16[4,64,4096]{2,1,0:T(8,128)(2,1)} %pad_maximum_fusion), channel_id=1, source_target_pairs={{0,2},{2,0},{4,6},{6,4},{8,10},{10,8},{12,14},{14,12},{16,18},{18,... | collective-permute-start | bytes 6291464 | tf_op jit(solution)/shard_map/ppermute | solution.py:44
  562.9 59.7 %collective-permute-start.44 = (bf16[4,64,4096]{2,1,0:T(8,128)(2,1)}, bf16[4,64,4096]{2,1,0:T(8,128)(2,1)}, u32[]{:S(2)}, u32[]{:S(2)}) collective-permute-start(bf16[4,64,4096]{2,1,0:T(8,128)(2,1)} %pad_maximum_fusion.1), channel_id=1, source_target_pairs={{0,4},{2,6},{4,0},{6,2},{8,12},{10,14},{12,8},{14,10},{16,20},{18,... | collective-permute-start | bytes 6291464 | tf_op jit(solution)/shard_map/ppermute | solution.py:44
  633.2 27.9 %all-to-all-start.6 = ((bf16[16,8,2048]{2,1,0:T(8,128)(2,1)}), bf16[16,8,2048]{2,1,0:T(8,128)(2,1)S(1)}, u32[]{:S(2)}, u32[]{:S(2)}) async-start(bf16[16,8,2048]{2,1,0:T(8,128)(2,1)} %broadcast_in_dim.158), calls=%async_computation.6 | async-start | bytes 1048576 | tf_op jit(solution)/shard_map/all_to_all | solution.py:144
  638.7 126.2 %reduce-scatter.3.cloned.1.call-start = ((), (), s32[]{:S(2)}) async-start(), calls=%async_computation.13 | async-start | bytes 2621440 | tf_op jit(solution)/shard_map/reduce_scatter | solution.py:65
  665.8 32.9 %collective-permute-start.48 = (bf16[2048,1024]{1,0:T(8,128)(2,1)}, bf16[2048,1024]{1,0:T(8,128)(2,1)}, u32[]{:S(2)}, u32[]{:S(2)}) collective-permute-start(bf16[2048,1024]{1,0:T(8,128)(2,1)} %get-tuple-element.416), channel_id=1, source_target_pairs={{0,1},{1,0},{2,3},{3,2},{4,5},{5,4},{6,7},{7,6},{8,9},{9,8},{10,11... | collective-permute-start | bytes 12582920 | tf_op jit(solution)/shard_map/ppermute | solution.py:48
  670.9 25.9 %collective-permute-start.49 = (bf16[4,64,2048]{2,1,0:T(8,128)(2,1)}, bf16[4,64,2048]{2,1,0:T(8,128)(2,1)}, u32[]{:S(2)}, u32[]{:S(2)}) collective-permute-start(bf16[4,64,2048]{2,1,0:T(8,128)(2,1)} %pad_maximum_fusion.4), channel_id=1, source_target_pairs={{0,2},{2,0},{4,6},{6,4},{8,10},{10,8},{12,14},{14,12},{16,18},{18,... | collective-permute-start | bytes 3145736 | tf_op jit(solution)/shard_map/ppermute | solution.py:44
  672.4 26.4 %collective-permute-start.50 = (bf16[4,64,2048]{2,1,0:T(8,128)(2,1)}, bf16[4,64,2048]{2,1,0:T(8,128)(2,1)}, u32[]{:S(2)}, u32[]{:S(2)}) collective-permute-start(bf16[4,64,2048]{2,1,0:T(8,128)(2,1)} %pad_maximum_fusion.5), channel_id=1, source_target_pairs={{0,4},{2,6},{4,0},{6,2},{8,12},{10,14},{12,8},{14,10},{16,20},{18,... | collective-permute-start | bytes 3145736 | tf_op jit(solution)/shard_map/ppermute | solution.py:44
  727.5 33.4 %all-to-all-start.7 = ((bf16[4,64,2048]{2,1,0:T(8,128)(2,1)}), bf16[4,64,2048]{2,1,0:T(8,128)(2,1)S(1)}, u32[]{:S(2)}, u32[]{:S(2)}) async-start(bf16[4,64,2048]{2,1,0:T(8,128)(2,1)} %add_convert_fusion.2), calls=%async_computation.7 | async-start | bytes 2097152 | tf_op jit(solution)/shard_map/all_to_all | solution.py:61
  764.9 29.7 %all-to-all-start.8 = ((bf16[4,128,1024]{2,1,0:T(8,128)(2,1)}), bf16[4,128,1024]{2,1,0:T(8,128)(2,1)}, u32[]{:S(2)}, u32[]{:S(2)}) async-start(bf16[4,128,1024]{2,1,0:T(8,128)(2,1)} %add_convert_fusion.1), calls=%async_computation.10 | async-start | bytes 2097152 | tf_op jit(solution)/shard_map/all_to_all | solution.py:61
  (113 other events, 916.9 us)
Sparse Core Ops, SparseCore 0:
  562.0 60.2 all-gather.1
Sparse Core Ops, SparseCore 1:
  633.3 51.7 reduce-scatter.4
  687.4 44.4 reduce-scatter.2

commit v3 on v2

--- a/solution.py
+++ b/solution.py
@@ -28,9 +28,11 @@
 PYRAMID = (1, 5, 14, 30, 55, 91, 155, 255, 424)
 
 SCORE_SCALE = SOFTMAX_WARMTH / HEAD_WIDTH
+SCORE_POWER = SCORE_SCALE * math.log2(math.e)
 GELU_C = math.sqrt(2.0 / math.pi)
 PAIR = 2 * HEAD_WIDTH
 BLOCK = 512
+JOIN_BLOCK = 1024
 ATTEND_FLOPS = LEN * PAIR * (8 * D + 4 * LEN)
 VMEM_LIMIT = 60 * 2**20
 
@@ -79,19 +81,22 @@
     total = parts[0].shape[1]
     return pl.pallas_call(
         join_kernel,
-        grid=(total // BLOCK,),
-        in_specs=[pl.BlockSpec((part.shape[0], BLOCK), lambda i: (0, i)) for part in parts],
-        out_specs=pl.BlockSpec((rows, BLOCK), lambda i: (0, i)),
+        grid=(total // JOIN_BLOCK,),
+        in_specs=[pl.BlockSpec((part.shape[0], JOIN_BLOCK), lambda i: (0, i)) for part in parts],
+        out_specs=pl.BlockSpec((rows, JOIN_BLOCK), lambda i: (0, i)),
         out_shape=jax.ShapeDtypeStruct((rows, total), parts[0].dtype),
     )(*parts)
 
 
 class Gather:
-    def __init__(self, block):
+    def __init__(self, block, behind=False):
         self.block = block
+        self.behind = behind
         self.step = 0
 
     def request(self):
+        if self.step == 0 and self.behind:
+            return self.block
         if self.step == 0:
             return jnp.broadcast_to(self.block[None], (quarter(),) + self.block.shape)
         if self.step == 1:
@@ -103,6 +108,9 @@
 
     def send(self, values):
         self.step += 1
+        if self.step == 1 and self.behind:
+            self.group = lax.all_gather(values, "dp", axis=0, tiled=True, axis_index_groups=columns_of_chips())
+            return None
         if self.step == 1:
             return over_z(values)
         if self.step == 2:
@@ -112,6 +120,8 @@
         return swap_core(values)
 
     def accept(self, out):
+        if out is None:
+            return
         if self.step == 1:
             self.group = out.reshape((-1,) + self.block.shape[1:])
         elif self.step == 2:
@@ -410,7 +420,7 @@
         cut = [slice(i * PAIR + head * HEAD_WIDTH, i * PAIR + (head + 1) * HEAD_WIDTH) for i in range(3)]
         _, query_n = unit_pair(raw[:, cut[0]])
         _, key_n = unit_pair(raw[:, cut[1]])
-        raised = jnp.exp(matmul_nt(query_n, key_n) * SCORE_SCALE + bias_ref[...])
+        raised = jnp.exp2(matmul_nt(query_n, key_n) * SCORE_POWER + bias_ref[...])
         share = 1.0 / jnp.sum(raised, axis=-1, keepdims=True)
         outs.append(matmul((raised * share).astype(bf16), raw[:, cut[2]].astype(bf16)).astype(bf16))
     return jnp.concatenate(outs, axis=1)
@@ -492,7 +502,7 @@
         grad_out = grad_att[:, head * HEAD_WIDTH : (head + 1) * HEAD_WIDTH]
         grad_q, grad_k, grad_v = [], 0.0, 0.0
         for low, high in ((0, 384), (384, LEN)):
-            raised = jnp.exp(matmul_nt(key_n, query_n[low:high]) * SCORE_SCALE + bias_ref[:, low:high])
+            raised = jnp.exp2(matmul_nt(key_n, query_n[low:high]) * SCORE_POWER + bias_ref[:, low:high])
             attention = raised * (1.0 / jnp.sum(raised, axis=0, keepdims=True))
             grad_probs = matmul_nt(value_b, grad_out[low:high])
             row_dot = jnp.sum(attention * grad_probs, axis=0, keepdims=True)
@@ -991,13 +1001,13 @@
         [expand_weight.reshape(-1, blocks, BLOCK), contract_weight.T.reshape(-1, blocks, BLOCK)], axis=2
     ).astype(bf16)
     code_w, attn_w, mlp_a, mlp_b, head_w = [
-        Gather(block)
-        for block in (
-            code_block,
-            attn_block.astype(bf16),
-            mlp_blocks[:, 0::2].reshape(-1, wide),
-            mlp_blocks[:, 1::2].reshape(-1, wide),
-            head_weight.astype(bf16),
+        Gather(block, behind)
+        for block, behind in (
+            (code_block, False),
+            (attn_block.astype(bf16), False),
+            (mlp_blocks[:, 0::2].reshape(-1, wide), True),
+            (mlp_blocks[:, 1::2].reshape(-1, wide), True),
+            (head_weight.astype(bf16), True),
         )
     ]
     begin = Ticks()
@@ -1026,11 +1036,11 @@
 
     mod_job = Scatter(None, mod_parts, dtype=f32)
     attn_w.block, mod_job.own = begin.wait((attn_w.block, mod_job.own))
-    begin([code_w, attn_w, mod_job])
-    mlp_a.block = begin.wait(mlp_a.block)
-    begin([code_w, mlp_a, mod_job])
+    begin([code_w, attn_w, mod_job, mlp_a])
     begin.wait()
-    begin([code_w, attn_w, mod_job])
+    begin([code_w, mod_job])
+    mlp_a.group = begin.wait(mlp_a.group)
+    begin([code_w, attn_w, mlp_b, mod_job])
     begin.wait()
 
     lengths = mine(item_lengths)[0]
@@ -1075,10 +1085,10 @@
     code_col = code_rows.reshape(LEN, 1)
 
     code_own, code_peer, code_col = begin(
-        [attn_w, mlp_a, mlp_b], (code_w.own, code_w.peer, code_col)
+        [attn_w, mlp_a, head_w], (code_w.own, code_w.peer, code_col)
     )
     tokens, na, na_t = begin.wait(embed(code_col, code_own, code_peer, turn, hot, mods_embed))
-    na = begin([attn_w, mlp_a, mlp_b, head_w], na)
+    na = begin([attn_w, mlp_a, mlp_b], na)
     att_own, part = begin.wait(attend_first(na, attn_w.own, bias))
     mods = placed(mod_job.total[:, 2 * D :])
     gate_attn, gate_mlp, scale_mlp, shift_mlp = jnp.split(mods, 4, axis=1)
@@ -1120,7 +1130,7 @@
     item_job = Exchange(turned([items_mlp[:ITEMS, :D], items_head[:ITEMS], items_mlp[:ITEMS, D:]]), behind=True)
     gao = begin([head_job, mlp_job, item_job], gao)
     dattn_peer, part = begin.wait(attend_back_first(na, na_t, gao, gao_t, att_peer, attn_w.peer, bias_t))
-    attn_job = Scatter(dattn_peer)
+    attn_job = Scatter(dattn_peer, behind=True)
     part = begin([head_job, mlp_job, attn_job], part)
     attn_job.own, grad_tokens, items_attn = begin.wait(
         attend_back_last(
@@ -1135,9 +1145,9 @@
     code_job = Scatter(dcode_peer)
     flat = begin([code_job, attn_job], flat)
     code_job.own = begin.wait(code_back_last(code_row, flat, n * half_rows))
-    begin([code_job, item_job, late_job])
+    begin([code_job, item_job, late_job, attn_job])
     begin.wait()
-    begin([code_job, attn_job])
+    begin([code_job])
     begin.wait()
     head_job.total, mlp_job.total = begin([code_job], (head_job.total, mlp_job.total))
     begin.wait()

time: 848 us -> 820 us (0.967)
  starting transfers between devices: 107 us -> 87 us
  waiting for transfers between devices: 146 us -> 163 us
  local copies, waits for them, and re-layouts: 66.3 us -> 57.8 us
    ppermute x46, waiting for transfers between devices: 104 us -> 129 us  [swap(): return lax.ppermute(values, 'dp', [(i, i ^ bits) for i in range(n)])]
    all_to_all x8 -> x4, starting transfers between devices: 41.6 us -> 21.2 us  [over_z(): lax.all_to_all(values, 'dp', 0, 0, tiled=True, axis_index_groups=columns_...]
    all_to_all x8 -> x4, waiting for transfers between devices: 31.3 us -> 23.6 us  [over_z(): lax.all_to_all(values, 'dp', 0, 0, tiled=True, axis_index_groups=columns_...]
  transfers between devices with their start and end apart: 71 -> 71, of which waited for: 25 -> 26; matrix products, arithmetic and copies ran while one was open for 16% -> 16% of each run, Pallas kernels for 35% -> 37%
where the time goes in v3:
time: 820 us; the launch traced here: 812 us
  Pallas kernels  363 us (44%)
  waiting for transfers between devices  163 us (20%)
  other arithmetic  108 us (13%)
  starting transfers between devices  87 us (11%)
  local copies, waits for them, and re-layouts  57.8 us (7%)
  between operations  22.5 us (3%)
  matrix products  10.6 us (1%)
    ppermute x46, waiting for transfers between devices, swap(): return lax.ppermute(values, 'dp', [(i, i ^ bits) for i in range(n)])  129 us
    ppermute x46, starting transfers between devices, swap(): return lax.ppermute(values, 'dp', [(i, i ^ bits) for i in range(n)])  55.4 us
    pallas_call x1, Pallas kernels, attend_back_last(): kernel_call(attend_back_last_kernel, (steps,), attend_back_specs() + [who...  52.5 us
    pallas_call x1, Pallas kernels, head(): kernel_call(head_kernel, (2 * half,), [whole(LEN, D), whole(D, LEN), w_sp...  48.9 us
    pallas_call x1, Pallas kernels, attend_back_first(): kernel_call(attend_back_first_kernel, (steps,), attend_back_specs(), [col...  46.7 us
    pallas_call x1, Pallas kernels, mlp_back_last(): kernel_call(mlp_back_last_kernel, (steps,), mlp_back_specs() + [whole(LEN...  36.8 us
    pallas_call x1, Pallas kernels, attend_last(): kernel_call(attend_last_kernel, (steps,), [whole(LEN, D), columns(D, 4 *...  34.9 us
    pallas_call x1, Pallas kernels, attend_first(): kernel_call(attend_first_kernel, (steps,), [whole(LEN, D), columns(D, 4 *...  28.8 us
  transfers between devices with their start and end apart: 71, of which 26 were waited for; matrix products, arithmetic and copies ran while one was open for 16% of the time, Pallas kernels for 37%

profile of v3, /device:TPU:0, one launch (start us, length us, event | category | flops | bytes accessed | tf_op | source)
XLA Modules:
  0.0 812.1 jit_solution(11665140319371090605)
XLA Ops:
  15.9 5.1 all-to-all-start
  41.9 4.1 all-to-all-done
  48.1 4.3 all-to-all-start.1
  56.6 28.8 %collective-permute-done.8 = f32[2,8,6144]{2,1,0:T(8,128)} collective-permute-done((f32[2,8,6144]{2,1,0:T(8,128)}, f32[2,8,6144]{2,1,0:T(8,128)}, u32[]{:S(2)}, u32[]{:S(2)}) %collective-permute-start.8) | collective-permute-done | bytes 393248 | tf_op jit(solution)/shard_map/ppermute | solution.py:46
  86.6 5.0 all-to-all-done.1
  103.8 19.9 %collective-permute-done.10.refs_3_ = bf16[256,1024]{1,0:T(8,128)(2,1)} collective-permute-done((bf16[256,1024]{1,0:T(8,128)(2,1)}, bf16[256,1024]{1,0:T(8,128)(2,1)}, u32[]{:S(2)}, u32[]{:S(2)}) %collective-permute-start.10) | collective-permute-done | bytes 524320 | tf_op jit(solution)/shard_map/ppermute | solution.py:46
  127.3 4.5 shard_map.502.own_ref
  131.9 3.6 all-to-all-start.2
  144.6 16.8 %collective-permute-done.15.refs_1_ = bf16[256,2048]{1,0:T(8,128)(2,1)S(1)} collective-permute-done((bf16[256,2048]{1,0:T(8,128)(2,1)}, bf16[256,2048]{1,0:T(8,128)(2,1)S(1)}, u32[]{:S(2)}, u32[]{:S(2)}) %collective-permute-start.15) | collective-permute-done | bytes 1048608 | tf_op jit(solution)/shard_map/ppermute | solution.py:46
  161.6 4.8 all-to-all-done.2
  174.6 16.9 %shard_map.503 = (bf16[800,1024]{1,0:T(8,128)(2,1)}, bf16[800,1024]{1,0:T(8,128)(2,1)}, bf16[1024,800]{1,0:T(8,128)(2,1)}) custom-call(s32[800,1]{1,0:T(8,128)} %fusion.42.code_ref, bf16[2048,1024]{1,0:T(8,128)(2,1)} %shard_map.502.own_ref, bf16[2048,1024]{1,0:T(8,128)(2,1)} %collective-permute-done.14.peer_ref, bf16[1024,1024]{1,0:T(8,128)(2,1)} %fusion.turn_ref, ...), custom_call_target="tpu_custom_call" | custom-call | flops 6710886400 | bytes 16777216 | tf_op jit(solution)/shard_map/pallas_call | solution.py:405
  191.5 10.4 %collective-permute-done.17.refs_3_ = bf16[128,2048]{1,0:T(8,128)(2,1)S(1)} collective-permute-done((bf16[128,2048]{1,0:T(8,128)(2,1)}, bf16[128,2048]{1,0:T(8,128)(2,1)S(1)}, u32[]{:S(2)}, u32[]{:S(2)}) %collective-permute-start.17) | collective-permute-done | bytes 524320 | tf_op jit(solution)/shard_map/ppermute | solution.py:46
  204.5 3.8 shard_map.504.w_ref
  213.3 3.2 fusion.2
  216.5 28.8 %shard_map.505 = (bf16[800,512]{1,0:T(8,128)(2,1)}, f32[800,1024]{1,0:T(8,128)}) custom-call(bf16[800,1024]{1,0:T(8,128)(2,1)} %get-tuple-element.283.na_ref, bf16[1024,2048]{1,0:T(8,128)(2,1)} %shard_map.504.w_ref, f32[800,800]{1,0:T(8,128)} %get-tuple-element.513.bias_ref), custom_call_target="tpu_custom_call" | custom-call | flops 4666163200 | bytes 16777216 | tf_op jit(solution)/shard_map/pallas_call | solution.py:456
  249.3 3.7 shard_map.506.w0_ref
  259.6 34.9 %shard_map.507 = (bf16[800,512]{1,0:T(8,128)(2,1)}, f32[800,1024]{1,0:T(8,128)}, f32[800,1024]{1,0:T(8,128)}, bf16[800,1024]{1,0:T(8,128)(2,1)}, bf16[1024,800]{1,0:T(8,128)(2,1)}) custom-call(bf16[800,1024]{1,0:T(8,128)(2,1)} %get-tuple-element.283.na_ref, bf16[1024,2048]{1,0:T(8,128)(2,1)} %collective-permute-done.21.w_ref, ...), custom_call_target="tpu_custom_call" | custom-call | flops 4666163200 | bytes 16777216 | tf_op jit(solution)/shard_map/pallas_call | solution.py:468
  296.5 3.7 shard_map.508.w1_ref
  302.4 14.0 %shard_map.509 = (f32[800,1024]{1,0:T(8,128)}, f32[800,1024]{1,0:T(8,128)}, f32[800,1024]{1,0:T(8,128)}) custom-call(bf16[800,1024]{1,0:T(8,128)(2,1)} %get-tuple-element.311.nm_ref, bf16[1024,2048]{1,0:T(8,128)(2,1)} %shard_map.506.w0_ref, bf16[1024,2048]{1,0:T(8,128)(2,1)} %shard_map.508.w1_ref), custom_call_target="tpu_custom_call" | custom-call | flops 6710886400 | bytes 16777216 | tf_op jit(solution)/shard_map/pallas_call | solution.py:621
  317.3 4.1 shard_map.510.own_ref
  326.6 19.1 %shard_map.511 = (f32[800,1024]{1,0:T(8,128)}, f32[800,1024]{1,0:T(8,128)}, f32[800,1024]{1,0:T(8,128)}, f32[800,1024]{1,0:T(8,128)}, bf16[800,1024]{1,0:T(8,128)(2,1)}, /*index=5*/bf16[1024,800]{1,0:T(8,128)(2,1)}) custom-call(bf16[800,1024]{1,0:T(8,128)(2,1)} %get-tuple-element.311.nm_ref, bf16[1024,2048]{1,0:T(8,128)(2,1)} %collective-permute-done.26.w0_ref, ...), custom_call_target="tpu_custom_call" | custom-call | flops 6710886400 | bytes 16777216 | tf_op jit(solution)/shard_map/pallas_call | solution.py:635
  345.7 48.9 %shard_map.512 = (bf16[1024,2048]{1,0:T(8,128)(2,1)}, bf16[1024,2048]{1,0:T(8,128)(2,1)}, f32[8,128]{1,0:T(8,128)}, f32[800,1024]{1,0:T(8,128)}, bf16[800,1024]{...) custom-call(bf16[800,1024]{1,0:T(8,128)(2,1)} %get-tuple-element.329.nh_ref, ...), custom_call_target="tpu_custom_call" | custom-call | flops 20132659200 | bytes 16777216 | tf_op jit(solution)/shard_map/pallas_call | solution.py:814
  395.2 26.2 %shard_map.513 = (bf16[1024,4096]{1,0:T(8,128)(2,1)}, f32[800,1024]{1,0:T(8,128)}) custom-call(bf16[1024,800]{1,0:T(8,128)(2,1)} %get-tuple-element.338.nm_t_ref, bf16[800,1024]{1,0:T(8,128)(2,1)} %get-tuple-element.339.g_ref, bf16[1024,800]{1,0:T(8,128)(2,1)} %get-tuple-element.340.g_t_ref, f32[800,1024]{1,0:T(8,128)} %get-tuple-element.341.h0_ref, ...), custom_call_target="tpu_custom_call" | custom-call | flops 13421772800 | bytes 16777216 | tf_op jit(solution)/shard_map/pallas_call | solution.py:706
  421.4 4.0 fusion.25
  428.9 36.8 %shard_map.514 = (bf16[1024,4096]{1,0:T(8,128)(2,1)}, f32[800,1024]{1,0:T(8,128)}, bf16[800,1024]{1,0:T(8,128)(2,1)}, bf16[1024,800]{1,0:T(8,128)(2,1)}, f32[16,3072]{1,0:T(8,128)}) custom-call(bf16[1024,800]{1,0:T(8,128)(2,1)} %get-tuple-element.338.nm_t_ref, bf16[800,1024]{1,0:T(8,128)(2,1)} %get-tuple-element.339.g_ref, ...), custom_call_target="tpu_custom_call" | custom-call | flops 13421772800 | bytes 16777216 | tf_op jit(solution)/shard_map/pallas_call | solution.py:718
  471.2 5.2 fusion.10
  484.9 46.7 %shard_map.515 = (bf16[1024,2048]{1,0:T(8,128)(2,1)}, f32[800,1024]{1,0:T(8,128)}) custom-call(bf16[800,1024]{1,0:T(8,128)(2,1)} %get-tuple-element.283.na_ref, bf16[1024,800]{1,0:T(8,128)(2,1)} %get-tuple-element.372.na_t_ref, bf16[800,1024]{1,0:T(8,128)(2,1)} %get-tuple-element.373.go_ref, bf16[1024,800]{1,0:T(8,128)(2,1)} %get-tuple-element.374.go_t_ref, ...), custom_call_target="tpu_custom_call" | custom-call | flops 13998489600 | bytes 16777216 | tf_op jit(solution)/shard_map/pallas_call | solution.py:559
  531.7 4.0 fusion.3
  538.8 3.3 convert_add_fusion.3
  544.9 4.9 convert_add_fusion
  549.8 52.5 %shard_map.516 = (bf16[1024,2048]{1,0:T(8,128)(2,1)}, bf16[800,1024]{1,0:T(8,128)(2,1)}, f32[16,2048]{1,0:T(8,128)}) custom-call(bf16[800,1024]{1,0:T(8,128)(2,1)} %get-tuple-element.283.na_ref, bf16[1024,800]{1,0:T(8,128)(2,1)} %get-tuple-element.372.na_t_ref, bf16[800,1024]{1,0:T(8,128)(2,1)} %get-tuple-element.373.go_ref, ...), custom_call_target="tpu_custom_call" | custom-call | flops 13998489600 | bytes 16777216 | tf_op jit(solution)/shard_map/pallas_call | solution.py:571
  604.2 4.1 fusion.29
  608.3 4.0 add_convert_fusion
  613.2 4.3 all-to-all-start.3
  621.6 10.0 %shard_map.517 = (bf16[2048,1024]{1,0:T(8,128)(2,1)}, bf16[800,1024]{1,0:T(8,128)(2,1)}) custom-call(s32[1,800]{1,0:T(1,128)} %fusion.91.code_ref, bf16[800,1024]{1,0:T(8,128)(2,1)} %get-tuple-element.402.gt_ref, bf16[1024,1024]{1,0:T(8,128)(2,1)} %fusion.turn_ref), custom_call_target="tpu_custom_call" | custom-call | flops 3355443200 | bytes 16777216 | tf_op jit(solution)/shard_map/pallas_call | solution.py:879
  631.6 3.7 collective-permute-done.46
  636.0 4.2 all-to-all-done.3
  659.1 7.9 shard_map.518
  667.0 8.7 %collective-permute-done.49 = bf16[4,64,2048]{2,1,0:T(8,128)(2,1)} collective-permute-done((bf16[4,64,2048]{2,1,0:T(8,128)(2,1)}, bf16[4,64,2048]{2,1,0:T(8,128)(2,1)}, u32[]{:S(2)}, u32[]{:S(2)}) %collective-permute-start.49) | collective-permute-done | bytes 1048608 | tf_op jit(solution)/shard_map/ppermute | solution.py:46
  677.7 4.2 fusion.33
  691.2 8.3 %collective-permute-done.51 = bf16[2,128,1024]{2,1,0:T(8,128)(2,1)S(1)} collective-permute-done((bf16[2,128,1024]{2,1,0:T(8,128)(2,1)}, bf16[2,128,1024]{2,1,0:T(8,128)(2,1)S(1)}, u32[]{:S(2)}, u32[]{:S(2)}) %collective-permute-start.51) | collective-permute-done | bytes 524320 | tf_op jit(solution)/shard_map/ppermute | solution.py:46
  711.0 18.7 %collective-permute-done.55 = bf16[4,128,1024]{2,1,0:T(8,128)(2,1)S(1)} collective-permute-done((bf16[4,128,1024]{2,1,0:T(8,128)(2,1)S(1)}, bf16[4,128,1024]{2,1,0:T(8,128)(2,1)S(1)}, u32[]{:S(2)}, u32[]{:S(2)}) %collective-permute-start.55) | collective-permute-done | bytes 1048608 | tf_op jit(solution)/shard_map/ppermute | solution.py:46
  732.3 8.2 %all-to-all-start.4 = ((bf16[4,128,1024]{2,1,0:T(8,128)(2,1)}), bf16[4,128,1024]{2,1,0:T(8,128)(2,1)}, u32[]{:S(2)}, u32[]{:S(2)}) async-start(bf16[4,128,1024]{2,1,0:T(8,128)(2,1)} %add_convert_fusion.1), calls=%async_computation.6 | async-start | bytes 2097152 | tf_op jit(solution)/shard_map/all_to_all | solution.py:63
  755.6 9.7 %all-to-all-done.4 = bf16[4,128,1024]{2,1,0:T(8,128)(2,1)} async-done(((bf16[4,128,1024]{2,1,0:T(8,128)(2,1)}), bf16[4,128,1024]{2,1,0:T(8,128)(2,1)}, u32[]{:S(2)}, u32[]{:S(2)}) %all-to-all-start.4) | async-done | bytes 1048608 | tf_op jit(solution)/shard_map/all_to_all | solution.py:63
  772.1 3.7 all-to-all-start.5
  776.8 6.1 all-to-all-done.5
  793.9 3.1 multiply_subtract_fusion
  800.4 3.6 multiply_subtract_fusion.1
  (494 shorter events, 205.0 us)
Async XLA Ops:
  15.9 30.1 %all-to-all-start = ((bf16[4,128,1024]{2,1,0:T(8,128)(2,1)}), bf16[4,128,1024]{2,1,0:T(8,128)(2,1)}, u32[]{:S(2)}, u32[]{:S(2)}) async-start(bf16[4,128,1024]{2,1,0:T(8,128)(2,1)} %broadcast_in_dim.80), calls=%async_computation | async-start | bytes 2097152 | tf_op jit(solution)/shard_map/all_to_all | solution.py:63
  48.1 43.5 %all-to-all-start.1 = ((bf16[4,64,2048]{2,1,0:T(8,128)(2,1)}), bf16[4,64,2048]{2,1,0:T(8,128)(2,1)}, u32[]{:S(2)}, u32[]{:S(2)}) async-start(bf16[4,64,2048]{2,1,0:T(8,128)(2,1)} %broadcast_in_dim.83), calls=%async_computation.1 | async-start | bytes 2097152 | tf_op jit(solution)/shard_map/all_to_all | solution.py:63
  52.4 51.4 %all-gather.5.cloned.1.call-start = ((), (), s32[]{:S(2)}) async-start(), calls=%async_computation.9 | async-start | bytes 1310720 | tf_op jit(solution)/shard_map/all_gather | solution.py:112
  52.4 34.1 %collective-permute-start.6 = (bf16[512,1024]{1,0:T(8,128)(2,1)}, bf16[512,1024]{1,0:T(8,128)(2,1)}, u32[]{:S(2)}, u32[]{:S(2)}) collective-permute-start(bf16[512,1024]{1,0:T(8,128)(2,1)} %bitcast.10.refs_0_), channel_id=1, source_target_pairs={{0,2},{2,0},{4,6},{6,4},{8,10},{10,8},{12,14},{14,12},{16,18},{18,... | collective-permute-start | bytes 3145736 | tf_op jit(solution)/shard_map/ppermute | solution.py:46
  54.0 32.6 %collective-permute-start.7 = (bf16[512,1024]{1,0:T(8,128)(2,1)}, bf16[512,1024]{1,0:T(8,128)(2,1)}, u32[]{:S(2)}, u32[]{:S(2)}) collective-permute-start(bf16[512,1024]{1,0:T(8,128)(2,1)} %bitcast.10.refs_0_), channel_id=1, source_target_pairs={{0,4},{2,6},{4,0},{6,2},{8,12},{10,14},{12,8},{14,10},{16,20},{18,... | collective-permute-start | bytes 3145736 | tf_op jit(solution)/shard_map/ppermute | solution.py:46
  55.5 29.8 %collective-permute-start.8 = (f32[2,8,6144]{2,1,0:T(8,128)}, f32[2,8,6144]{2,1,0:T(8,128)}, u32[]{:S(2)}, u32[]{:S(2)}) collective-permute-start(f32[2,8,6144]{2,1,0:T(8,128)} %get-tuple-element.239), channel_id=1, source_target_pairs={{0,2},{2,0},{4,6},{6,4},{8,10},{10,8},{12,14},{14,12},{16,18},{18,... | collective-permute-start | bytes 1179656 | tf_op jit(solution)/shard_map/ppermute | solution.py:46
  56.1 30.5 %collective-permute-start.9 = (f32[2,8,6144]{2,1,0:T(8,128)}, f32[2,8,6144]{2,1,0:T(8,128)}, u32[]{:S(2)}, u32[]{:S(2)}) collective-permute-start(f32[2,8,6144]{2,1,0:T(8,128)} %get-tuple-element.240), channel_id=1, source_target_pairs={{0,4},{2,6},{4,0},{6,2},{8,12},{10,14},{12,8},{14,10},{16,20},{18,... | collective-permute-start | bytes 1179656 | tf_op jit(solution)/shard_map/ppermute | solution.py:46
  97.9 27.0 %collective-permute-start.12 = (f32[4,8,6144]{2,1,0:T(8,128)}, f32[4,8,6144]{2,1,0:T(8,128)}, u32[]{:S(2)}, u32[]{:S(2)}) collective-permute-start(f32[4,8,6144]{2,1,0:T(8,128)} %get-tuple-element.247), channel_id=1, source_target_pairs={{0,2},{2,0},{4,6},{6,4},{8,10},{10,8},{12,14},{14,12},{16,18},{18,... | collective-permute-start | bytes 2359304 | tf_op jit(solution)/shard_map/ppermute | solution.py:46
  99.4 25.5 %collective-permute-start.13 = (f32[4,8,6144]{2,1,0:T(8,128)}, f32[4,8,6144]{2,1,0:T(8,128)}, u32[]{:S(2)}, u32[]{:S(2)}) collective-permute-start(f32[4,8,6144]{2,1,0:T(8,128)} %get-tuple-element.248), channel_id=1, source_target_pairs={{0,4},{2,6},{4,0},{6,2},{8,12},{10,14},{12,8},{14,10},{16,20},{18,... | collective-permute-start | bytes 2359304 | tf_op jit(solution)/shard_map/ppermute | solution.py:46
  131.8 34.6 %collective-permute-start.14 = (bf16[2048,1024]{1,0:T(8,128)(2,1)}, bf16[2048,1024]{1,0:T(8,128)(2,1)}, u32[]{:S(2)}, u32[]{:S(2)}) collective-permute-start(bf16[2048,1024]{1,0:T(8,128)(2,1)} %shard_map.502.own_ref), channel_id=1, source_target_pairs={{0,1},{1,0},{2,3},{3,2},{4,5},{5,4},{6,7},{7,6},{8,9},{9,8},{10,11... | collective-permute-start | bytes 12582920 | tf_op jit(solution)/shard_map/ppermute | solution.py:50
  131.9 34.4 %all-to-all-start.2 = ((f32[4,8,6144]{2,1,0:T(8,128)}), f32[4,8,6144]{2,1,0:T(8,128)S(1)}, u32[]{:S(2)}, u32[]{:S(2)}) async-start(f32[4,8,6144]{2,1,0:T(8,128)} %fusion.18), calls=%async_computation.2 | async-start | bytes 1572864 | tf_op jit(solution)/shard_map/all_to_all | solution.py:63
  135.6 72.7 %all-gather.9.cloned.1.call-start = ((), (), s32[]{:S(2)}) async-start(), calls=%async_computation.11 | async-start | bytes 1310720 | tf_op jit(solution)/shard_map/all_gather | solution.py:112
  135.7 25.7 %collective-permute-start.15 = (bf16[256,2048]{1,0:T(8,128)(2,1)}, bf16[256,2048]{1,0:T(8,128)(2,1)S(1)}, u32[]{:S(2)}, u32[]{:S(2)}) collective-permute-start(bf16[256,2048]{1,0:T(8,128)(2,1)} %bitcast.19.refs_0_), channel_id=1, source_target_pairs={{0,2},{2,0},{4,6},{6,4},{8,10},{10,8},{12,14},{14,12},{16,18},{18,... | collective-permute-start | bytes 3145736 | tf_op jit(solution)/shard_map/ppermute | solution.py:46
  139.9 113.1 %all-gather.7.cloned.1.call-start = ((), (), s32[]{:S(2)}) async-start(), calls=%async_computation.10 | async-start | bytes 1310720 | tf_op jit(solution)/shard_map/all_gather | solution.py:112
  168.1 33.9 %collective-permute-start.19 = (bf16[256,2048]{1,0:T(8,128)(2,1)}, bf16[256,2048]{1,0:T(8,128)(2,1)S(1)}, u32[]{:S(2)}, u32[]{:S(2)}) collective-permute-start(bf16[256,2048]{1,0:T(8,128)(2,1)} %all-gather.5.cloned.1.call-done.refs_0_), channel_id=1, source_target_pairs={{0,2},{2,0},{4,6},{6,4},{8,10},{10,8},{12,14},{14,12},{16,18},{18,... | collective-permute-start | bytes 3145736 | tf_op jit(solution)/shard_map/ppermute | solution.py:46
  168.1 33.9 %collective-permute-start.20 = (bf16[256,2048]{1,0:T(8,128)(2,1)}, bf16[256,2048]{1,0:T(8,128)(2,1)S(1)}, u32[]{:S(2)}, u32[]{:S(2)}) collective-permute-start(bf16[256,2048]{1,0:T(8,128)(2,1)} %all-gather.5.cloned.1.call-done.refs_0_), channel_id=1, source_target_pairs={{0,4},{2,6},{4,0},{6,2},{8,12},{10,14},{12,8},{14,10},{16,20},{18,... | collective-permute-start | bytes 3145736 | tf_op jit(solution)/shard_map/ppermute | solution.py:46
  172.1 29.8 %collective-permute-start.17 = (bf16[128,2048]{1,0:T(8,128)(2,1)}, bf16[128,2048]{1,0:T(8,128)(2,1)S(1)}, u32[]{:S(2)}, u32[]{:S(2)}) collective-permute-start(bf16[128,2048]{1,0:T(8,128)(2,1)} %slice.378), channel_id=1, source_target_pairs={{0,2},{2,0},{4,6},{6,4},{8,10},{10,8},{12,14},{14,12},{16,18},{18,... | collective-permute-start | bytes 1572872 | tf_op jit(solution)/shard_map/ppermute | solution.py:46
  174.1 27.8 %collective-permute-start.18 = (bf16[128,2048]{1,0:T(8,128)(2,1)}, bf16[128,2048]{1,0:T(8,128)(2,1)S(1)}, u32[]{:S(2)}, u32[]{:S(2)}) collective-permute-start(bf16[128,2048]{1,0:T(8,128)(2,1)} %slice.379), channel_id=1, source_target_pairs={{0,4},{2,6},{4,0},{6,2},{8,12},{10,14},{12,8},{14,10},{16,20},{18,... | collective-permute-start | bytes 1572872 | tf_op jit(solution)/shard_map/ppermute | solution.py:46
  208.3 39.2 %collective-permute-start.21 = (bf16[1024,2048]{1,0:T(8,128)(2,1)}, bf16[1024,2048]{1,0:T(8,128)(2,1)}, u32[]{:S(2)}, u32[]{:S(2)}) collective-permute-start(bf16[1024,2048]{1,0:T(8,128)(2,1)} %shard_map.504.w_ref), channel_id=1, source_target_pairs={{0,1},{1,0},{2,3},{3,2},{4,5},{5,4},{6,7},{7,6},{8,9},{9,8},{10,11... | collective-permute-start | bytes 12582920 | tf_op jit(solution)/shard_map/ppermute | solution.py:50
  208.4 438.3 %all-gather.11.cloned.1.call-start = ((), (), s32[]{:S(2)}) async-start(), calls=%async_computation.12 | async-start | bytes 1114112 | tf_op jit(solution)/shard_map/all_gather | solution.py:152
  209.0 38.5 %collective-permute-start.24 = (bf16[256,2048]{1,0:T(8,128)(2,1)}, bf16[256,2048]{1,0:T(8,128)(2,1)S(1)}, u32[]{:S(2)}, u32[]{:S(2)}) collective-permute-start(bf16[256,2048]{1,0:T(8,128)(2,1)} %all-gather.9.cloned.1.call-done.refs_0_), channel_id=1, source_target_pairs={{0,2},{2,0},{4,6},{6,4},{8,10},{10,8},{12,14},{14,12},{16,18},{18,... | collective-permute-start | bytes 3145736 | tf_op jit(solution)/shard_map/ppermute | solution.py:46
  210.7 36.7 %collective-permute-start.25 = (bf16[256,2048]{1,0:T(8,128)(2,1)}, bf16[256,2048]{1,0:T(8,128)(2,1)S(1)}, u32[]{:S(2)}, u32[]{:S(2)}) collective-permute-start(bf16[256,2048]{1,0:T(8,128)(2,1)} %all-gather.9.cloned.1.call-done.refs_0_), channel_id=1, source_target_pairs={{0,4},{2,6},{4,0},{6,2},{8,12},{10,14},{12,8},{14,10},{16,20},{18,... | collective-permute-start | bytes 3145736 | tf_op jit(solution)/shard_map/ppermute | solution.py:46
  212.4 33.7 %collective-permute-start.22 = (bf16[128,2048]{1,0:T(8,128)(2,1)}, bf16[128,2048]{1,0:T(8,128)(2,1)S(1)}, u32[]{:S(2)}, u32[]{:S(2)}) collective-permute-start(bf16[128,2048]{1,0:T(8,128)(2,1)} %slice.381), channel_id=1, source_target_pairs={{0,2},{2,0},{4,6},{6,4},{8,10},{10,8},{12,14},{14,12},{16,18},{18,... | collective-permute-start | bytes 1572872 | tf_op jit(solution)/shard_map/ppermute | solution.py:46
  212.7 34.7 %collective-permute-start.23 = (bf16[128,2048]{1,0:T(8,128)(2,1)}, bf16[128,2048]{1,0:T(8,128)(2,1)S(1)}, u32[]{:S(2)}, u32[]{:S(2)}) collective-permute-start(bf16[128,2048]{1,0:T(8,128)(2,1)} %slice.382), channel_id=1, source_target_pairs={{0,4},{2,6},{4,0},{6,2},{8,12},{10,14},{12,8},{14,10},{16,20},{18,... | collective-permute-start | bytes 1572872 | tf_op jit(solution)/shard_map/ppermute | solution.py:46
  253.0 41.6 %collective-permute-start.26 = (bf16[1024,2048]{1,0:T(8,128)(2,1)}, bf16[1024,2048]{1,0:T(8,128)(2,1)}, u32[]{:S(2)}, u32[]{:S(2)}) collective-permute-start(bf16[1024,2048]{1,0:T(8,128)(2,1)} %shard_map.506.w0_ref), channel_id=1, source_target_pairs={{0,1},{1,0},{2,3},{3,2},{4,5},{5,4},{6,7},{7,6},{8,9},{9,8},{10,11... | collective-permute-start | bytes 12582920 | tf_op jit(solution)/shard_map/ppermute | solution.py:50
  253.9 40.7 %collective-permute-start.29 = (bf16[256,2048]{1,0:T(8,128)(2,1)}, bf16[256,2048]{1,0:T(8,128)(2,1)S(1)}, u32[]{:S(2)}, u32[]{:S(2)}) collective-permute-start(bf16[256,2048]{1,0:T(8,128)(2,1)} %all-gather.7.cloned.1.call-done.refs_0_), channel_id=1, source_target_pairs={{0,2},{2,0},{4,6},{6,4},{8,10},{10,8},{12,14},{14,12},{16,18},{18,... | collective-permute-start | bytes 3145736 | tf_op jit(solution)/shard_map/ppermute | solution.py:46
  254.4 40.2 %collective-permute-start.30 = (bf16[256,2048]{1,0:T(8,128)(2,1)}, bf16[256,2048]{1,0:T(8,128)(2,1)S(1)}, u32[]{:S(2)}, u32[]{:S(2)}) collective-permute-start(bf16[256,2048]{1,0:T(8,128)(2,1)} %all-gather.7.cloned.1.call-done.refs_0_), channel_id=1, source_target_pairs={{0,4},{2,6},{4,0},{6,2},{8,12},{10,14},{12,8},{14,10},{16,20},{18,... | collective-permute-start | bytes 3145736 | tf_op jit(solution)/shard_map/ppermute | solution.py:46
  256.9 37.6 %collective-permute-start.27 = (bf16[128,2048]{1,0:T(8,128)(2,1)}, bf16[128,2048]{1,0:T(8,128)(2,1)S(1)}, u32[]{:S(2)}, u32[]{:S(2)}) collective-permute-start(bf16[128,2048]{1,0:T(8,128)(2,1)} %slice.383), channel_id=1, source_target_pairs={{0,2},{2,0},{4,6},{6,4},{8,10},{10,8},{12,14},{14,12},{16,18},{18,... | collective-permute-start | bytes 1572872 | tf_op jit(solution)/shard_map/ppermute | solution.py:46
  258.5 36.0 %collective-permute-start.28 = (bf16[128,2048]{1,0:T(8,128)(2,1)}, bf16[128,2048]{1,0:T(8,128)(2,1)S(1)}, u32[]{:S(2)}, u32[]{:S(2)}) collective-permute-start(bf16[128,2048]{1,0:T(8,128)(2,1)} %slice.384), channel_id=1, source_target_pairs={{0,4},{2,6},{4,0},{6,2},{8,12},{10,14},{12,8},{14,10},{16,20},{18,... | collective-permute-start | bytes 1572872 | tf_op jit(solution)/shard_map/ppermute | solution.py:46
  394.6 26.8 %collective-permute-start.35 = (bf16[1024,2048]{1,0:T(8,128)(2,1)}, bf16[1024,2048]{1,0:T(8,128)(2,1)}, u32[]{:S(2)}, u32[]{:S(2)}) collective-permute-start(bf16[1024,2048]{1,0:T(8,128)(2,1)} %get-tuple-element.337), channel_id=1, source_target_pairs={{0,1},{1,0},{2,3},{3,2},{4,5},{5,4},{6,7},{7,6},{8,9},{9,8},{10,11... | collective-permute-start | bytes 12582920 | tf_op jit(solution)/shard_map/ppermute | solution.py:50
  425.4 42.3 %collective-permute-start.38 = (bf16[1024,4096]{1,0:T(8,128)(2,1)}, bf16[1024,4096]{1,0:T(8,128)(2,1)}, u32[]{:S(2)}, u32[]{:S(2)}) collective-permute-start(bf16[1024,4096]{1,0:T(8,128)(2,1)} %get-tuple-element.350), channel_id=1, source_target_pairs={{0,1},{1,0},{2,3},{3,2},{4,5},{5,4},{6,7},{7,6},{8,9},{9,8},{10,11... | collective-permute-start | bytes 25165832 | tf_op jit(solution)/shard_map/ppermute | solution.py:50
  426.9 40.8 %collective-permute-start.36 = (bf16[2,64,2048]{2,1,0:T(8,128)(2,1)S(1)}, bf16[2,64,2048]{2,1,0:T(8,128)(2,1)S(1)}, u32[]{:S(2)}, u32[]{:S(2)}) collective-permute-start(bf16[2,64,2048]{2,1,0:T(8,128)(2,1)S(1)} %get-tuple-element.348), channel_id=1, source_target_pairs={{0,2},{2,0},{4,6},{6,4},{8,10},{10,8},{12,14},{14,12},{16,18},{18,... | collective-permute-start | bytes 1572872 | tf_op jit(solution)/shard_map/ppermute | solution.py:46
  428.5 39.2 %collective-permute-start.37 = (bf16[2,64,2048]{2,1,0:T(8,128)(2,1)S(1)}, bf16[2,64,2048]{2,1,0:T(8,128)(2,1)}, u32[]{:S(2)}, u32[]{:S(2)}) collective-permute-start(bf16[2,64,2048]{2,1,0:T(8,128)(2,1)S(1)} %get-tuple-element.349), channel_id=1, source_target_pairs={{0,4},{2,6},{4,0},{6,2},{8,12},{10,14},{12,8},{14,10},{16,20},{18,... | collective-permute-start | bytes 1572872 | tf_op jit(solution)/shard_map/ppermute | solution.py:46
  480.9 50.8 %collective-permute-start.39 = (bf16[4,64,2048]{2,1,0:T(8,128)(2,1)}, bf16[4,64,2048]{2,1,0:T(8,128)(2,1)}, u32[]{:S(2)}, u32[]{:S(2)}) collective-permute-start(bf16[4,64,2048]{2,1,0:T(8,128)(2,1)} %pad_maximum_fusion.2), channel_id=1, source_target_pairs={{0,2},{2,0},{4,6},{6,4},{8,10},{10,8},{12,14},{14,12},{16,18},{18,... | collective-permute-start | bytes 3145736 | tf_op jit(solution)/shard_map/ppermute | solution.py:46
  481.3 50.3 %collective-permute-start.40 = (bf16[4,64,2048]{2,1,0:T(8,128)(2,1)}, bf16[4,64,2048]{2,1,0:T(8,128)(2,1)}, u32[]{:S(2)}, u32[]{:S(2)}) collective-permute-start(bf16[4,64,2048]{2,1,0:T(8,128)(2,1)} %pad_maximum_fusion.3), channel_id=1, source_target_pairs={{0,4},{2,6},{4,0},{6,2},{8,12},{10,14},{12,8},{14,10},{16,20},{18,... | collective-permute-start | bytes 3145736 | tf_op jit(solution)/shard_map/ppermute | solution.py:46
  482.9 48.8 %collective-permute-start.41 = (bf16[2,64,4096]{2,1,0:T(8,128)(2,1)}, bf16[2,64,4096]{2,1,0:T(8,128)(2,1)}, u32[]{:S(2)}, u32[]{:S(2)}) collective-permute-start(bf16[2,64,4096]{2,1,0:T(8,128)(2,1)} %get-tuple-element.370), channel_id=1, source_target_pairs={{0,2},{2,0},{4,6},{6,4},{8,10},{10,8},{12,14},{14,12},{16,18},{18,... | collective-permute-start | bytes 3145736 | tf_op jit(solution)/shard_map/ppermute | solution.py:46
  484.5 47.2 %collective-permute-start.42 = (bf16[2,64,4096]{2,1,0:T(8,128)(2,1)}, bf16[2,64,4096]{2,1,0:T(8,128)(2,1)}, u32[]{:S(2)}, u32[]{:S(2)}) collective-permute-start(bf16[2,64,4096]{2,1,0:T(8,128)(2,1)} %get-tuple-element.371), channel_id=1, source_target_pairs={{0,4},{2,6},{4,0},{6,2},{8,12},{10,14},{12,8},{14,10},{16,20},{18,... | collective-permute-start | bytes 3145736 | tf_op jit(solution)/shard_map/ppermute | solution.py:46
  542.1 60.2 %collective-permute-start.45 = (bf16[1024,2048]{1,0:T(8,128)(2,1)}, bf16[1024,2048]{1,0:T(8,128)(2,1)}, u32[]{:S(2)}, u32[]{:S(2)}) collective-permute-start(bf16[1024,2048]{1,0:T(8,128)(2,1)} %get-tuple-element.386), channel_id=1, source_target_pairs={{0,1},{1,0},{2,3},{3,2},{4,5},{5,4},{6,7},{7,6},{8,9},{9,8},{10,11... | collective-permute-start | bytes 12582920 | tf_op jit(solution)/shard_map/ppermute | solution.py:50
  542.8 145.3 %reduce-scatter.6.cloned.1.call-start = ((), (), s32[]{:S(2)}) async-start(), calls=%async_computation.14 | async-start | bytes 2621440 | tf_op jit(solution)/shard_map/reduce_scatter | solution.py:67
  542.8 59.5 %collective-permute-start.43 = (bf16[4,64,4096]{2,1,0:T(8,128)(2,1)}, bf16[4,64,4096]{2,1,0:T(8,128)(2,1)S(1)}, u32[]{:S(2)}, u32[]{:S(2)}) collective-permute-start(bf16[4,64,4096]{2,1,0:T(8,128)(2,1)} %pad_maximum_fusion), channel_id=1, source_target_pairs={{0,2},{2,0},{4,6},{6,4},{8,10},{10,8},{12,14},{14,12},{16,18},{18,... | collective-permute-start | bytes 6291464 | tf_op jit(solution)/shard_map/ppermute | solution.py:46
  543.3 59.0 %collective-permute-start.44 = (bf16[4,64,4096]{2,1,0:T(8,128)(2,1)}, bf16[4,64,4096]{2,1,0:T(8,128)(2,1)}, u32[]{:S(2)}, u32[]{:S(2)}) collective-permute-start(bf16[4,64,4096]{2,1,0:T(8,128)(2,1)} %pad_maximum_fusion.1), channel_id=1, source_target_pairs={{0,4},{2,6},{4,0},{6,2},{8,12},{10,14},{12,8},{14,10},{16,20},{18,... | collective-permute-start | bytes 6291464 | tf_op jit(solution)/shard_map/ppermute | solution.py:46
  613.2 27.1 %all-to-all-start.3 = ((bf16[16,8,2048]{2,1,0:T(8,128)(2,1)}), bf16[16,8,2048]{2,1,0:T(8,128)(2,1)}, u32[]{:S(2)}, u32[]{:S(2)}) async-start(bf16[16,8,2048]{2,1,0:T(8,128)(2,1)} %broadcast_in_dim.135), calls=%async_computation.3 | async-start | bytes 1048576 | tf_op jit(solution)/shard_map/all_to_all | solution.py:154
  617.5 114.9 %reduce-scatter.4.cloned.1.call-start = ((), (), s32[]{:S(2)}) async-start(), calls=%async_computation.13 | async-start | bytes 2621440 | tf_op jit(solution)/shard_map/reduce_scatter | solution.py:67
  644.6 33.0 %collective-permute-start.48 = (bf16[2048,1024]{1,0:T(8,128)(2,1)}, bf16[2048,1024]{1,0:T(8,128)(2,1)}, u32[]{:S(2)}, u32[]{:S(2)}) collective-permute-start(bf16[2048,1024]{1,0:T(8,128)(2,1)} %get-tuple-element.409), channel_id=1, source_target_pairs={{0,1},{1,0},{2,3},{3,2},{4,5},{5,4},{6,7},{7,6},{8,9},{9,8},{10,11... | collective-permute-start | bytes 12582920 | tf_op jit(solution)/shard_map/ppermute | solution.py:50
  646.6 102.0 %reduce-scatter.8.cloned.1.call-start = ((), (), s32[]{:S(2)}) async-start(), calls=%async_computation.15 | async-start | bytes 1310720 | tf_op jit(solution)/shard_map/reduce_scatter | solution.py:67
  649.8 25.9 %collective-permute-start.49 = (bf16[4,64,2048]{2,1,0:T(8,128)(2,1)}, bf16[4,64,2048]{2,1,0:T(8,128)(2,1)}, u32[]{:S(2)}, u32[]{:S(2)}) collective-permute-start(bf16[4,64,2048]{2,1,0:T(8,128)(2,1)} %pad_maximum_fusion.4), channel_id=1, source_target_pairs={{0,2},{2,0},{4,6},{6,4},{8,10},{10,8},{12,14},{14,12},{16,18},{18,... | collective-permute-start | bytes 3145736 | tf_op jit(solution)/shard_map/ppermute | solution.py:46
  651.3 26.3 %collective-permute-start.50 = (bf16[4,64,2048]{2,1,0:T(8,128)(2,1)}, bf16[4,64,2048]{2,1,0:T(8,128)(2,1)}, u32[]{:S(2)}, u32[]{:S(2)}) collective-permute-start(bf16[4,64,2048]{2,1,0:T(8,128)(2,1)} %pad_maximum_fusion.5), channel_id=1, source_target_pairs={{0,4},{2,6},{4,0},{6,2},{8,12},{10,14},{12,8},{14,10},{16,20},{18,... | collective-permute-start | bytes 3145736 | tf_op jit(solution)/shard_map/ppermute | solution.py:46
  732.3 32.9 %all-to-all-start.4 = ((bf16[4,128,1024]{2,1,0:T(8,128)(2,1)}), bf16[4,128,1024]{2,1,0:T(8,128)(2,1)}, u32[]{:S(2)}, u32[]{:S(2)}) async-start(bf16[4,128,1024]{2,1,0:T(8,128)(2,1)} %add_convert_fusion.1), calls=%async_computation.6 | async-start | bytes 2097152 | tf_op jit(solution)/shard_map/all_to_all | solution.py:63
  (108 other events, 745.6 us)
Sparse Core Ops, SparseCore 0:
  56.7 38.0 all-gather.4
  140.0 33.6 all-gather.8
  208.5 27.7 all-gather.6
  542.9 58.1 all-gather.10
  613.3 50.7 reduce-scatter.5
  666.3 44.8 reduce-scatter.3
  714.0 26.4 reduce-scatter.7

commit v4 on v3

--- a/solution.py
+++ b/solution.py
@@ -376,6 +376,30 @@
         ref[...] += part
 
 
+def held_back(refs, held, sems, into=()):
+    def copies():
+        places = [held.at[i] for i in range(len(refs) - len(into))] + list(into)
+        return [pltpu.make_async_copy(ref, place, sems.at[i]) for i, (ref, place) in enumerate(zip(refs, places))]
+
+    @pl.when(pl.program_id(0) == 0)
+    def _():
+        for copy in copies():
+            copy.start()
+
+    def arrive():
+        for copy in copies():
+            copy.wait()
+
+    return arrive
+
+
+ANYWHERE = pl.BlockSpec(memory_space=pl.ANY)
+
+
+def held_scratch(count, copies=None):
+    return [pltpu.VMEM((count, LEN, D), f32), pltpu.SemaphoreType.DMA((copies or count,))]
+
+
 def at_end(fn):
     pl.when(pl.program_id(0) == pl.num_programs(0) - 1)(fn)
 
@@ -433,14 +457,18 @@
 
 
 def attend_last_kernel(
-    na_ref, w_ref, bias_ref, part_ref, tok_ref, hot_ref, mod_ref, out_ref, acc_ref, mid_ref, nm_ref, nm_t_ref
+    na_ref, w_ref, bias_ref, part_ref, tok_ref, hot_ref, mod_ref, out_ref, acc_ref, mid_ref, nm_ref, nm_t_ref,
+    held, sems,
 ):
+    arrive = held_back([part_ref], held, sems)
     out = attend_pair(na_ref, w_ref, bias_ref)
     out_ref[...] = out
-    add_up(acc_ref, matmul_nt(out, w_ref[:, 3 * PAIR :]), part_ref)
+    add_up(acc_ref, matmul_nt(out, w_ref[:, 3 * PAIR :]))
 
     @at_end
     def _():
+        arrive()
+        acc_ref[...] += held[0]
         middle = tok_ref[...].astype(f32) + spread(hot_ref[...], mod_ref[:, :D]) * acc_ref[...]
         mid_ref[...] = middle
         hat, _ = normed(middle)
@@ -472,7 +500,7 @@
             whole(LEN, D),
             columns(D, 4 * PAIR),
             whole(LEN, LEN),
-            whole(LEN, D),
+            ANYWHERE,
             whole(LEN, D),
             whole(LEN, 24),
             whole(ITEMS, 3 * D),
@@ -486,6 +514,7 @@
             sds((D, LEN), bf16),
         ],
         steps * ATTEND_FLOPS,
+        held_scratch(1),
     )(na, w, bias, part, tokens, hot, mod)
 
 
@@ -527,19 +556,20 @@
 def attend_back_last_kernel(
     na_ref, na_t_ref, go_ref, go_t_ref, o_ref, w_ref, bias_ref,
     part_ref, tok_ref, gm_ref, hot_ref, hot_t_ref, mod_ref,
-    dw_ref, gt_ref, items_ref, acc_ref,
+    dw_ref, gt_ref, items_ref, acc_ref, held, sems,
 ):
-    part = attend_pair_back(na_ref, na_t_ref, go_ref, go_t_ref, o_ref, w_ref, bias_ref, dw_ref)
-    add_up(acc_ref, part, part_ref)
+    arrive = held_back([part_ref, gm_ref], held, sems)
+    add_up(acc_ref, attend_pair_back(na_ref, na_t_ref, go_ref, go_t_ref, o_ref, w_ref, bias_ref, dw_ref))
 
     @at_end
     def _():
-        grad = acc_ref[...]
+        arrive()
+        grad = acc_ref[...] + held[0]
         hat, factor = normed(tok_ref[...].astype(f32))
         items_ref[:, :D] = item_sum(hot_t_ref[...], grad * hat)
         items_ref[:, D:] = item_sum(hot_t_ref[...], grad)
         inner = normed_back(hat, factor, grad * (1.0 + spread(hot_ref[...], mod_ref[...])))
-        gt_ref[...] = (gm_ref[...] + inner).astype(bf16)
+        gt_ref[...] = (held[1] + inner).astype(bf16)
 
 
 def attend_back_specs():
@@ -573,9 +603,9 @@
         (steps,),
         attend_back_specs()
         + [
+            ANYWHERE,
             whole(LEN, D),
-            whole(LEN, D),
-            whole(LEN, D),
+            ANYWHERE,
             whole(LEN, 24),
             whole(2 * ITEMS, LEN),
             whole(ITEMS, D),
@@ -583,7 +613,7 @@
         [columns(D, 4 * PAIR), whole(LEN, D), whole(2 * ITEMS, 2 * D)],
         [sds(w.shape, bf16), sds((LEN, D), bf16), sds((2 * ITEMS, 2 * D), f32)],
         3 * steps * ATTEND_FLOPS,
-        [pltpu.VMEM((LEN, D), f32)],
+        [pltpu.VMEM((LEN, D), f32)] + held_scratch(2),
     )(na, na_t, go, go_t, out, w, bias_t, part, tokens, grad_middle, hot, hot_t, mod)
 
 
@@ -602,13 +632,17 @@
 
 
 def mlp_last_kernel(
-    nm_ref, w0_ref, w1_ref, part_ref, mid_ref, hot_ref, mod_ref, h0_ref, h1_ref, acc_ref, res_ref, nh_ref, nh_t_ref
+    nm_ref, w0_ref, w1_ref, part_ref, mid_ref, hot_ref, mod_ref, h0_ref, h1_ref, acc_ref, res_ref, nh_ref, nh_t_ref,
+    held, sems,
 ):
-    add_up(acc_ref, mlp_part(nm_ref, (w0_ref, w1_ref), (h0_ref, h1_ref)), part_ref)
+    arrive = held_back([part_ref, mid_ref], held, sems)
+    add_up(acc_ref, mlp_part(nm_ref, (w0_ref, w1_ref), (h0_ref, h1_ref)))
 
     @at_end
     def _():
-        residual = mid_ref[...] + spread(hot_ref[...], mod_ref[...]) * acc_ref[...]
+        arrive()
+        acc_ref[...] += held[0]
+        residual = held[1] + spread(hot_ref[...], mod_ref[...]) * acc_ref[...]
         res_ref[...] = residual
         hat, _ = normed(residual)
         nh_ref[...] = hat.astype(bf16)
@@ -637,7 +671,7 @@
         (steps,),
         [whole(LEN, D)]
         + [columns(D, 2 * BLOCK)] * 2
-        + [whole(LEN, D), whole(LEN, D), whole(LEN, 24), whole(ITEMS, D)],
+        + [ANYWHERE, ANYWHERE, whole(LEN, 24), whole(ITEMS, D)],
         [columns(LEN, BLOCK)] * 2 + [whole(LEN, D), whole(LEN, D), whole(LEN, D), whole(D, LEN)],
         [
             hidden,
@@ -648,6 +682,7 @@
             sds((D, LEN), bf16),
         ],
         8 * steps * LEN * D * BLOCK,
+        held_scratch(2),
     )(nm, *ws, part, middle, hot, mod)
     return [h0, h1], *rest
 
@@ -672,22 +707,23 @@
 def mlp_back_last_kernel(
     nm_t_ref, g_ref, g_t_ref, h0_ref, h1_ref, w0_ref, w1_ref,
     part_ref, mid_ref, gr_ref, out_ref, hot_ref, hot_t_ref, mod_ref,
-    dw_ref, gm_ref, go_ref, go_t_ref, items_ref, acc_ref,
+    dw_ref, gm_ref, go_ref, go_t_ref, items_ref, acc_ref, held, sems,
 ):
-    part = mlp_part_back(nm_t_ref, g_ref, g_t_ref, (h0_ref, h1_ref), (w0_ref, w1_ref), dw_ref)
-    add_up(acc_ref, part, part_ref)
+    arrive = held_back([part_ref, mid_ref, out_ref, gr_ref], held, sems, [gm_ref])
+    add_up(acc_ref, mlp_part_back(nm_t_ref, g_ref, g_t_ref, (h0_ref, h1_ref), (w0_ref, w1_ref), dw_ref))
 
     @at_end
     def _():
-        grad = acc_ref[...]
-        hat, factor = normed(mid_ref[...])
+        arrive()
+        grad = acc_ref[...] + held[0]
+        hat, factor = normed(held[1])
         items_ref[:, D : 2 * D] = item_sum(hot_t_ref[...], grad * hat)
         items_ref[:, 2 * D :] = item_sum(hot_t_ref[...], grad)
-        grad_middle = gr_ref[...] + normed_back(
+        grad_middle = gm_ref[...] + normed_back(
             hat, factor, grad * (1.0 + spread(hot_ref[...], mod_ref[:, D:]))
         )
         gm_ref[...] = grad_middle
-        items_ref[:, :D] = item_sum(hot_t_ref[...], grad_middle * out_ref[...])
+        items_ref[:, :D] = item_sum(hot_t_ref[...], grad_middle * held[2])
         grad_out = spread(hot_ref[...], mod_ref[:, :D]) * grad_middle
         go_ref[...] = grad_out.astype(bf16)
         go_t_ref[...] = flip(grad_out)
@@ -719,7 +755,7 @@
         mlp_back_last_kernel,
         (steps,),
         mlp_back_specs()
-        + [whole(LEN, D)] * 4
+        + [ANYWHERE] * 4
         + [whole(LEN, 24), whole(2 * ITEMS, LEN), whole(ITEMS, 2 * D)],
         [
             columns(D, 4 * BLOCK),
@@ -736,15 +772,16 @@
             sds((2 * ITEMS, 3 * D), f32),
         ],
         16 * steps * LEN * D * BLOCK,
-        [pltpu.VMEM((LEN, D), f32)],
+        [pltpu.VMEM((LEN, D), f32)] + held_scratch(3, 4),
     )(nm_t, g, g_t, *hiddens, *ws, part, middle, grad_res, attn_out, hot, hot_t, mod)
 
 
 def head_kernel(
     nh_ref, nh_t_ref, own_ref, peer_ref, target_ref, weight_ref, res_ref, mlp_ref, hot_ref, hot_t_ref, mod_ref,
     dw_own_ref, dw_peer_ref, loss_ref, gr_ref, gmo_ref, gmo_t_ref, items_ref,
-    logits, most, total, chosen, acc,
+    logits, most, total, chosen, acc, held, sems,
 ):
+    arrive = held_back([res_ref, mlp_ref], held, sems)
     step = pl.program_id(0)
     half = pl.num_programs(0) // 2
     block = own_ref.shape[1]
@@ -798,10 +835,11 @@
 
     @at_end
     def _():
-        hat, factor = normed(res_ref[...])
+        arrive()
+        hat, factor = normed(held[0])
         grad_res = normed_back(hat, factor, acc[...])
         gr_ref[...] = grad_res
-        items_ref[...] = item_sum(hot_t_ref[...], grad_res * mlp_ref[...])
+        items_ref[...] = item_sum(hot_t_ref[...], grad_res * held[1])
         grad_mlp = spread(hot_ref[...], mod_ref[...]) * grad_res
         gmo_ref[...] = grad_mlp.astype(bf16)
         gmo_t_ref[...] = flip(grad_mlp)
@@ -821,8 +859,8 @@
             w_spec,
             whole(LEN, 1),
             whole(LEN, 1),
-            whole(LEN, D),
-            whole(LEN, D),
+            ANYWHERE,
+            ANYWHERE,
             whole(LEN, 24),
             whole(2 * ITEMS, LEN),
             whole(ITEMS, D),
@@ -852,6 +890,7 @@
             pltpu.VMEM((LEN, 1), f32),
             pltpu.VMEM((LEN, 1), f32),
             pltpu.VMEM((LEN, D), f32),
+            *held_scratch(2),
         ],
     )(nh, nh_t, own, peer, target, weight, residual, mlp_out, hot, hot_t, mod)
 
@@ -1038,11 +1077,6 @@
     attn_w.block, mod_job.own = begin.wait((attn_w.block, mod_job.own))
     begin([code_w, attn_w, mod_job, mlp_a])
     begin.wait()
-    begin([code_w, mod_job])
-    mlp_a.group = begin.wait(mlp_a.group)
-    begin([code_w, attn_w, mlp_b, mod_job])
-    begin.wait()
-
     lengths = mine(item_lengths)[0]
     code_ids = mine(input_codes)[0]
     target_ids = mine(target_codes)[0]
@@ -1073,6 +1107,13 @@
     code_rows = other * (n * half_rows) + place_of(code_ids // rows) * half_rows + within % half_rows
     target = jnp.where(target_ids // codes_local == core, 0, codes_local) + target_ids % codes_local
 
+    begin([code_w, mod_job])
+    mlp_a.group, bias, bias_t, turn, hot, hot_t, code_rows, target, token_weight = begin.wait(
+        (mlp_a.group, bias, bias_t, turn, hot, hot_t, code_rows, target, token_weight)
+    )
+    begin([code_w, attn_w, mlp_b, mod_job])
+    begin.wait()
+
     def placed(values):
         values = values.reshape(-1, n, block_width)
         return jnp.take(values, block_at, axis=1).reshape(ITEMS, -1)

time: 820 us -> 809 us (0.987)
  Pallas kernels: 363 us -> 352 us
  waiting for transfers between devices: 163 us -> 154 us
where the time goes in v4:
time: 809 us; the launch traced here: 800 us
  Pallas kernels  352 us (44%)
  waiting for transfers between devices  154 us (19%)
  other arithmetic  108 us (13%)
  starting transfers between devices  88.8 us (11%)
  local copies, waits for them, and re-layouts  63.9 us (8%)
  between operations  22.8 us (3%)
  matrix products  10.6 us (1%)
    ppermute x46, waiting for transfers between devices, swap(): return lax.ppermute(values, 'dp', [(i, i ^ bits) for i in range(n)])  127 us
    ppermute x46, starting transfers between devices, swap(): return lax.ppermute(values, 'dp', [(i, i ^ bits) for i in range(n)])  56.9 us
    pallas_call x1, Pallas kernels, attend_back_last(): kernel_call(attend_back_last_kernel, (steps,), attend_back_specs() + [ANY...  50.7 us
    pallas_call x1, Pallas kernels, head(): kernel_call(head_kernel, (2 * half,), [whole(LEN, D), whole(D, LEN), w_sp...  47.4 us
    pallas_call x1, Pallas kernels, attend_back_first(): kernel_call(attend_back_first_kernel, (steps,), attend_back_specs(), [col...  46.7 us
    pallas_call x1, Pallas kernels, attend_last(): kernel_call(attend_last_kernel, (steps,), [whole(LEN, D), columns(D, 4 *...  34.3 us
    pallas_call x1, Pallas kernels, mlp_back_last(): kernel_call(mlp_back_last_kernel, (steps,), mlp_back_specs() + [ANYWHERE]...  32.8 us
    pallas_call x1, Pallas kernels, attend_first(): kernel_call(attend_first_kernel, (steps,), [whole(LEN, D), columns(D, 4 *...  28.8 us
  transfers between devices with their start and end apart: 71, of which 26 were waited for; matrix products, arithmetic and copies ran while one was open for 16% of the time, Pallas kernels for 37%

profile of v4, /device:TPU:0, one launch (start us, length us, event | category | flops | bytes accessed | tf_op | source)
XLA Modules:
  0.0 800.1 jit_solution(16432557055014169973)
XLA Ops:
  15.9 5.1 all-to-all-start
  48.1 4.3 all-to-all-start.1
  64.4 3.1 fusion.2
  67.5 21.1 %collective-permute-done.8 = f32[2,8,6144]{2,1,0:T(8,128)} collective-permute-done((f32[2,8,6144]{2,1,0:T(8,128)}, f32[2,8,6144]{2,1,0:T(8,128)}, u32[]{:S(2)}, u32[]{:S(2)}) %collective-permute-start.8) | collective-permute-done | bytes 393248 | tf_op jit(solution)/shard_map/ppermute | solution.py:46
  105.8 19.3 %collective-permute-done.10.refs_3_ = bf16[256,1024]{1,0:T(8,128)(2,1)} collective-permute-done((bf16[256,1024]{1,0:T(8,128)(2,1)}, bf16[256,1024]{1,0:T(8,128)(2,1)}, u32[]{:S(2)}, u32[]{:S(2)}) %collective-permute-start.10) | collective-permute-done | bytes 524320 | tf_op jit(solution)/shard_map/ppermute | solution.py:46
  127.8 4.4 shard_map.502.own_ref
  132.2 4.6 all-to-all-start.2
  140.8 21.3 %collective-permute-done.15.refs_1_ = bf16[256,2048]{1,0:T(8,128)(2,1)S(1)} collective-permute-done((bf16[256,2048]{1,0:T(8,128)(2,1)}, bf16[256,2048]{1,0:T(8,128)(2,1)S(1)}, u32[]{:S(2)}, u32[]{:S(2)}) %collective-permute-start.15) | collective-permute-done | bytes 1048608 | tf_op jit(solution)/shard_map/ppermute | solution.py:46
  163.3 4.5 all-to-all-done.2
  176.2 16.9 %shard_map.503 = (bf16[800,1024]{1,0:T(8,128)(2,1)}, bf16[800,1024]{1,0:T(8,128)(2,1)}, bf16[1024,800]{1,0:T(8,128)(2,1)}) custom-call(s32[800,1]{1,0:T(8,128)} %copy.137.code_ref, bf16[2048,1024]{1,0:T(8,128)(2,1)} %shard_map.502.own_ref, bf16[2048,1024]{1,0:T(8,128)(2,1)} %collective-permute-done.14.peer_ref, bf16[1024,1024]{1,0:T(8,128)(2,1)} %fusion.turn_ref, ...), custom_call_target="tpu_custom_call" | custom-call | flops 6710886400 | bytes 16777216 | tf_op jit(solution)/shard_map/pallas_call | solution.py:429
  193.1 8.5 %collective-permute-done.17.refs_3_ = bf16[128,2048]{1,0:T(8,128)(2,1)S(1)} collective-permute-done((bf16[128,2048]{1,0:T(8,128)(2,1)}, bf16[128,2048]{1,0:T(8,128)(2,1)S(1)}, u32[]{:S(2)}, u32[]{:S(2)}) %collective-permute-start.17) | collective-permute-done | bytes 524320 | tf_op jit(solution)/shard_map/ppermute | solution.py:46
  205.3 3.7 shard_map.504.w_ref
  213.3 28.8 %shard_map.505 = (bf16[800,512]{1,0:T(8,128)(2,1)}, f32[800,1024]{1,0:T(8,128)}) custom-call(bf16[800,1024]{1,0:T(8,128)(2,1)} %get-tuple-element.294.na_ref, bf16[1024,2048]{1,0:T(8,128)(2,1)} %shard_map.504.w_ref, f32[800,800]{1,0:T(8,128)} %get-tuple-element.295.bias_ref), custom_call_target="tpu_custom_call" | custom-call | flops 4666163200 | bytes 16777216 | tf_op jit(solution)/shard_map/pallas_call | solution.py:484
  242.2 4.1 collective-permute-done.22.refs_3_
  249.1 3.7 shard_map.506.w0_ref
  259.5 34.3 %shard_map.507 = (bf16[800,512]{1,0:T(8,128)(2,1)}, f32[800,1024]{1,0:T(8,128)}, f32[800,1024]{1,0:T(8,128)}, bf16[800,1024]{1,0:T(8,128)(2,1)}, bf16[1024,800]{1,0:T(8,128)(2,1)}) custom-call(bf16[800,1024]{1,0:T(8,128)(2,1)} %get-tuple-element.294.na_ref, bf16[1024,2048]{1,0:T(8,128)(2,1)} %collective-permute-done.21.w_ref, ...), custom_call_target="tpu_custom_call" | custom-call | flops 4666163200 | bytes 16777216 | tf_op jit(solution)/shard_map/pallas_call | solution.py:496
  295.8 3.7 shard_map.508.w1_ref
  302.6 14.0 %shard_map.509 = (f32[800,1024]{1,0:T(8,128)}, f32[800,1024]{1,0:T(8,128)}, f32[800,1024]{1,0:T(8,128)}) custom-call(bf16[800,1024]{1,0:T(8,128)(2,1)} %get-tuple-element.323.nm_ref, bf16[1024,2048]{1,0:T(8,128)(2,1)} %shard_map.506.w0_ref, bf16[1024,2048]{1,0:T(8,128)(2,1)} %shard_map.508.w1_ref), custom_call_target="tpu_custom_call" | custom-call | flops 6710886400 | bytes 16777216 | tf_op jit(solution)/shard_map/pallas_call | solution.py:655
  317.6 3.7 shard_map.510.own_ref
  323.1 17.6 %shard_map.511 = (f32[800,1024]{1,0:T(8,128)}, f32[800,1024]{1,0:T(8,128)}, f32[800,1024]{1,0:T(8,128)}, f32[800,1024]{1,0:T(8,128)}, bf16[800,1024]{1,0:T(8,128)(2,1)}, /*index=5*/bf16[1024,800]{1,0:T(8,128)(2,1)}) custom-call(bf16[800,1024]{1,0:T(8,128)(2,1)} %get-tuple-element.323.nm_ref, bf16[1024,2048]{1,0:T(8,128)(2,1)} %collective-permute-done.26.w0_ref, ...), custom_call_target="tpu_custom_call" | custom-call | flops 6710886400 | bytes 16777216 | tf_op jit(solution)/shard_map/pallas_call | solution.py:669
  340.7 47.4 %shard_map.512 = (bf16[1024,2048]{1,0:T(8,128)(2,1)}, bf16[1024,2048]{1,0:T(8,128)(2,1)}, f32[8,128]{1,0:T(8,128)}, f32[800,1024]{1,0:T(8,128)}, bf16[800,1024]{...) custom-call(bf16[800,1024]{1,0:T(8,128)(2,1)} %get-tuple-element.341.nh_ref, ...), custom_call_target="tpu_custom_call" | custom-call | flops 20132659200 | bytes 16777216 | tf_op jit(solution)/shard_map/pallas_call | solution.py:852
  388.7 26.4 %shard_map.513 = (bf16[1024,4096]{1,0:T(8,128)(2,1)}, f32[800,1024]{1,0:T(8,128)}) custom-call(bf16[1024,800]{1,0:T(8,128)(2,1)} %get-tuple-element.353.nm_t_ref, bf16[800,1024]{1,0:T(8,128)(2,1)} %get-tuple-element.354.g_ref, bf16[1024,800]{1,0:T(8,128)(2,1)} %get-tuple-element.355.g_t_ref, f32[800,1024]{1,0:T(8,128)} %get-tuple-element.356.h0_ref, ...), custom_call_target="tpu_custom_call" | custom-call | flops 13421772800 | bytes 16777216 | tf_op jit(solution)/shard_map/pallas_call | solution.py:742
  415.1 4.0 fusion.25
  421.6 32.8 %shard_map.514 = (bf16[1024,4096]{1,0:T(8,128)(2,1)}, f32[800,1024]{1,0:T(8,128)}, bf16[800,1024]{1,0:T(8,128)(2,1)}, bf16[1024,800]{1,0:T(8,128)(2,1)}, f32[16,3072]{1,0:T(8,128)}) custom-call(bf16[1024,800]{1,0:T(8,128)(2,1)} %get-tuple-element.353.nm_t_ref, bf16[800,1024]{1,0:T(8,128)(2,1)} %get-tuple-element.354.g_ref, ...), custom_call_target="tpu_custom_call" | custom-call | flops 13421772800 | bytes 16777216 | tf_op jit(solution)/shard_map/pallas_call | solution.py:754
  459.9 5.2 fusion.10
  473.5 46.7 %shard_map.515 = (bf16[1024,2048]{1,0:T(8,128)(2,1)}, f32[800,1024]{1,0:T(8,128)}) custom-call(bf16[800,1024]{1,0:T(8,128)(2,1)} %get-tuple-element.294.na_ref, bf16[1024,800]{1,0:T(8,128)(2,1)} %get-tuple-element.387.na_t_ref, bf16[800,1024]{1,0:T(8,128)(2,1)} %get-tuple-element.388.go_ref, bf16[1024,800]{1,0:T(8,128)(2,1)} %get-tuple-element.389.go_t_ref, ...), custom_call_target="tpu_custom_call" | custom-call | flops 13998489600 | bytes 16777216 | tf_op jit(solution)/shard_map/pallas_call | solution.py:589
  520.2 4.0 fusion.3
  527.4 3.4 convert_add_fusion.3
  534.5 4.9 convert_add_fusion
  539.4 50.7 %shard_map.516 = (bf16[1024,2048]{1,0:T(8,128)(2,1)}, bf16[800,1024]{1,0:T(8,128)(2,1)}, f32[16,2048]{1,0:T(8,128)}) custom-call(bf16[800,1024]{1,0:T(8,128)(2,1)} %get-tuple-element.294.na_ref, bf16[1024,800]{1,0:T(8,128)(2,1)} %get-tuple-element.387.na_t_ref, bf16[800,1024]{1,0:T(8,128)(2,1)} %get-tuple-element.388.go_ref, ...), custom_call_target="tpu_custom_call" | custom-call | flops 13998489600 | bytes 16777216 | tf_op jit(solution)/shard_map/pallas_call | solution.py:601
  592.0 4.1 fusion.29
  596.1 3.9 add_convert_fusion
  600.9 4.2 all-to-all-start.3
  609.0 10.0 %shard_map.517 = (bf16[2048,1024]{1,0:T(8,128)(2,1)}, bf16[800,1024]{1,0:T(8,128)(2,1)}) custom-call(s32[1,800]{1,0:T(1,128)} %reshape.592.code_ref, bf16[800,1024]{1,0:T(8,128)(2,1)} %get-tuple-element.418.gt_ref, bf16[1024,1024]{1,0:T(8,128)(2,1)} %fusion.turn_ref), custom_call_target="tpu_custom_call" | custom-call | flops 3355443200 | bytes 16777216 | tf_op jit(solution)/shard_map/pallas_call | solution.py:918
  619.1 4.0 collective-permute-done.46
  623.7 4.1 all-to-all-done.3
  646.5 7.7 shard_map.518
  654.3 9.1 %collective-permute-done.49 = bf16[4,64,2048]{2,1,0:T(8,128)(2,1)} collective-permute-done((bf16[4,64,2048]{2,1,0:T(8,128)(2,1)}, bf16[4,64,2048]{2,1,0:T(8,128)(2,1)}, u32[]{:S(2)}, u32[]{:S(2)}) %collective-permute-start.49) | collective-permute-done | bytes 1048608 | tf_op jit(solution)/shard_map/ppermute | solution.py:46
  665.1 4.2 fusion.33
  669.3 3.1 add_convert_fusion.2
  678.7 8.3 %collective-permute-done.51 = bf16[2,128,1024]{2,1,0:T(8,128)(2,1)S(1)} collective-permute-done((bf16[2,128,1024]{2,1,0:T(8,128)(2,1)}, bf16[2,128,1024]{2,1,0:T(8,128)(2,1)S(1)}, u32[]{:S(2)}, u32[]{:S(2)}) %collective-permute-start.51) | collective-permute-done | bytes 524320 | tf_op jit(solution)/shard_map/ppermute | solution.py:46
  698.5 18.7 %collective-permute-done.55 = bf16[4,128,1024]{2,1,0:T(8,128)(2,1)S(1)} collective-permute-done((bf16[4,128,1024]{2,1,0:T(8,128)(2,1)S(1)}, bf16[4,128,1024]{2,1,0:T(8,128)(2,1)S(1)}, u32[]{:S(2)}, u32[]{:S(2)}) %collective-permute-start.55) | collective-permute-done | bytes 1048608 | tf_op jit(solution)/shard_map/ppermute | solution.py:46
  719.8 8.4 %all-to-all-start.4 = ((bf16[4,128,1024]{2,1,0:T(8,128)(2,1)}), bf16[4,128,1024]{2,1,0:T(8,128)(2,1)}, u32[]{:S(2)}, u32[]{:S(2)}) async-start(bf16[4,128,1024]{2,1,0:T(8,128)(2,1)} %add_convert_fusion.1), calls=%async_computation.6 | async-start | bytes 2097152 | tf_op jit(solution)/shard_map/all_to_all | solution.py:63
  743.2 9.7 %all-to-all-done.4 = bf16[4,128,1024]{2,1,0:T(8,128)(2,1)} async-done(((bf16[4,128,1024]{2,1,0:T(8,128)(2,1)}), bf16[4,128,1024]{2,1,0:T(8,128)(2,1)}, u32[]{:S(2)}, u32[]{:S(2)}) %all-to-all-start.4) | async-done | bytes 1048608 | tf_op jit(solution)/shard_map/all_to_all | solution.py:63
  759.8 3.6 all-to-all-start.5
  764.4 6.1 all-to-all-done.5
  781.5 3.1 multiply_subtract_fusion
  788.0 3.6 multiply_subtract_fusion.1
  (498 shorter events, 209.2 us)
Async XLA Ops:
  15.9 30.1 %all-to-all-start = ((bf16[4,128,1024]{2,1,0:T(8,128)(2,1)}), bf16[4,128,1024]{2,1,0:T(8,128)(2,1)}, u32[]{:S(2)}, u32[]{:S(2)}) async-start(bf16[4,128,1024]{2,1,0:T(8,128)(2,1)} %broadcast_in_dim.80), calls=%async_computation | async-start | bytes 2097152 | tf_op jit(solution)/shard_map/all_to_all | solution.py:63
  48.1 41.7 %all-to-all-start.1 = ((bf16[4,64,2048]{2,1,0:T(8,128)(2,1)}), bf16[4,64,2048]{2,1,0:T(8,128)(2,1)}, u32[]{:S(2)}, u32[]{:S(2)}) async-start(bf16[4,64,2048]{2,1,0:T(8,128)(2,1)} %broadcast_in_dim.83), calls=%async_computation.1 | async-start | bytes 2097152 | tf_op jit(solution)/shard_map/all_to_all | solution.py:63
  52.4 53.4 %all-gather.5.cloned.1.call-start = ((), (), s32[]{:S(2)}) async-start(), calls=%async_computation.9 | async-start | bytes 1310720 | tf_op jit(solution)/shard_map/all_gather | solution.py:112
  55.8 34.1 %collective-permute-start.6 = (bf16[512,1024]{1,0:T(8,128)(2,1)}, bf16[512,1024]{1,0:T(8,128)(2,1)}, u32[]{:S(2)}, u32[]{:S(2)}) collective-permute-start(bf16[512,1024]{1,0:T(8,128)(2,1)} %bitcast.10.refs_0_), channel_id=1, source_target_pairs={{0,2},{2,0},{4,6},{6,4},{8,10},{10,8},{12,14},{14,12},{16,18},{18,... | collective-permute-start | bytes 3145736 | tf_op jit(solution)/shard_map/ppermute | solution.py:46
  57.3 32.6 %collective-permute-start.7 = (bf16[512,1024]{1,0:T(8,128)(2,1)}, bf16[512,1024]{1,0:T(8,128)(2,1)}, u32[]{:S(2)}, u32[]{:S(2)}) collective-permute-start(bf16[512,1024]{1,0:T(8,128)(2,1)} %bitcast.10.refs_0_), channel_id=1, source_target_pairs={{0,4},{2,6},{4,0},{6,2},{8,12},{10,14},{12,8},{14,10},{16,20},{18,... | collective-permute-start | bytes 3145736 | tf_op jit(solution)/shard_map/ppermute | solution.py:46
  61.4 27.2 %collective-permute-start.8 = (f32[2,8,6144]{2,1,0:T(8,128)}, f32[2,8,6144]{2,1,0:T(8,128)}, u32[]{:S(2)}, u32[]{:S(2)}) collective-permute-start(f32[2,8,6144]{2,1,0:T(8,128)} %get-tuple-element.247), channel_id=1, source_target_pairs={{0,2},{2,0},{4,6},{6,4},{8,10},{10,8},{12,14},{14,12},{16,18},{18,... | collective-permute-start | bytes 1179656 | tf_op jit(solution)/shard_map/ppermute | solution.py:46
  61.9 27.9 %collective-permute-start.9 = (f32[2,8,6144]{2,1,0:T(8,128)}, f32[2,8,6144]{2,1,0:T(8,128)}, u32[]{:S(2)}, u32[]{:S(2)}) collective-permute-start(f32[2,8,6144]{2,1,0:T(8,128)} %get-tuple-element.248), channel_id=1, source_target_pairs={{0,4},{2,6},{4,0},{6,2},{8,12},{10,14},{12,8},{14,10},{16,20},{18,... | collective-permute-start | bytes 1179656 | tf_op jit(solution)/shard_map/ppermute | solution.py:46
  96.2 29.2 %collective-permute-start.12 = (f32[4,8,6144]{2,1,0:T(8,128)}, f32[4,8,6144]{2,1,0:T(8,128)}, u32[]{:S(2)}, u32[]{:S(2)}) collective-permute-start(f32[4,8,6144]{2,1,0:T(8,128)} %get-tuple-element.255), channel_id=1, source_target_pairs={{0,2},{2,0},{4,6},{6,4},{8,10},{10,8},{12,14},{14,12},{16,18},{18,... | collective-permute-start | bytes 2359304 | tf_op jit(solution)/shard_map/ppermute | solution.py:46
  96.8 28.6 %collective-permute-start.13 = (f32[4,8,6144]{2,1,0:T(8,128)}, f32[4,8,6144]{2,1,0:T(8,128)}, u32[]{:S(2)}, u32[]{:S(2)}) collective-permute-start(f32[4,8,6144]{2,1,0:T(8,128)} %get-tuple-element.256), channel_id=1, source_target_pairs={{0,4},{2,6},{4,0},{6,2},{8,12},{10,14},{12,8},{14,10},{16,20},{18,... | collective-permute-start | bytes 2359304 | tf_op jit(solution)/shard_map/ppermute | solution.py:46
  132.2 35.6 %collective-permute-start.14 = (bf16[2048,1024]{1,0:T(8,128)(2,1)}, bf16[2048,1024]{1,0:T(8,128)(2,1)}, u32[]{:S(2)}, u32[]{:S(2)}) collective-permute-start(bf16[2048,1024]{1,0:T(8,128)(2,1)} %shard_map.502.own_ref), channel_id=1, source_target_pairs={{0,1},{1,0},{2,3},{3,2},{4,5},{5,4},{6,7},{7,6},{8,9},{9,8},{10,11... | collective-permute-start | bytes 12582920 | tf_op jit(solution)/shard_map/ppermute | solution.py:50
  132.2 35.6 %all-to-all-start.2 = ((f32[4,8,6144]{2,1,0:T(8,128)}), f32[4,8,6144]{2,1,0:T(8,128)S(1)}, u32[]{:S(2)}, u32[]{:S(2)}) async-start(f32[4,8,6144]{2,1,0:T(8,128)} %fusion.18), calls=%async_computation.2 | async-start | bytes 1572864 | tf_op jit(solution)/shard_map/all_to_all | solution.py:63
  136.8 72.3 %all-gather.9.cloned.1.call-start = ((), (), s32[]{:S(2)}) async-start(), calls=%async_computation.11 | async-start | bytes 1310720 | tf_op jit(solution)/shard_map/all_gather | solution.py:112
  136.8 25.4 %collective-permute-start.15 = (bf16[256,2048]{1,0:T(8,128)(2,1)}, bf16[256,2048]{1,0:T(8,128)(2,1)S(1)}, u32[]{:S(2)}, u32[]{:S(2)}) collective-permute-start(bf16[256,2048]{1,0:T(8,128)(2,1)} %bitcast.23.refs_0_), channel_id=1, source_target_pairs={{0,2},{2,0},{4,6},{6,4},{8,10},{10,8},{12,14},{14,12},{16,18},{18,... | collective-permute-start | bytes 3145736 | tf_op jit(solution)/shard_map/ppermute | solution.py:46
  139.8 113.1 %all-gather.7.cloned.1.call-start = ((), (), s32[]{:S(2)}) async-start(), calls=%async_computation.10 | async-start | bytes 1310720 | tf_op jit(solution)/shard_map/all_gather | solution.py:112
  169.5 33.3 %collective-permute-start.19 = (bf16[256,2048]{1,0:T(8,128)(2,1)}, bf16[256,2048]{1,0:T(8,128)(2,1)S(1)}, u32[]{:S(2)}, u32[]{:S(2)}) collective-permute-start(bf16[256,2048]{1,0:T(8,128)(2,1)} %all-gather.5.cloned.1.call-done.refs_0_), channel_id=1, source_target_pairs={{0,2},{2,0},{4,6},{6,4},{8,10},{10,8},{12,14},{14,12},{16,18},{18,... | collective-permute-start | bytes 3145736 | tf_op jit(solution)/shard_map/ppermute | solution.py:46
  171.0 31.9 %collective-permute-start.20 = (bf16[256,2048]{1,0:T(8,128)(2,1)}, bf16[256,2048]{1,0:T(8,128)(2,1)S(1)}, u32[]{:S(2)}, u32[]{:S(2)}) collective-permute-start(bf16[256,2048]{1,0:T(8,128)(2,1)} %all-gather.5.cloned.1.call-done.refs_0_), channel_id=1, source_target_pairs={{0,4},{2,6},{4,0},{6,2},{8,12},{10,14},{12,8},{14,10},{16,20},{18,... | collective-permute-start | bytes 3145736 | tf_op jit(solution)/shard_map/ppermute | solution.py:46
  175.1 26.6 %collective-permute-start.17 = (bf16[128,2048]{1,0:T(8,128)(2,1)}, bf16[128,2048]{1,0:T(8,128)(2,1)S(1)}, u32[]{:S(2)}, u32[]{:S(2)}) collective-permute-start(bf16[128,2048]{1,0:T(8,128)(2,1)} %slice.380), channel_id=1, source_target_pairs={{0,2},{2,0},{4,6},{6,4},{8,10},{10,8},{12,14},{14,12},{16,18},{18,... | collective-permute-start | bytes 1572872 | tf_op jit(solution)/shard_map/ppermute | solution.py:46
  175.6 27.2 %collective-permute-start.18 = (bf16[128,2048]{1,0:T(8,128)(2,1)}, bf16[128,2048]{1,0:T(8,128)(2,1)S(1)}, u32[]{:S(2)}, u32[]{:S(2)}) collective-permute-start(bf16[128,2048]{1,0:T(8,128)(2,1)} %slice.381), channel_id=1, source_target_pairs={{0,4},{2,6},{4,0},{6,2},{8,12},{10,14},{12,8},{14,10},{16,20},{18,... | collective-permute-start | bytes 1572872 | tf_op jit(solution)/shard_map/ppermute | solution.py:46
  209.1 38.3 %collective-permute-start.21 = (bf16[1024,2048]{1,0:T(8,128)(2,1)}, bf16[1024,2048]{1,0:T(8,128)(2,1)}, u32[]{:S(2)}, u32[]{:S(2)}) collective-permute-start(bf16[1024,2048]{1,0:T(8,128)(2,1)} %shard_map.504.w_ref), channel_id=1, source_target_pairs={{0,1},{1,0},{2,3},{3,2},{4,5},{5,4},{6,7},{7,6},{8,9},{9,8},{10,11... | collective-permute-start | bytes 12582920 | tf_op jit(solution)/shard_map/ppermute | solution.py:50
  209.2 425.1 %all-gather.11.cloned.1.call-start = ((), (), s32[]{:S(2)}) async-start(), calls=%async_computation.12 | async-start | bytes 1114112 | tf_op jit(solution)/shard_map/all_gather | solution.py:152
  209.2 37.4 %collective-permute-start.24 = (bf16[256,2048]{1,0:T(8,128)(2,1)}, bf16[256,2048]{1,0:T(8,128)(2,1)S(1)}, u32[]{:S(2)}, u32[]{:S(2)}) collective-permute-start(bf16[256,2048]{1,0:T(8,128)(2,1)} %all-gather.9.cloned.1.call-done.refs_0_), channel_id=1, source_target_pairs={{0,2},{2,0},{4,6},{6,4},{8,10},{10,8},{12,14},{14,12},{16,18},{18,... | collective-permute-start | bytes 3145736 | tf_op jit(solution)/shard_map/ppermute | solution.py:46
  209.9 36.7 %collective-permute-start.25 = (bf16[256,2048]{1,0:T(8,128)(2,1)}, bf16[256,2048]{1,0:T(8,128)(2,1)S(1)}, u32[]{:S(2)}, u32[]{:S(2)}) collective-permute-start(bf16[256,2048]{1,0:T(8,128)(2,1)} %all-gather.9.cloned.1.call-done.refs_0_), channel_id=1, source_target_pairs={{0,4},{2,6},{4,0},{6,2},{8,12},{10,14},{12,8},{14,10},{16,20},{18,... | collective-permute-start | bytes 3145736 | tf_op jit(solution)/shard_map/ppermute | solution.py:46
  211.4 34.9 %collective-permute-start.22 = (bf16[128,2048]{1,0:T(8,128)(2,1)}, bf16[128,2048]{1,0:T(8,128)(2,1)S(1)}, u32[]{:S(2)}, u32[]{:S(2)}) collective-permute-start(bf16[128,2048]{1,0:T(8,128)(2,1)} %slice.383), channel_id=1, source_target_pairs={{0,2},{2,0},{4,6},{6,4},{8,10},{10,8},{12,14},{14,12},{16,18},{18,... | collective-permute-start | bytes 1572872 | tf_op jit(solution)/shard_map/ppermute | solution.py:46
  212.8 33.7 %collective-permute-start.23 = (bf16[128,2048]{1,0:T(8,128)(2,1)}, bf16[128,2048]{1,0:T(8,128)(2,1)S(1)}, u32[]{:S(2)}, u32[]{:S(2)}) collective-permute-start(bf16[128,2048]{1,0:T(8,128)(2,1)} %slice.384), channel_id=1, source_target_pairs={{0,4},{2,6},{4,0},{6,2},{8,12},{10,14},{12,8},{14,10},{16,20},{18,... | collective-permute-start | bytes 1572872 | tf_op jit(solution)/shard_map/ppermute | solution.py:46
  252.8 41.0 %collective-permute-start.26 = (bf16[1024,2048]{1,0:T(8,128)(2,1)}, bf16[1024,2048]{1,0:T(8,128)(2,1)}, u32[]{:S(2)}, u32[]{:S(2)}) collective-permute-start(bf16[1024,2048]{1,0:T(8,128)(2,1)} %shard_map.506.w0_ref), channel_id=1, source_target_pairs={{0,1},{1,0},{2,3},{3,2},{4,5},{5,4},{6,7},{7,6},{8,9},{9,8},{10,11... | collective-permute-start | bytes 12582920 | tf_op jit(solution)/shard_map/ppermute | solution.py:50
  253.7 40.1 %collective-permute-start.29 = (bf16[256,2048]{1,0:T(8,128)(2,1)}, bf16[256,2048]{1,0:T(8,128)(2,1)S(1)}, u32[]{:S(2)}, u32[]{:S(2)}) collective-permute-start(bf16[256,2048]{1,0:T(8,128)(2,1)} %all-gather.7.cloned.1.call-done.refs_0_), channel_id=1, source_target_pairs={{0,2},{2,0},{4,6},{6,4},{8,10},{10,8},{12,14},{14,12},{16,18},{18,... | collective-permute-start | bytes 3145736 | tf_op jit(solution)/shard_map/ppermute | solution.py:46
  255.2 38.6 %collective-permute-start.30 = (bf16[256,2048]{1,0:T(8,128)(2,1)}, bf16[256,2048]{1,0:T(8,128)(2,1)S(1)}, u32[]{:S(2)}, u32[]{:S(2)}) collective-permute-start(bf16[256,2048]{1,0:T(8,128)(2,1)} %all-gather.7.cloned.1.call-done.refs_0_), channel_id=1, source_target_pairs={{0,4},{2,6},{4,0},{6,2},{8,12},{10,14},{12,8},{14,10},{16,20},{18,... | collective-permute-start | bytes 3145736 | tf_op jit(solution)/shard_map/ppermute | solution.py:46
  257.8 36.0 %collective-permute-start.27 = (bf16[128,2048]{1,0:T(8,128)(2,1)}, bf16[128,2048]{1,0:T(8,128)(2,1)S(1)}, u32[]{:S(2)}, u32[]{:S(2)}) collective-permute-start(bf16[128,2048]{1,0:T(8,128)(2,1)} %slice.385), channel_id=1, source_target_pairs={{0,2},{2,0},{4,6},{6,4},{8,10},{10,8},{12,14},{14,12},{16,18},{18,... | collective-permute-start | bytes 1572872 | tf_op jit(solution)/shard_map/ppermute | solution.py:46
  258.3 35.4 %collective-permute-start.28 = (bf16[128,2048]{1,0:T(8,128)(2,1)}, bf16[128,2048]{1,0:T(8,128)(2,1)S(1)}, u32[]{:S(2)}, u32[]{:S(2)}) collective-permute-start(bf16[128,2048]{1,0:T(8,128)(2,1)} %slice.386), channel_id=1, source_target_pairs={{0,4},{2,6},{4,0},{6,2},{8,12},{10,14},{12,8},{14,10},{16,20},{18,... | collective-permute-start | bytes 1572872 | tf_op jit(solution)/shard_map/ppermute | solution.py:46
  388.1 27.0 %collective-permute-start.35 = (bf16[1024,2048]{1,0:T(8,128)(2,1)}, bf16[1024,2048]{1,0:T(8,128)(2,1)}, u32[]{:S(2)}, u32[]{:S(2)}) collective-permute-start(bf16[1024,2048]{1,0:T(8,128)(2,1)} %get-tuple-element.352), channel_id=1, source_target_pairs={{0,1},{1,0},{2,3},{3,2},{4,5},{5,4},{6,7},{7,6},{8,9},{9,8},{10,11... | collective-permute-start | bytes 12582920 | tf_op jit(solution)/shard_map/ppermute | solution.py:50
  419.1 37.3 %collective-permute-start.38 = (bf16[1024,4096]{1,0:T(8,128)(2,1)}, bf16[1024,4096]{1,0:T(8,128)(2,1)}, u32[]{:S(2)}, u32[]{:S(2)}) collective-permute-start(bf16[1024,4096]{1,0:T(8,128)(2,1)} %get-tuple-element.365), channel_id=1, source_target_pairs={{0,1},{1,0},{2,3},{3,2},{4,5},{5,4},{6,7},{7,6},{8,9},{9,8},{10,11... | collective-permute-start | bytes 25165832 | tf_op jit(solution)/shard_map/ppermute | solution.py:50
  420.5 35.8 %collective-permute-start.36 = (bf16[2,64,2048]{2,1,0:T(8,128)(2,1)S(1)}, bf16[2,64,2048]{2,1,0:T(8,128)(2,1)S(1)}, u32[]{:S(2)}, u32[]{:S(2)}) collective-permute-start(bf16[2,64,2048]{2,1,0:T(8,128)(2,1)S(1)} %get-tuple-element.363), channel_id=1, source_target_pairs={{0,2},{2,0},{4,6},{6,4},{8,10},{10,8},{12,14},{14,12},{16,18},{18,... | collective-permute-start | bytes 1572872 | tf_op jit(solution)/shard_map/ppermute | solution.py:46
  421.1 35.2 %collective-permute-start.37 = (bf16[2,64,2048]{2,1,0:T(8,128)(2,1)S(1)}, bf16[2,64,2048]{2,1,0:T(8,128)(2,1)}, u32[]{:S(2)}, u32[]{:S(2)}) collective-permute-start(bf16[2,64,2048]{2,1,0:T(8,128)(2,1)S(1)} %get-tuple-element.364), channel_id=1, source_target_pairs={{0,4},{2,6},{4,0},{6,2},{8,12},{10,14},{12,8},{14,10},{16,20},{18,... | collective-permute-start | bytes 1572872 | tf_op jit(solution)/shard_map/ppermute | solution.py:46
  469.5 50.7 %collective-permute-start.39 = (bf16[4,64,2048]{2,1,0:T(8,128)(2,1)}, bf16[4,64,2048]{2,1,0:T(8,128)(2,1)}, u32[]{:S(2)}, u32[]{:S(2)}) collective-permute-start(bf16[4,64,2048]{2,1,0:T(8,128)(2,1)} %pad_maximum_fusion.2), channel_id=1, source_target_pairs={{0,2},{2,0},{4,6},{6,4},{8,10},{10,8},{12,14},{14,12},{16,18},{18,... | collective-permute-start | bytes 3145736 | tf_op jit(solution)/shard_map/ppermute | solution.py:46
  471.0 49.2 %collective-permute-start.40 = (bf16[4,64,2048]{2,1,0:T(8,128)(2,1)}, bf16[4,64,2048]{2,1,0:T(8,128)(2,1)}, u32[]{:S(2)}, u32[]{:S(2)}) collective-permute-start(bf16[4,64,2048]{2,1,0:T(8,128)(2,1)} %pad_maximum_fusion.3), channel_id=1, source_target_pairs={{0,4},{2,6},{4,0},{6,2},{8,12},{10,14},{12,8},{14,10},{16,20},{18,... | collective-permute-start | bytes 3145736 | tf_op jit(solution)/shard_map/ppermute | solution.py:46
  472.5 47.7 %collective-permute-start.41 = (bf16[2,64,4096]{2,1,0:T(8,128)(2,1)}, bf16[2,64,4096]{2,1,0:T(8,128)(2,1)}, u32[]{:S(2)}, u32[]{:S(2)}) collective-permute-start(bf16[2,64,4096]{2,1,0:T(8,128)(2,1)} %get-tuple-element.385), channel_id=1, source_target_pairs={{0,2},{2,0},{4,6},{6,4},{8,10},{10,8},{12,14},{14,12},{16,18},{18,... | collective-permute-start | bytes 3145736 | tf_op jit(solution)/shard_map/ppermute | solution.py:46
  473.1 47.1 %collective-permute-start.42 = (bf16[2,64,4096]{2,1,0:T(8,128)(2,1)}, bf16[2,64,4096]{2,1,0:T(8,128)(2,1)}, u32[]{:S(2)}, u32[]{:S(2)}) collective-permute-start(bf16[2,64,4096]{2,1,0:T(8,128)(2,1)} %get-tuple-element.386), channel_id=1, source_target_pairs={{0,4},{2,6},{4,0},{6,2},{8,12},{10,14},{12,8},{14,10},{16,20},{18,... | collective-permute-start | bytes 3145736 | tf_op jit(solution)/shard_map/ppermute | solution.py:46
  530.7 59.4 %collective-permute-start.45 = (bf16[1024,2048]{1,0:T(8,128)(2,1)}, bf16[1024,2048]{1,0:T(8,128)(2,1)}, u32[]{:S(2)}, u32[]{:S(2)}) collective-permute-start(bf16[1024,2048]{1,0:T(8,128)(2,1)} %get-tuple-element.402), channel_id=1, source_target_pairs={{0,1},{1,0},{2,3},{3,2},{4,5},{5,4},{6,7},{7,6},{8,9},{9,8},{10,11... | collective-permute-start | bytes 12582920 | tf_op jit(solution)/shard_map/ppermute | solution.py:50
  531.4 144.2 %reduce-scatter.6.cloned.1.call-start = ((), (), s32[]{:S(2)}) async-start(), calls=%async_computation.14 | async-start | bytes 2621440 | tf_op jit(solution)/shard_map/reduce_scatter | solution.py:67
  531.4 58.7 %collective-permute-start.43 = (bf16[4,64,4096]{2,1,0:T(8,128)(2,1)}, bf16[4,64,4096]{2,1,0:T(8,128)(2,1)S(1)}, u32[]{:S(2)}, u32[]{:S(2)}) collective-permute-start(bf16[4,64,4096]{2,1,0:T(8,128)(2,1)} %pad_maximum_fusion), channel_id=1, source_target_pairs={{0,2},{2,0},{4,6},{6,4},{8,10},{10,8},{12,14},{14,12},{16,18},{18,... | collective-permute-start | bytes 6291464 | tf_op jit(solution)/shard_map/ppermute | solution.py:46
  533.0 57.1 %collective-permute-start.44 = (bf16[4,64,4096]{2,1,0:T(8,128)(2,1)}, bf16[4,64,4096]{2,1,0:T(8,128)(2,1)}, u32[]{:S(2)}, u32[]{:S(2)}) collective-permute-start(bf16[4,64,4096]{2,1,0:T(8,128)(2,1)} %pad_maximum_fusion.1), channel_id=1, source_target_pairs={{0,4},{2,6},{4,0},{6,2},{8,12},{10,14},{12,8},{14,10},{16,20},{18,... | collective-permute-start | bytes 6291464 | tf_op jit(solution)/shard_map/ppermute | solution.py:46
  600.9 26.9 %all-to-all-start.3 = ((bf16[16,8,2048]{2,1,0:T(8,128)(2,1)}), bf16[16,8,2048]{2,1,0:T(8,128)(2,1)}, u32[]{:S(2)}, u32[]{:S(2)}) async-start(bf16[16,8,2048]{2,1,0:T(8,128)(2,1)} %broadcast_in_dim.135), calls=%async_computation.3 | async-start | bytes 1048576 | tf_op jit(solution)/shard_map/all_to_all | solution.py:154
  605.1 114.7 %reduce-scatter.4.cloned.1.call-start = ((), (), s32[]{:S(2)}) async-start(), calls=%async_computation.13 | async-start | bytes 2621440 | tf_op jit(solution)/shard_map/reduce_scatter | solution.py:67
  632.2 32.9 %collective-permute-start.48 = (bf16[2048,1024]{1,0:T(8,128)(2,1)}, bf16[2048,1024]{1,0:T(8,128)(2,1)}, u32[]{:S(2)}, u32[]{:S(2)}) collective-permute-start(bf16[2048,1024]{1,0:T(8,128)(2,1)} %get-tuple-element.425), channel_id=1, source_target_pairs={{0,1},{1,0},{2,3},{3,2},{4,5},{5,4},{6,7},{7,6},{8,9},{9,8},{10,11... | collective-permute-start | bytes 12582920 | tf_op jit(solution)/shard_map/ppermute | solution.py:50
  634.2 102.1 %reduce-scatter.8.cloned.1.call-start = ((), (), s32[]{:S(2)}) async-start(), calls=%async_computation.15 | async-start | bytes 1310720 | tf_op jit(solution)/shard_map/reduce_scatter | solution.py:67
  637.4 26.0 %collective-permute-start.49 = (bf16[4,64,2048]{2,1,0:T(8,128)(2,1)}, bf16[4,64,2048]{2,1,0:T(8,128)(2,1)}, u32[]{:S(2)}, u32[]{:S(2)}) collective-permute-start(bf16[4,64,2048]{2,1,0:T(8,128)(2,1)} %pad_maximum_fusion.4), channel_id=1, source_target_pairs={{0,2},{2,0},{4,6},{6,4},{8,10},{10,8},{12,14},{14,12},{16,18},{18,... | collective-permute-start | bytes 3145736 | tf_op jit(solution)/shard_map/ppermute | solution.py:46
  638.9 26.1 %collective-permute-start.50 = (bf16[4,64,2048]{2,1,0:T(8,128)(2,1)}, bf16[4,64,2048]{2,1,0:T(8,128)(2,1)}, u32[]{:S(2)}, u32[]{:S(2)}) collective-permute-start(bf16[4,64,2048]{2,1,0:T(8,128)(2,1)} %pad_maximum_fusion.5), channel_id=1, source_target_pairs={{0,4},{2,6},{4,0},{6,2},{8,12},{10,14},{12,8},{14,10},{16,20},{18,... | collective-permute-start | bytes 3145736 | tf_op jit(solution)/shard_map/ppermute | solution.py:46
  719.8 33.1 %all-to-all-start.4 = ((bf16[4,128,1024]{2,1,0:T(8,128)(2,1)}), bf16[4,128,1024]{2,1,0:T(8,128)(2,1)}, u32[]{:S(2)}, u32[]{:S(2)}) async-start(bf16[4,128,1024]{2,1,0:T(8,128)(2,1)} %add_convert_fusion.1), calls=%async_computation.6 | async-start | bytes 2097152 | tf_op jit(solution)/shard_map/all_to_all | solution.py:63
  (109 other events, 793.9 us)
Sparse Core Ops, SparseCore 0:
  67.6 29.2 all-gather.4
  139.9 34.6 all-gather.8
  209.3 27.1 all-gather.6
  531.5 59.5 all-gather.10
  601.0 50.4 reduce-scatter.5
  653.7 44.7 reduce-scatter.3
  701.3 26.4 reduce-scatter.7

commit v5 on v4

--- a/solution.py
+++ b/solution.py
@@ -1179,12 +1179,13 @@
         )
     )
     late_job = Exchange(turned([items_attn[:ITEMS]]))
-    grad_tokens = begin([attn_job, late_job, mlp_job], grad_tokens)
+    grad_tokens = begin([attn_job, late_job], grad_tokens)
     code_row, flat, dcode_peer = begin.wait(
         code_back_first(code_rows.reshape(1, LEN), grad_tokens, turn, n * half_rows)
     )
     code_job = Scatter(dcode_peer)
     flat = begin([code_job, attn_job], flat)
+    mlp_job.send(mlp_job.request())
     code_job.own = begin.wait(code_back_last(code_row, flat, n * half_rows))
     begin([code_job, item_job, late_job, attn_job])
     begin.wait()

time: 809 us -> 810 us (level)
  no operation moved by 1% of the time
where the time goes in v5:
time: 810 us; the launch traced here: 800 us
  Pallas kernels  353 us (44%)
  waiting for transfers between devices  155 us (19%)
  other arithmetic  108 us (13%)
  starting transfers between devices  87.8 us (11%)
  local copies, waits for them, and re-layouts  63.9 us (8%)
  between operations  22.8 us (3%)
  matrix products  10.6 us (1%)
    ppermute x46, waiting for transfers between devices, swap(): return lax.ppermute(values, 'dp', [(i, i ^ bits) for i in range(n)])  127 us
    ppermute x46, starting transfers between devices, swap(): return lax.ppermute(values, 'dp', [(i, i ^ bits) for i in range(n)])  56.1 us
    pallas_call x1, Pallas kernels, attend_back_last(): kernel_call(attend_back_last_kernel, (steps,), attend_back_specs() + [ANY...  50.7 us
    pallas_call x1, Pallas kernels, head(): kernel_call(head_kernel, (2 * half,), [whole(LEN, D), whole(D, LEN), w_sp...  47.4 us
    pallas_call x1, Pallas kernels, attend_back_first(): kernel_call(attend_back_first_kernel, (steps,), attend_back_specs(), [col...  46.6 us
    pallas_call x1, Pallas kernels, attend_last(): kernel_call(attend_last_kernel, (steps,), [whole(LEN, D), columns(D, 4 *...  34.2 us
    pallas_call x1, Pallas kernels, mlp_back_last(): kernel_call(mlp_back_last_kernel, (steps,), mlp_back_specs() + [ANYWHERE]...  32.9 us
    pallas_call x1, Pallas kernels, attend_first(): kernel_call(attend_first_kernel, (steps,), [whole(LEN, D), columns(D, 4 *...  28.9 us
  transfers between devices with their start and end apart: 71, of which 26 were waited for; matrix products, arithmetic and copies ran while one was open for 16% of the time, Pallas kernels for 37%

profile of v5, /device:TPU:0, one launch (start us, length us, event | category | flops | bytes accessed | tf_op | source)
XLA Modules:
  0.0 800.4 jit_solution(7691564098695485314)
XLA Ops:
  8.1 3.1 collective-permute-start
  15.9 5.1 all-to-all-start
  48.1 4.2 all-to-all-start.1
  64.4 3.1 fusion.2
  67.5 21.1 %collective-permute-done.8 = f32[2,8,6144]{2,1,0:T(8,128)} collective-permute-done((f32[2,8,6144]{2,1,0:T(8,128)}, f32[2,8,6144]{2,1,0:T(8,128)}, u32[]{:S(2)}, u32[]{:S(2)}) %collective-permute-start.8) | collective-permute-done | bytes 393248 | tf_op jit(solution)/shard_map/ppermute | solution.py:46
  105.7 19.3 %collective-permute-done.10.refs_3_ = bf16[256,1024]{1,0:T(8,128)(2,1)} collective-permute-done((bf16[256,1024]{1,0:T(8,128)(2,1)}, bf16[256,1024]{1,0:T(8,128)(2,1)}, u32[]{:S(2)}, u32[]{:S(2)}) %collective-permute-start.10) | collective-permute-done | bytes 524320 | tf_op jit(solution)/shard_map/ppermute | solution.py:46
  127.8 4.3 shard_map.502.own_ref
  132.2 4.6 all-to-all-start.2
  140.8 21.3 %collective-permute-done.15.refs_1_ = bf16[256,2048]{1,0:T(8,128)(2,1)S(1)} collective-permute-done((bf16[256,2048]{1,0:T(8,128)(2,1)}, bf16[256,2048]{1,0:T(8,128)(2,1)S(1)}, u32[]{:S(2)}, u32[]{:S(2)}) %collective-permute-start.15) | collective-permute-done | bytes 1048608 | tf_op jit(solution)/shard_map/ppermute | solution.py:46
  163.3 4.5 all-to-all-done.2
  176.1 16.9 %shard_map.503 = (bf16[800,1024]{1,0:T(8,128)(2,1)}, bf16[800,1024]{1,0:T(8,128)(2,1)}, bf16[1024,800]{1,0:T(8,128)(2,1)}) custom-call(s32[800,1]{1,0:T(8,128)} %copy.137.code_ref, bf16[2048,1024]{1,0:T(8,128)(2,1)} %shard_map.502.own_ref, bf16[2048,1024]{1,0:T(8,128)(2,1)} %collective-permute-done.14.peer_ref, bf16[1024,1024]{1,0:T(8,128)(2,1)} %fusion.turn_ref, ...), custom_call_target="tpu_custom_call" | custom-call | flops 6710886400 | bytes 16777216 | tf_op jit(solution)/shard_map/pallas_call | solution.py:429
  193.1 8.5 %collective-permute-done.17.refs_3_ = bf16[128,2048]{1,0:T(8,128)(2,1)S(1)} collective-permute-done((bf16[128,2048]{1,0:T(8,128)(2,1)}, bf16[128,2048]{1,0:T(8,128)(2,1)S(1)}, u32[]{:S(2)}, u32[]{:S(2)}) %collective-permute-start.17) | collective-permute-done | bytes 524320 | tf_op jit(solution)/shard_map/ppermute | solution.py:46
  205.3 3.8 shard_map.504.w_ref
  213.4 28.9 %shard_map.505 = (bf16[800,512]{1,0:T(8,128)(2,1)}, f32[800,1024]{1,0:T(8,128)}) custom-call(bf16[800,1024]{1,0:T(8,128)(2,1)} %get-tuple-element.293.na_ref, bf16[1024,2048]{1,0:T(8,128)(2,1)} %shard_map.504.w_ref, f32[800,800]{1,0:T(8,128)} %get-tuple-element.294.bias_ref), custom_call_target="tpu_custom_call" | custom-call | flops 4666163200 | bytes 16777216 | tf_op jit(solution)/shard_map/pallas_call | solution.py:484
  242.2 4.1 collective-permute-done.22.refs_3_
  249.2 3.7 shard_map.506.w0_ref
  259.5 34.2 %shard_map.507 = (bf16[800,512]{1,0:T(8,128)(2,1)}, f32[800,1024]{1,0:T(8,128)}, f32[800,1024]{1,0:T(8,128)}, bf16[800,1024]{1,0:T(8,128)(2,1)}, bf16[1024,800]{1,0:T(8,128)(2,1)}) custom-call(bf16[800,1024]{1,0:T(8,128)(2,1)} %get-tuple-element.293.na_ref, bf16[1024,2048]{1,0:T(8,128)(2,1)} %collective-permute-done.21.w_ref, ...), custom_call_target="tpu_custom_call" | custom-call | flops 4666163200 | bytes 16777216 | tf_op jit(solution)/shard_map/pallas_call | solution.py:496
  295.8 3.6 shard_map.508.w1_ref
  302.6 14.0 %shard_map.509 = (f32[800,1024]{1,0:T(8,128)}, f32[800,1024]{1,0:T(8,128)}, f32[800,1024]{1,0:T(8,128)}) custom-call(bf16[800,1024]{1,0:T(8,128)(2,1)} %get-tuple-element.322.nm_ref, bf16[1024,2048]{1,0:T(8,128)(2,1)} %shard_map.506.w0_ref, bf16[1024,2048]{1,0:T(8,128)(2,1)} %shard_map.508.w1_ref), custom_call_target="tpu_custom_call" | custom-call | flops 6710886400 | bytes 16777216 | tf_op jit(solution)/shard_map/pallas_call | solution.py:655
  317.5 3.6 shard_map.510.own_ref
  323.0 17.6 %shard_map.511 = (f32[800,1024]{1,0:T(8,128)}, f32[800,1024]{1,0:T(8,128)}, f32[800,1024]{1,0:T(8,128)}, f32[800,1024]{1,0:T(8,128)}, bf16[800,1024]{1,0:T(8,128)(2,1)}, /*index=5*/bf16[1024,800]{1,0:T(8,128)(2,1)}) custom-call(bf16[800,1024]{1,0:T(8,128)(2,1)} %get-tuple-element.322.nm_ref, bf16[1024,2048]{1,0:T(8,128)(2,1)} %collective-permute-done.26.w0_ref, ...), custom_call_target="tpu_custom_call" | custom-call | flops 6710886400 | bytes 16777216 | tf_op jit(solution)/shard_map/pallas_call | solution.py:669
  340.6 47.4 %shard_map.512 = (bf16[1024,2048]{1,0:T(8,128)(2,1)}, bf16[1024,2048]{1,0:T(8,128)(2,1)}, f32[8,128]{1,0:T(8,128)}, f32[800,1024]{1,0:T(8,128)}, bf16[800,1024]{...) custom-call(bf16[800,1024]{1,0:T(8,128)(2,1)} %get-tuple-element.340.nh_ref, ...), custom_call_target="tpu_custom_call" | custom-call | flops 20132659200 | bytes 16777216 | tf_op jit(solution)/shard_map/pallas_call | solution.py:852
  388.6 26.6 %shard_map.513 = (bf16[1024,4096]{1,0:T(8,128)(2,1)}, f32[800,1024]{1,0:T(8,128)}) custom-call(bf16[1024,800]{1,0:T(8,128)(2,1)} %get-tuple-element.352.nm_t_ref, bf16[800,1024]{1,0:T(8,128)(2,1)} %get-tuple-element.353.g_ref, bf16[1024,800]{1,0:T(8,128)(2,1)} %get-tuple-element.354.g_t_ref, f32[800,1024]{1,0:T(8,128)} %get-tuple-element.355.h0_ref, ...), custom_call_target="tpu_custom_call" | custom-call | flops 13421772800 | bytes 16777216 | tf_op jit(solution)/shard_map/pallas_call | solution.py:742
  415.1 4.0 fusion.25
  421.6 32.9 %shard_map.514 = (bf16[1024,4096]{1,0:T(8,128)(2,1)}, f32[800,1024]{1,0:T(8,128)}, bf16[800,1024]{1,0:T(8,128)(2,1)}, bf16[1024,800]{1,0:T(8,128)(2,1)}, f32[16,3072]{1,0:T(8,128)}) custom-call(bf16[1024,800]{1,0:T(8,128)(2,1)} %get-tuple-element.352.nm_t_ref, bf16[800,1024]{1,0:T(8,128)(2,1)} %get-tuple-element.353.g_ref, ...), custom_call_target="tpu_custom_call" | custom-call | flops 13421772800 | bytes 16777216 | tf_op jit(solution)/shard_map/pallas_call | solution.py:754
  460.0 5.2 fusion.10
  473.6 46.6 %shard_map.515 = (bf16[1024,2048]{1,0:T(8,128)(2,1)}, f32[800,1024]{1,0:T(8,128)}) custom-call(bf16[800,1024]{1,0:T(8,128)(2,1)} %get-tuple-element.293.na_ref, bf16[1024,800]{1,0:T(8,128)(2,1)} %get-tuple-element.386.na_t_ref, bf16[800,1024]{1,0:T(8,128)(2,1)} %get-tuple-element.387.go_ref, bf16[1024,800]{1,0:T(8,128)(2,1)} %get-tuple-element.388.go_t_ref, ...), custom_call_target="tpu_custom_call" | custom-call | flops 13998489600 | bytes 16777216 | tf_op jit(solution)/shard_map/pallas_call | solution.py:589
  520.3 4.0 fusion.3
  527.4 3.4 convert_add_fusion.3
  534.6 5.0 convert_add_fusion
  539.6 50.7 %shard_map.516 = (bf16[1024,2048]{1,0:T(8,128)(2,1)}, bf16[800,1024]{1,0:T(8,128)(2,1)}, f32[16,2048]{1,0:T(8,128)}) custom-call(bf16[800,1024]{1,0:T(8,128)(2,1)} %get-tuple-element.293.na_ref, bf16[1024,800]{1,0:T(8,128)(2,1)} %get-tuple-element.386.na_t_ref, bf16[800,1024]{1,0:T(8,128)(2,1)} %get-tuple-element.387.go_ref, ...), custom_call_target="tpu_custom_call" | custom-call | flops 13998489600 | bytes 16777216 | tf_op jit(solution)/shard_map/pallas_call | solution.py:601
  590.4 5.2 add_convert_fusion
  601.2 4.2 all-to-all-start.3
  609.4 10.0 %shard_map.517 = (bf16[2048,1024]{1,0:T(8,128)(2,1)}, bf16[800,1024]{1,0:T(8,128)(2,1)}) custom-call(s32[1,800]{1,0:T(1,128)} %reshape.592.code_ref, bf16[800,1024]{1,0:T(8,128)(2,1)} %get-tuple-element.415.gt_ref, bf16[1024,1024]{1,0:T(8,128)(2,1)} %fusion.turn_ref), custom_call_target="tpu_custom_call" | custom-call | flops 3355443200 | bytes 16777216 | tf_op jit(solution)/shard_map/pallas_call | solution.py:918
  619.4 4.0 collective-permute-done.46
  623.9 5.5 all-to-all-done.3
  647.3 7.7 shard_map.518
  654.9 9.9 %collective-permute-done.49 = bf16[4,64,2048]{2,1,0:T(8,128)(2,1)} collective-permute-done((bf16[4,64,2048]{2,1,0:T(8,128)(2,1)}, bf16[4,64,2048]{2,1,0:T(8,128)(2,1)}, u32[]{:S(2)}, u32[]{:S(2)}) %collective-permute-start.49) | collective-permute-done | bytes 1048608 | tf_op jit(solution)/shard_map/ppermute | solution.py:46
  665.7 4.2 fusion.33
  670.0 3.1 add_convert_fusion.2
  679.4 8.3 %collective-permute-done.51 = bf16[2,128,1024]{2,1,0:T(8,128)(2,1)S(1)} collective-permute-done((bf16[2,128,1024]{2,1,0:T(8,128)(2,1)}, bf16[2,128,1024]{2,1,0:T(8,128)(2,1)S(1)}, u32[]{:S(2)}, u32[]{:S(2)}) %collective-permute-start.51) | collective-permute-done | bytes 524320 | tf_op jit(solution)/shard_map/ppermute | solution.py:46
  699.2 18.7 %collective-permute-done.55 = bf16[4,128,1024]{2,1,0:T(8,128)(2,1)S(1)} collective-permute-done((bf16[4,128,1024]{2,1,0:T(8,128)(2,1)S(1)}, bf16[4,128,1024]{2,1,0:T(8,128)(2,1)S(1)}, u32[]{:S(2)}, u32[]{:S(2)}) %collective-permute-start.55) | collective-permute-done | bytes 1048608 | tf_op jit(solution)/shard_map/ppermute | solution.py:46
  720.5 8.1 %all-to-all-start.4 = ((bf16[4,128,1024]{2,1,0:T(8,128)(2,1)}), bf16[4,128,1024]{2,1,0:T(8,128)(2,1)}, u32[]{:S(2)}, u32[]{:S(2)}) async-start(bf16[4,128,1024]{2,1,0:T(8,128)(2,1)} %add_convert_fusion.1), calls=%async_computation.6 | async-start | bytes 2097152 | tf_op jit(solution)/shard_map/all_to_all | solution.py:63
  743.6 9.7 %all-to-all-done.4 = bf16[4,128,1024]{2,1,0:T(8,128)(2,1)} async-done(((bf16[4,128,1024]{2,1,0:T(8,128)(2,1)}), bf16[4,128,1024]{2,1,0:T(8,128)(2,1)}, u32[]{:S(2)}, u32[]{:S(2)}) %all-to-all-start.4) | async-done | bytes 1048608 | tf_op jit(solution)/shard_map/all_to_all | solution.py:63
  760.1 3.7 all-to-all-start.5
  764.7 6.1 all-to-all-done.5
  781.9 3.1 multiply_subtract_fusion
  788.4 3.6 multiply_subtract_fusion.1
  (492 shorter events, 207.2 us)
Async XLA Ops:
  15.9 30.1 %all-to-all-start = ((bf16[4,128,1024]{2,1,0:T(8,128)(2,1)}), bf16[4,128,1024]{2,1,0:T(8,128)(2,1)}, u32[]{:S(2)}, u32[]{:S(2)}) async-start(bf16[4,128,1024]{2,1,0:T(8,128)(2,1)} %broadcast_in_dim.80), calls=%async_computation | async-start | bytes 2097152 | tf_op jit(solution)/shard_map/all_to_all | solution.py:63
  48.1 41.7 %all-to-all-start.1 = ((bf16[4,64,2048]{2,1,0:T(8,128)(2,1)}), bf16[4,64,2048]{2,1,0:T(8,128)(2,1)}, u32[]{:S(2)}, u32[]{:S(2)}) async-start(bf16[4,64,2048]{2,1,0:T(8,128)(2,1)} %broadcast_in_dim.83), calls=%async_computation.1 | async-start | bytes 2097152 | tf_op jit(solution)/shard_map/all_to_all | solution.py:63
  52.4 53.4 %all-gather.5.cloned.1.call-start = ((), (), s32[]{:S(2)}) async-start(), calls=%async_computation.9 | async-start | bytes 1310720 | tf_op jit(solution)/shard_map/all_gather | solution.py:112
  55.8 34.1 %collective-permute-start.6 = (bf16[512,1024]{1,0:T(8,128)(2,1)}, bf16[512,1024]{1,0:T(8,128)(2,1)}, u32[]{:S(2)}, u32[]{:S(2)}) collective-permute-start(bf16[512,1024]{1,0:T(8,128)(2,1)} %bitcast.10.refs_0_), channel_id=1, source_target_pairs={{0,2},{2,0},{4,6},{6,4},{8,10},{10,8},{12,14},{14,12},{16,18},{18,... | collective-permute-start | bytes 3145736 | tf_op jit(solution)/shard_map/ppermute | solution.py:46
  57.2 32.6 %collective-permute-start.7 = (bf16[512,1024]{1,0:T(8,128)(2,1)}, bf16[512,1024]{1,0:T(8,128)(2,1)}, u32[]{:S(2)}, u32[]{:S(2)}) collective-permute-start(bf16[512,1024]{1,0:T(8,128)(2,1)} %bitcast.10.refs_0_), channel_id=1, source_target_pairs={{0,4},{2,6},{4,0},{6,2},{8,12},{10,14},{12,8},{14,10},{16,20},{18,... | collective-permute-start | bytes 3145736 | tf_op jit(solution)/shard_map/ppermute | solution.py:46
  61.4 27.2 %collective-permute-start.8 = (f32[2,8,6144]{2,1,0:T(8,128)}, f32[2,8,6144]{2,1,0:T(8,128)}, u32[]{:S(2)}, u32[]{:S(2)}) collective-permute-start(f32[2,8,6144]{2,1,0:T(8,128)} %get-tuple-element.246), channel_id=1, source_target_pairs={{0,2},{2,0},{4,6},{6,4},{8,10},{10,8},{12,14},{14,12},{16,18},{18,... | collective-permute-start | bytes 1179656 | tf_op jit(solution)/shard_map/ppermute | solution.py:46
  61.9 27.9 %collective-permute-start.9 = (f32[2,8,6144]{2,1,0:T(8,128)}, f32[2,8,6144]{2,1,0:T(8,128)}, u32[]{:S(2)}, u32[]{:S(2)}) collective-permute-start(f32[2,8,6144]{2,1,0:T(8,128)} %get-tuple-element.247), channel_id=1, source_target_pairs={{0,4},{2,6},{4,0},{6,2},{8,12},{10,14},{12,8},{14,10},{16,20},{18,... | collective-permute-start | bytes 1179656 | tf_op jit(solution)/shard_map/ppermute | solution.py:46
  96.2 29.2 %collective-permute-start.12 = (f32[4,8,6144]{2,1,0:T(8,128)}, f32[4,8,6144]{2,1,0:T(8,128)}, u32[]{:S(2)}, u32[]{:S(2)}) collective-permute-start(f32[4,8,6144]{2,1,0:T(8,128)} %get-tuple-element.254), channel_id=1, source_target_pairs={{0,2},{2,0},{4,6},{6,4},{8,10},{10,8},{12,14},{14,12},{16,18},{18,... | collective-permute-start | bytes 2359304 | tf_op jit(solution)/shard_map/ppermute | solution.py:46
  96.8 28.6 %collective-permute-start.13 = (f32[4,8,6144]{2,1,0:T(8,128)}, f32[4,8,6144]{2,1,0:T(8,128)}, u32[]{:S(2)}, u32[]{:S(2)}) collective-permute-start(f32[4,8,6144]{2,1,0:T(8,128)} %get-tuple-element.255), channel_id=1, source_target_pairs={{0,4},{2,6},{4,0},{6,2},{8,12},{10,14},{12,8},{14,10},{16,20},{18,... | collective-permute-start | bytes 2359304 | tf_op jit(solution)/shard_map/ppermute | solution.py:46
  132.2 35.6 %collective-permute-start.14 = (bf16[2048,1024]{1,0:T(8,128)(2,1)}, bf16[2048,1024]{1,0:T(8,128)(2,1)}, u32[]{:S(2)}, u32[]{:S(2)}) collective-permute-start(bf16[2048,1024]{1,0:T(8,128)(2,1)} %shard_map.502.own_ref), channel_id=1, source_target_pairs={{0,1},{1,0},{2,3},{3,2},{4,5},{5,4},{6,7},{7,6},{8,9},{9,8},{10,11... | collective-permute-start | bytes 12582920 | tf_op jit(solution)/shard_map/ppermute | solution.py:50
  132.2 35.6 %all-to-all-start.2 = ((f32[4,8,6144]{2,1,0:T(8,128)}), f32[4,8,6144]{2,1,0:T(8,128)S(1)}, u32[]{:S(2)}, u32[]{:S(2)}) async-start(f32[4,8,6144]{2,1,0:T(8,128)} %fusion.18), calls=%async_computation.2 | async-start | bytes 1572864 | tf_op jit(solution)/shard_map/all_to_all | solution.py:63
  136.7 72.4 %all-gather.9.cloned.1.call-start = ((), (), s32[]{:S(2)}) async-start(), calls=%async_computation.11 | async-start | bytes 1310720 | tf_op jit(solution)/shard_map/all_gather | solution.py:112
  136.8 25.4 %collective-permute-start.15 = (bf16[256,2048]{1,0:T(8,128)(2,1)}, bf16[256,2048]{1,0:T(8,128)(2,1)S(1)}, u32[]{:S(2)}, u32[]{:S(2)}) collective-permute-start(bf16[256,2048]{1,0:T(8,128)(2,1)} %bitcast.23.refs_0_), channel_id=1, source_target_pairs={{0,2},{2,0},{4,6},{6,4},{8,10},{10,8},{12,14},{14,12},{16,18},{18,... | collective-permute-start | bytes 3145736 | tf_op jit(solution)/shard_map/ppermute | solution.py:46
  139.8 113.1 %all-gather.7.cloned.1.call-start = ((), (), s32[]{:S(2)}) async-start(), calls=%async_computation.10 | async-start | bytes 1310720 | tf_op jit(solution)/shard_map/all_gather | solution.py:112
  169.5 33.3 %collective-permute-start.19 = (bf16[256,2048]{1,0:T(8,128)(2,1)}, bf16[256,2048]{1,0:T(8,128)(2,1)S(1)}, u32[]{:S(2)}, u32[]{:S(2)}) collective-permute-start(bf16[256,2048]{1,0:T(8,128)(2,1)} %all-gather.5.cloned.1.call-done.refs_0_), channel_id=1, source_target_pairs={{0,2},{2,0},{4,6},{6,4},{8,10},{10,8},{12,14},{14,12},{16,18},{18,... | collective-permute-start | bytes 3145736 | tf_op jit(solution)/shard_map/ppermute | solution.py:46
  170.9 31.9 %collective-permute-start.20 = (bf16[256,2048]{1,0:T(8,128)(2,1)}, bf16[256,2048]{1,0:T(8,128)(2,1)S(1)}, u32[]{:S(2)}, u32[]{:S(2)}) collective-permute-start(bf16[256,2048]{1,0:T(8,128)(2,1)} %all-gather.5.cloned.1.call-done.refs_0_), channel_id=1, source_target_pairs={{0,4},{2,6},{4,0},{6,2},{8,12},{10,14},{12,8},{14,10},{16,20},{18,... | collective-permute-start | bytes 3145736 | tf_op jit(solution)/shard_map/ppermute | solution.py:46
  175.1 26.6 %collective-permute-start.17 = (bf16[128,2048]{1,0:T(8,128)(2,1)}, bf16[128,2048]{1,0:T(8,128)(2,1)S(1)}, u32[]{:S(2)}, u32[]{:S(2)}) collective-permute-start(bf16[128,2048]{1,0:T(8,128)(2,1)} %slice.380), channel_id=1, source_target_pairs={{0,2},{2,0},{4,6},{6,4},{8,10},{10,8},{12,14},{14,12},{16,18},{18,... | collective-permute-start | bytes 1572872 | tf_op jit(solution)/shard_map/ppermute | solution.py:46
  175.6 27.2 %collective-permute-start.18 = (bf16[128,2048]{1,0:T(8,128)(2,1)}, bf16[128,2048]{1,0:T(8,128)(2,1)S(1)}, u32[]{:S(2)}, u32[]{:S(2)}) collective-permute-start(bf16[128,2048]{1,0:T(8,128)(2,1)} %slice.381), channel_id=1, source_target_pairs={{0,4},{2,6},{4,0},{6,2},{8,12},{10,14},{12,8},{14,10},{16,20},{18,... | collective-permute-start | bytes 1572872 | tf_op jit(solution)/shard_map/ppermute | solution.py:46
  209.1 38.3 %collective-permute-start.21 = (bf16[1024,2048]{1,0:T(8,128)(2,1)}, bf16[1024,2048]{1,0:T(8,128)(2,1)}, u32[]{:S(2)}, u32[]{:S(2)}) collective-permute-start(bf16[1024,2048]{1,0:T(8,128)(2,1)} %shard_map.504.w_ref), channel_id=1, source_target_pairs={{0,1},{1,0},{2,3},{3,2},{4,5},{5,4},{6,7},{7,6},{8,9},{9,8},{10,11... | collective-permute-start | bytes 12582920 | tf_op jit(solution)/shard_map/ppermute | solution.py:50
  209.2 426.6 %all-gather.11.cloned.1.call-start = ((), (), s32[]{:S(2)}) async-start(), calls=%async_computation.12 | async-start | bytes 1114112 | tf_op jit(solution)/shard_map/all_gather | solution.py:152
  209.3 37.4 %collective-permute-start.24 = (bf16[256,2048]{1,0:T(8,128)(2,1)}, bf16[256,2048]{1,0:T(8,128)(2,1)S(1)}, u32[]{:S(2)}, u32[]{:S(2)}) collective-permute-start(bf16[256,2048]{1,0:T(8,128)(2,1)} %all-gather.9.cloned.1.call-done.refs_0_), channel_id=1, source_target_pairs={{0,2},{2,0},{4,6},{6,4},{8,10},{10,8},{12,14},{14,12},{16,18},{18,... | collective-permute-start | bytes 3145736 | tf_op jit(solution)/shard_map/ppermute | solution.py:46
  209.9 36.7 %collective-permute-start.25 = (bf16[256,2048]{1,0:T(8,128)(2,1)}, bf16[256,2048]{1,0:T(8,128)(2,1)S(1)}, u32[]{:S(2)}, u32[]{:S(2)}) collective-permute-start(bf16[256,2048]{1,0:T(8,128)(2,1)} %all-gather.9.cloned.1.call-done.refs_0_), channel_id=1, source_target_pairs={{0,4},{2,6},{4,0},{6,2},{8,12},{10,14},{12,8},{14,10},{16,20},{18,... | collective-permute-start | bytes 3145736 | tf_op jit(solution)/shard_map/ppermute | solution.py:46
  211.4 34.9 %collective-permute-start.22 = (bf16[128,2048]{1,0:T(8,128)(2,1)}, bf16[128,2048]{1,0:T(8,128)(2,1)S(1)}, u32[]{:S(2)}, u32[]{:S(2)}) collective-permute-start(bf16[128,2048]{1,0:T(8,128)(2,1)} %slice.383), channel_id=1, source_target_pairs={{0,2},{2,0},{4,6},{6,4},{8,10},{10,8},{12,14},{14,12},{16,18},{18,... | collective-permute-start | bytes 1572872 | tf_op jit(solution)/shard_map/ppermute | solution.py:46
  212.9 33.7 %collective-permute-start.23 = (bf16[128,2048]{1,0:T(8,128)(2,1)}, bf16[128,2048]{1,0:T(8,128)(2,1)S(1)}, u32[]{:S(2)}, u32[]{:S(2)}) collective-permute-start(bf16[128,2048]{1,0:T(8,128)(2,1)} %slice.384), channel_id=1, source_target_pairs={{0,4},{2,6},{4,0},{6,2},{8,12},{10,14},{12,8},{14,10},{16,20},{18,... | collective-permute-start | bytes 1572872 | tf_op jit(solution)/shard_map/ppermute | solution.py:46
  252.9 41.0 %collective-permute-start.26 = (bf16[1024,2048]{1,0:T(8,128)(2,1)}, bf16[1024,2048]{1,0:T(8,128)(2,1)}, u32[]{:S(2)}, u32[]{:S(2)}) collective-permute-start(bf16[1024,2048]{1,0:T(8,128)(2,1)} %shard_map.506.w0_ref), channel_id=1, source_target_pairs={{0,1},{1,0},{2,3},{3,2},{4,5},{5,4},{6,7},{7,6},{8,9},{9,8},{10,11... | collective-permute-start | bytes 12582920 | tf_op jit(solution)/shard_map/ppermute | solution.py:50
  253.7 40.1 %collective-permute-start.29 = (bf16[256,2048]{1,0:T(8,128)(2,1)}, bf16[256,2048]{1,0:T(8,128)(2,1)S(1)}, u32[]{:S(2)}, u32[]{:S(2)}) collective-permute-start(bf16[256,2048]{1,0:T(8,128)(2,1)} %all-gather.7.cloned.1.call-done.refs_0_), channel_id=1, source_target_pairs={{0,2},{2,0},{4,6},{6,4},{8,10},{10,8},{12,14},{14,12},{16,18},{18,... | collective-permute-start | bytes 3145736 | tf_op jit(solution)/shard_map/ppermute | solution.py:46
  255.2 38.6 %collective-permute-start.30 = (bf16[256,2048]{1,0:T(8,128)(2,1)}, bf16[256,2048]{1,0:T(8,128)(2,1)S(1)}, u32[]{:S(2)}, u32[]{:S(2)}) collective-permute-start(bf16[256,2048]{1,0:T(8,128)(2,1)} %all-gather.7.cloned.1.call-done.refs_0_), channel_id=1, source_target_pairs={{0,4},{2,6},{4,0},{6,2},{8,12},{10,14},{12,8},{14,10},{16,20},{18,... | collective-permute-start | bytes 3145736 | tf_op jit(solution)/shard_map/ppermute | solution.py:46
  257.8 36.0 %collective-permute-start.27 = (bf16[128,2048]{1,0:T(8,128)(2,1)}, bf16[128,2048]{1,0:T(8,128)(2,1)S(1)}, u32[]{:S(2)}, u32[]{:S(2)}) collective-permute-start(bf16[128,2048]{1,0:T(8,128)(2,1)} %slice.385), channel_id=1, source_target_pairs={{0,2},{2,0},{4,6},{6,4},{8,10},{10,8},{12,14},{14,12},{16,18},{18,... | collective-permute-start | bytes 1572872 | tf_op jit(solution)/shard_map/ppermute | solution.py:46
  258.4 35.4 %collective-permute-start.28 = (bf16[128,2048]{1,0:T(8,128)(2,1)}, bf16[128,2048]{1,0:T(8,128)(2,1)S(1)}, u32[]{:S(2)}, u32[]{:S(2)}) collective-permute-start(bf16[128,2048]{1,0:T(8,128)(2,1)} %slice.386), channel_id=1, source_target_pairs={{0,4},{2,6},{4,0},{6,2},{8,12},{10,14},{12,8},{14,10},{16,20},{18,... | collective-permute-start | bytes 1572872 | tf_op jit(solution)/shard_map/ppermute | solution.py:46
  388.0 27.1 %collective-permute-start.35 = (bf16[1024,2048]{1,0:T(8,128)(2,1)}, bf16[1024,2048]{1,0:T(8,128)(2,1)}, u32[]{:S(2)}, u32[]{:S(2)}) collective-permute-start(bf16[1024,2048]{1,0:T(8,128)(2,1)} %get-tuple-element.351), channel_id=1, source_target_pairs={{0,1},{1,0},{2,3},{3,2},{4,5},{5,4},{6,7},{7,6},{8,9},{9,8},{10,11... | collective-permute-start | bytes 12582920 | tf_op jit(solution)/shard_map/ppermute | solution.py:50
  419.1 37.4 %collective-permute-start.38 = (bf16[1024,4096]{1,0:T(8,128)(2,1)}, bf16[1024,4096]{1,0:T(8,128)(2,1)}, u32[]{:S(2)}, u32[]{:S(2)}) collective-permute-start(bf16[1024,4096]{1,0:T(8,128)(2,1)} %get-tuple-element.364), channel_id=1, source_target_pairs={{0,1},{1,0},{2,3},{3,2},{4,5},{5,4},{6,7},{7,6},{8,9},{9,8},{10,11... | collective-permute-start | bytes 25165832 | tf_op jit(solution)/shard_map/ppermute | solution.py:50
  420.6 35.9 %collective-permute-start.36 = (bf16[2,64,2048]{2,1,0:T(8,128)(2,1)S(1)}, bf16[2,64,2048]{2,1,0:T(8,128)(2,1)S(1)}, u32[]{:S(2)}, u32[]{:S(2)}) collective-permute-start(bf16[2,64,2048]{2,1,0:T(8,128)(2,1)S(1)} %get-tuple-element.362), channel_id=1, source_target_pairs={{0,2},{2,0},{4,6},{6,4},{8,10},{10,8},{12,14},{14,12},{16,18},{18,... | collective-permute-start | bytes 1572872 | tf_op jit(solution)/shard_map/ppermute | solution.py:46
  421.1 35.4 %collective-permute-start.37 = (bf16[2,64,2048]{2,1,0:T(8,128)(2,1)S(1)}, bf16[2,64,2048]{2,1,0:T(8,128)(2,1)}, u32[]{:S(2)}, u32[]{:S(2)}) collective-permute-start(bf16[2,64,2048]{2,1,0:T(8,128)(2,1)S(1)} %get-tuple-element.363), channel_id=1, source_target_pairs={{0,4},{2,6},{4,0},{6,2},{8,12},{10,14},{12,8},{14,10},{16,20},{18,... | collective-permute-start | bytes 1572872 | tf_op jit(solution)/shard_map/ppermute | solution.py:46
  469.6 50.7 %collective-permute-start.39 = (bf16[4,64,2048]{2,1,0:T(8,128)(2,1)}, bf16[4,64,2048]{2,1,0:T(8,128)(2,1)}, u32[]{:S(2)}, u32[]{:S(2)}) collective-permute-start(bf16[4,64,2048]{2,1,0:T(8,128)(2,1)} %pad_maximum_fusion.2), channel_id=1, source_target_pairs={{0,2},{2,0},{4,6},{6,4},{8,10},{10,8},{12,14},{14,12},{16,18},{18,... | collective-permute-start | bytes 3145736 | tf_op jit(solution)/shard_map/ppermute | solution.py:46
  471.0 49.3 %collective-permute-start.40 = (bf16[4,64,2048]{2,1,0:T(8,128)(2,1)}, bf16[4,64,2048]{2,1,0:T(8,128)(2,1)}, u32[]{:S(2)}, u32[]{:S(2)}) collective-permute-start(bf16[4,64,2048]{2,1,0:T(8,128)(2,1)} %pad_maximum_fusion.3), channel_id=1, source_target_pairs={{0,4},{2,6},{4,0},{6,2},{8,12},{10,14},{12,8},{14,10},{16,20},{18,... | collective-permute-start | bytes 3145736 | tf_op jit(solution)/shard_map/ppermute | solution.py:46
  472.6 47.7 %collective-permute-start.41 = (bf16[2,64,4096]{2,1,0:T(8,128)(2,1)}, bf16[2,64,4096]{2,1,0:T(8,128)(2,1)}, u32[]{:S(2)}, u32[]{:S(2)}) collective-permute-start(bf16[2,64,4096]{2,1,0:T(8,128)(2,1)} %get-tuple-element.384), channel_id=1, source_target_pairs={{0,2},{2,0},{4,6},{6,4},{8,10},{10,8},{12,14},{14,12},{16,18},{18,... | collective-permute-start | bytes 3145736 | tf_op jit(solution)/shard_map/ppermute | solution.py:46
  473.1 47.2 %collective-permute-start.42 = (bf16[2,64,4096]{2,1,0:T(8,128)(2,1)}, bf16[2,64,4096]{2,1,0:T(8,128)(2,1)}, u32[]{:S(2)}, u32[]{:S(2)}) collective-permute-start(bf16[2,64,4096]{2,1,0:T(8,128)(2,1)} %get-tuple-element.385), channel_id=1, source_target_pairs={{0,4},{2,6},{4,0},{6,2},{8,12},{10,14},{12,8},{14,10},{16,20},{18,... | collective-permute-start | bytes 3145736 | tf_op jit(solution)/shard_map/ppermute | solution.py:46
  530.8 59.5 %collective-permute-start.45 = (bf16[1024,2048]{1,0:T(8,128)(2,1)}, bf16[1024,2048]{1,0:T(8,128)(2,1)}, u32[]{:S(2)}, u32[]{:S(2)}) collective-permute-start(bf16[1024,2048]{1,0:T(8,128)(2,1)} %get-tuple-element.401), channel_id=1, source_target_pairs={{0,1},{1,0},{2,3},{3,2},{4,5},{5,4},{6,7},{7,6},{8,9},{9,8},{10,11... | collective-permute-start | bytes 12582920 | tf_op jit(solution)/shard_map/ppermute | solution.py:50
  531.5 144.8 %reduce-scatter.6.cloned.1.call-start = ((), (), s32[]{:S(2)}) async-start(), calls=%async_computation.14 | async-start | bytes 2621440 | tf_op jit(solution)/shard_map/reduce_scatter | solution.py:67
  531.5 58.8 %collective-permute-start.43 = (bf16[4,64,4096]{2,1,0:T(8,128)(2,1)}, bf16[4,64,4096]{2,1,0:T(8,128)(2,1)S(1)}, u32[]{:S(2)}, u32[]{:S(2)}) collective-permute-start(bf16[4,64,4096]{2,1,0:T(8,128)(2,1)} %pad_maximum_fusion), channel_id=1, source_target_pairs={{0,2},{2,0},{4,6},{6,4},{8,10},{10,8},{12,14},{14,12},{16,18},{18,... | collective-permute-start | bytes 6291464 | tf_op jit(solution)/shard_map/ppermute | solution.py:46
  533.0 57.4 %collective-permute-start.44 = (bf16[4,64,4096]{2,1,0:T(8,128)(2,1)}, bf16[4,64,4096]{2,1,0:T(8,128)(2,1)}, u32[]{:S(2)}, u32[]{:S(2)}) collective-permute-start(bf16[4,64,4096]{2,1,0:T(8,128)(2,1)} %pad_maximum_fusion.1), channel_id=1, source_target_pairs={{0,4},{2,6},{4,0},{6,2},{8,12},{10,14},{12,8},{14,10},{16,20},{18,... | collective-permute-start | bytes 6291464 | tf_op jit(solution)/shard_map/ppermute | solution.py:46
  601.2 28.3 %all-to-all-start.3 = ((bf16[16,8,2048]{2,1,0:T(8,128)(2,1)}), bf16[16,8,2048]{2,1,0:T(8,128)(2,1)}, u32[]{:S(2)}, u32[]{:S(2)}) async-start(bf16[16,8,2048]{2,1,0:T(8,128)(2,1)} %broadcast_in_dim.135), calls=%async_computation.3 | async-start | bytes 1048576 | tf_op jit(solution)/shard_map/all_to_all | solution.py:154
  605.4 115.0 %reduce-scatter.4.cloned.1.call-start = ((), (), s32[]{:S(2)}) async-start(), calls=%async_computation.13 | async-start | bytes 2621440 | tf_op jit(solution)/shard_map/reduce_scatter | solution.py:67
  633.7 32.0 %collective-permute-start.48 = (bf16[2048,1024]{1,0:T(8,128)(2,1)}, bf16[2048,1024]{1,0:T(8,128)(2,1)}, u32[]{:S(2)}, u32[]{:S(2)}) collective-permute-start(bf16[2048,1024]{1,0:T(8,128)(2,1)} %get-tuple-element.422), channel_id=1, source_target_pairs={{0,1},{1,0},{2,3},{3,2},{4,5},{5,4},{6,7},{7,6},{8,9},{9,8},{10,11... | collective-permute-start | bytes 12582920 | tf_op jit(solution)/shard_map/ppermute | solution.py:50
  635.7 101.0 %reduce-scatter.8.cloned.1.call-start = ((), (), s32[]{:S(2)}) async-start(), calls=%async_computation.15 | async-start | bytes 1310720 | tf_op jit(solution)/shard_map/reduce_scatter | solution.py:67
  638.9 25.9 %collective-permute-start.49 = (bf16[4,64,2048]{2,1,0:T(8,128)(2,1)}, bf16[4,64,2048]{2,1,0:T(8,128)(2,1)}, u32[]{:S(2)}, u32[]{:S(2)}) collective-permute-start(bf16[4,64,2048]{2,1,0:T(8,128)(2,1)} %pad_maximum_fusion.4), channel_id=1, source_target_pairs={{0,2},{2,0},{4,6},{6,4},{8,10},{10,8},{12,14},{14,12},{16,18},{18,... | collective-permute-start | bytes 3145736 | tf_op jit(solution)/shard_map/ppermute | solution.py:46
  639.5 26.2 %collective-permute-start.50 = (bf16[4,64,2048]{2,1,0:T(8,128)(2,1)}, bf16[4,64,2048]{2,1,0:T(8,128)(2,1)}, u32[]{:S(2)}, u32[]{:S(2)}) collective-permute-start(bf16[4,64,2048]{2,1,0:T(8,128)(2,1)} %pad_maximum_fusion.5), channel_id=1, source_target_pairs={{0,4},{2,6},{4,0},{6,2},{8,12},{10,14},{12,8},{14,10},{16,20},{18,... | collective-permute-start | bytes 3145736 | tf_op jit(solution)/shard_map/ppermute | solution.py:46
  720.5 32.8 %all-to-all-start.4 = ((bf16[4,128,1024]{2,1,0:T(8,128)(2,1)}), bf16[4,128,1024]{2,1,0:T(8,128)(2,1)}, u32[]{:S(2)}, u32[]{:S(2)}) async-start(bf16[4,128,1024]{2,1,0:T(8,128)(2,1)} %add_convert_fusion.1), calls=%async_computation.6 | async-start | bytes 2097152 | tf_op jit(solution)/shard_map/all_to_all | solution.py:63
  (106 other events, 775.7 us)
Sparse Core Ops, SparseCore 0:
  67.6 29.2 all-gather.4
  139.9 34.6 all-gather.8
  209.3 27.1 all-gather.6
  531.6 59.5 all-gather.10
  595.7 50.4 reduce-scatter.5
  648.4 44.7 reduce-scatter.3
  696.0 26.4 reduce-scatter.7
